TPU v7x, 32 devices: a whole 2x2x4 slice. The times are simulated.
32 devices in a mesh: cube: 8 (over y, x, core), blk: 4 (over z).
Axes of the slice: x: 2, y: 2, z: 4, core: 2. Of those that a mesh axis runs over, the one named last changes fastest.
Arguments:
- inputs: bfloat16 [8, 1728, 768], P('cube', 'blk'), may hold values from -6 to 6
- cotangent: bfloat16 [8, 1728, 768], P('cube', 'blk'), may hold values from -6 to 6
- absent_groups: int32 [8, 12], P('cube'), may hold values from 0 to 1, as said below
- token_group: int32 [8, 1728], P('cube', 'blk'), may hold values from 0 to 11, as said below
- pre_gain: float32 [768], replicated, may hold values from 0.25 to 1.75
- pre_shift: float32 [768], replicated, may hold values from -3 to 3
- input_weight: bfloat16 [768, 2304], replicated, may hold values from -0.3125 to 0.3125
- input_bias: float32 [2, 768], replicated, may hold values from -3 to 3
- output_weight: bfloat16 [768, 768], replicated, may hold values from -1.75 to 1.75
- output_bias: float32 [768], replicated, may hold values from -2 to 2
- mid_gain: float32 [768], replicated, may hold values from 0.25 to 1.75
- mid_shift: float32 [768], replicated, may hold values from -3 to 3
- up_weight: bfloat16 [768, 3072], replicated, may hold values from -0.21875 to 0.21875
- up_bias: float32 [3072], replicated, may hold values from -3 to 3
- down_weight: bfloat16 [3072, 768], replicated, may hold values from -0.109375 to 0.109375
- down_bias: float32 [768], replicated, may hold values from -2 to 2
Outputs:
- layer_out: bfloat16 [8, 1728, 768], P('cube', 'blk')
- input_grad: float32 [8, 1728, 768], P('cube', 'blk')
- grad_pre_gain: float32 [768], replicated
- grad_pre_shift: float32 [768], replicated
- grad_input_weight: float32 [768, 2304], replicated
- grad_input_bias: float32 [2, 768], replicated
- grad_output_weight: float32 [768, 768], replicated
- grad_output_bias: float32 [768], replicated
- grad_mid_gain: float32 [768], replicated
- grad_mid_shift: float32 [768], replicated
- grad_up_weight: float32 [768, 3072], replicated
- grad_up_bias: float32 [3072], replicated
- grad_down_weight: float32 [3072, 768], replicated
- grad_down_bias: float32 [768], replicated
Inputs may be any that keep to these rules, and one draw needn't show every extreme that they name: `absent_groups`: each cube lacks between 1 and 3 of its 12 band groups; 1 marks a lacking group. `token_group`: each cube's positions form 12 runs of consecutive positions, position t lying in run t * 12 // 1728; each run belongs to a different group.
All inputs are finite; a program needn't handle non-finite values.
Results may differ from a plain program's by a relative error of at most 0.015.
Values may be sent and summed in bfloat16 or wider, within the bound.
No kernel may reach another device: no remote copies, remote signals or barrier semaphores. Data moves between devices by JAX's collectives and lax.ppermute only.
A program may use at most 192 MiB of HBM per device.

v0:
```python
import jax
import jax.numpy as jnp
from jax import lax
from jax.sharding import PartitionSpec as P

HEADS = 12
HD = 64
GROUPS = 12


NEG_FILL = -32768.0
EPSILON = 1e-06


def passed_along(value, axis, steps):
    count = lax.axis_size(axis)
    pairs = [(source, (source + steps) % count) for source in range(count)]
    return lax.ppermute(value, axis, pairs)


def layer_norm(values, gain_vec, shift_vec):
    centered = values - jnp.mean(values, axis=-1, keepdims=True)
    normed = centered * lax.rsqrt(jnp.mean(centered * centered, axis=-1, keepdims=True) + EPSILON)
    return normed * gain_vec + shift_vec


def gelu_exact(values):
    return jax.nn.gelu(values, approximate=False)


def split_heads(matrix):
    return matrix.reshape(matrix.shape[:-1] + (HEADS, HD))


def merge_heads(tensor):
    return tensor.reshape(tensor.shape[:-2] + (HEADS * HD,))


def matmul_rows(left_side, right_side):
    return jnp.dot(left_side, right_side, preferred_element_type=jnp.float32)


def matmul_back(left_side, right_side):
    return jnp.einsum("rf,df->rd", left_side, right_side, preferred_element_type=jnp.float32)


def weight_grad(left_side, right_side):
    return jnp.einsum("rd,rf->df", left_side, right_side, preferred_element_type=jnp.float32)


def column_sums(low_rows):
    return jnp.sum(low_rows, axis=0, dtype=jnp.float32)


def body(
    inputs,
    cotangent,
    absent_groups,
    token_group,
    pre_gain,
    pre_shift,
    input_weight,
    input_bias,
    output_weight,
    output_bias,
    mid_gain,
    mid_shift,
    up_weight,
    up_bias,
    down_weight,
    down_bias,
):
    cube_count, row_count, model_width = inputs.shape
    flat_rows = cube_count * row_count
    head_scale = HD ** (-0.5)
    group_match = token_group[:, :, None] == jnp.arange(GROUPS, dtype=jnp.int32)[None, None, :]
    lacking = jnp.sum(jnp.where(group_match, absent_groups[:, None, :], 0), axis=2)
    valid_rows = (1 - lacking).astype(jnp.float32)
    key_mask = (NEG_FILL * (1.0 - valid_rows)).astype(jnp.bfloat16)
    residual_in = inputs.astype(jnp.float32).reshape(flat_rows, model_width)
    normed_pre, pre_back = jax.vjp(layer_norm, residual_in, pre_gain, pre_shift)
    normed_low = normed_pre.astype(jnp.bfloat16)
    projected = matmul_rows(normed_low, input_weight)
    query_low = (projected[:, :model_width] + input_bias[0]).astype(jnp.bfloat16)
    key_low = projected[:, model_width : 2 * model_width].astype(jnp.bfloat16)
    value_low = (projected[:, 2 * model_width :] + input_bias[1]).astype(jnp.bfloat16)
    cube_shape = (cube_count, row_count, model_width)
    query_heads = split_heads(query_low.reshape(cube_shape))
    key_cubes = key_low.reshape(cube_shape)
    value_cubes = value_low.reshape(cube_shape)

    def score_block(key_part, mask_part):
        raw_scores = jnp.einsum(
            "cqhd,ckhd->chqk",
            query_heads,
            split_heads(key_part),
            preferred_element_type=jnp.float32,
        )
        return raw_scores * head_scale + mask_part.astype(jnp.float32)[:, None, None, :]

    stat_shape = (cube_count, HEADS, row_count)
    run_max = jnp.full(stat_shape, -jnp.inf, jnp.float32)
    run_sum = jnp.zeros(stat_shape, jnp.float32)
    run_acc = jnp.zeros(stat_shape + (HD,), jnp.float32)
    key_part = lax.all_gather(key_cubes, "blk", axis=1, tiled=True)
    value_part = lax.all_gather(value_cubes, "blk", axis=1, tiled=True)
    mask_part = lax.all_gather(key_mask, "blk", axis=1, tiled=True)
    scores = score_block(key_part, mask_part)
    new_max = jnp.max(scores, axis=3)
    weights = jnp.exp(scores - new_max[..., None])
    factor = jnp.exp(run_max - new_max)
    new_sum = run_sum * factor + jnp.sum(weights, axis=3)
    added = jnp.einsum(
        "chqk,ckhd->chqd",
        weights.astype(jnp.bfloat16),
        split_heads(value_part),
        preferred_element_type=jnp.float32,
    )
    run_max, run_sum, run_acc = (new_max, new_sum, run_acc * factor[..., None] + added)
    log_total = run_max + jnp.log(run_sum)
    attended_heads = run_acc / run_sum[..., None]
    attended_low = (
        merge_heads(jnp.transpose(attended_heads, (0, 2, 1, 3)))
        .reshape(flat_rows, model_width)
        .astype(jnp.bfloat16)
    )
    hidden = residual_in + matmul_rows(attended_low, output_weight) + output_bias
    normed_mid, mid_back = jax.vjp(layer_norm, hidden, mid_gain, mid_shift)
    normed_mid_low = normed_mid.astype(jnp.bfloat16)
    gate_pre = matmul_rows(normed_mid_low, up_weight) + up_bias
    activated, gelu_back = jax.vjp(gelu_exact, gate_pre)
    activated_low = activated.astype(jnp.bfloat16)
    result = hidden + matmul_rows(activated_low, down_weight) + down_bias
    valid_flat = valid_rows.reshape(flat_rows, 1)
    layer_out = (valid_flat * result).astype(jnp.bfloat16).reshape(cube_shape)
    grad_out = valid_flat * cotangent.astype(jnp.float32).reshape(flat_rows, model_width)
    grad_down_low = grad_out.astype(jnp.bfloat16)
    grad_down_weight = weight_grad(activated_low, grad_down_low)
    grad_down_bias = column_sums(grad_down_low)
    (grad_gate,) = gelu_back(matmul_back(grad_down_low, down_weight))
    grad_gate_low = grad_gate.astype(jnp.bfloat16)
    grad_up_weight = weight_grad(normed_mid_low, grad_gate_low)
    grad_up_bias = column_sums(grad_gate_low)
    grad_mid, grad_mid_gain, grad_mid_shift = mid_back(matmul_back(grad_gate_low, up_weight))
    grad_hidden = grad_out + grad_mid
    grad_branch_low = grad_hidden.astype(jnp.bfloat16)
    grad_output_weight = weight_grad(attended_low, grad_branch_low)
    grad_output_bias = column_sums(grad_branch_low)
    grad_attended_low = matmul_back(grad_branch_low, output_weight).astype(jnp.bfloat16)
    grad_heads = split_heads(grad_attended_low.reshape(cube_shape))
    row_delta = jnp.einsum("cqhd,chqd->chq", grad_heads.astype(jnp.float32), attended_heads)

    def block_grads(key_part, value_part, mask_part):
        key_heads = split_heads(key_part)
        value_heads = split_heads(value_part)
        prob_rows = jnp.exp(score_block(key_part, mask_part) - log_total[..., None])
        grad_probs = jnp.einsum(
            "cqhd,ckhd->chqk", grad_heads, value_heads, preferred_element_type=jnp.float32
        )
        grad_scores = (prob_rows * (grad_probs - row_delta[..., None])).astype(jnp.bfloat16)
        part_query = (
            jnp.einsum(
                "chqk,ckhd->cqhd", grad_scores, key_heads, preferred_element_type=jnp.float32
            )
            * head_scale
        )
        part_key = (
            jnp.einsum(
                "chqk,cqhd->ckhd", grad_scores, query_heads, preferred_element_type=jnp.float32
            )
            * head_scale
        )
        part_value = jnp.einsum(
            "chqk,cqhd->ckhd",
            prob_rows.astype(jnp.bfloat16),
            grad_heads,
            preferred_element_type=jnp.float32,
        )
        return (merge_heads(part_query), merge_heads(part_key), merge_heads(part_value))

    def cycle_step(index_step, cycle_state):
        held_key, held_value, held_mask, sum_key, sum_value, sum_query = cycle_state
        part_query, part_key, part_value = block_grads(held_key, held_value, held_mask)
        next_key, next_value, next_mask = passed_along((held_key, held_value, held_mask), "blk", -1)
        next_sum_key, next_sum_value = (
            passed_along((sum_key + part_key).astype(jnp.bfloat16), "blk", -1).astype(jnp.float32),
            passed_along((sum_value + part_value).astype(jnp.bfloat16), "blk", -1).astype(
                jnp.float32
            ),
        )
        return (
            next_key,
            next_value,
            next_mask,
            next_sum_key,
            next_sum_value,
            sum_query + part_query,
        )

    zeros_rows = jnp.zeros(cube_shape, jnp.float32)
    held_key, held_value, held_mask, sum_key, sum_value, sum_query = lax.fori_loop(
        0,
        lax.axis_size("blk") - 1,
        cycle_step,
        (key_cubes, value_cubes, key_mask, zeros_rows, zeros_rows, zeros_rows),
    )
    part_query, part_key, part_value = block_grads(held_key, held_value, held_mask)
    grad_query = sum_query + part_query
    grad_key, grad_value = (
        passed_along((sum_key + part_key).astype(jnp.bfloat16), "blk", -1).astype(jnp.float32),
        passed_along((sum_value + part_value).astype(jnp.bfloat16), "blk", -1).astype(jnp.float32),
    )
    grad_query_low = grad_query.reshape(flat_rows, model_width).astype(jnp.bfloat16)
    grad_key_low = grad_key.reshape(flat_rows, model_width).astype(jnp.bfloat16)
    grad_value_low = grad_value.reshape(flat_rows, model_width).astype(jnp.bfloat16)
    grad_projected = jnp.concatenate([grad_query_low, grad_key_low, grad_value_low], axis=1)
    grad_input_weight = weight_grad(normed_low, grad_projected)
    grad_input_bias = jnp.stack([column_sums(grad_query_low), column_sums(grad_value_low)])
    grad_pre, grad_pre_gain, grad_pre_shift = pre_back(matmul_back(grad_projected, input_weight))
    input_grad = (grad_hidden + grad_pre).reshape(cube_shape)
    totals = lax.psum(
        (
            grad_pre_gain,
            grad_pre_shift,
            grad_input_weight,
            grad_input_bias,
            grad_output_weight,
            grad_output_bias,
            grad_mid_gain,
            grad_mid_shift,
            grad_up_weight,
            grad_up_bias,
            grad_down_weight,
            grad_down_bias,
        ),
        ("cube", "blk"),
    )
    return (layer_out, input_grad) + tuple(totals)


def solution(mesh):
    return jax.shard_map(
        body,
        mesh=mesh,
        in_specs=(
            P("cube", "blk", None),
            P("cube", "blk", None),
            P("cube", None),
            P("cube", "blk"),
            P(),
            P(),
            P(),
            P(),
            P(),
            P(),
            P(),
            P(),
            P(),
            P(),
            P(),
            P(),
        ),
        out_specs=(
            P("cube", "blk", None),
            P("cube", "blk", None),
            P(),
            P(),
            P(),
            P(),
            P(),
            P(),
            P(),
            P(),
            P(),
            P(),
            P(),
            P(),
        ),
        check_vma=False,
    )
```

profile of v0, /device:TPU:1, one launch (start us, length us, event | category | flops | bytes accessed | tf_op | source)
XLA Modules:
  0.0 920.3 jit_solution(13068362550005029191)
XLA Ops:
  10.7 3.0 fusion.73
  16.7 3.0 fusion.44
  24.3 11.1 %all-reduce = bf16[1728]{0:T(1024)(128)(2,1)S(1)} all-reduce(bf16[1728]{0:T(1024)(128)(2,1)S(1)} %dynamic-update-slice), channel_id=3, replica_groups=mesh['cube'=8,'blk'=4] {'blk'}, use_global_device_ids=true, to_apply=%add | all-reduce | flops 1728 | bytes 6912
  37.6 36.9 %all-gather.6.cloned.1.call-done = bf16[1728,768]{1,0:T(8,128)(2,1)} async-done(((bf16[432,768]{1,0:T(8,128)(2,1)}), bf16[1728,768]{1,0:T(8,128)(2,1)}) %all-gather.6.cloned.1.call-update) | async-done | bytes 2654224 | tf_op jit(solution)/shard_map/all_gather | solution.py:105
  74.5 4.7 copy.88
  79.2 16.5 %fusion.11 = (f32[12,432]{1,0:T(8,128)S(1)}, f32[12,432,1728]{2,1,0:T(8,128)}) fusion(f32[1728]{0:T(1024)S(1)} %add.259, bf16[432,12,64]{0,2,1:T(8,128)(2,1)} %bitcast.224, bf16[1728,12,64]{0,2,1:T(8,128)(2,1)} %bitcast.236), kind=kOutput, calls=%fused_computation.19 | convolution fusion | flops 1173486592 | bytes 39177216 | tf_op jit(solution)/shard_map/cqhd,ckhd->chqk/dot_general | solution.py:93
  95.6 15.9 %fusion.12 = f32[12,432]{1,0:T(8,128)S(1)} fusion(f32[12,432,1728]{2,1,0:T(8,128)} %get-tuple-element.198, f32[1728]{0:T(1024)S(1)} %add.259, f32[12,432]{1,0:T(8,128)S(1)} %get-tuple-element.197), kind=kLoop, calls=%fused_computation.20 | loop fusion | flops 35826624 | bytes 35880192 | tf_op jit(solution)/shard_map/reduce_sum | solution.py:112
  112.8 17.2 %all-gather.8.cloned.1.call-done = bf16[1728,768]{1,0:T(8,128)(2,1)} async-done(((bf16[432,768]{1,0:T(8,128)(2,1)}), bf16[1728,768]{1,0:T(8,128)(2,1)}) %all-gather.8.cloned.1.call-update) | async-done | bytes 2654224 | tf_op jit(solution)/shard_map/all_gather | solution.py:106
  130.0 4.5 copy.89
  134.5 16.9 %fusion.83 = (bf16[12,432,64]{1,2,0:T(8,128)(2,1)S(1)}, f32[12,432,64]{1,2,0:T(8,128)}) fusion(f32[12,432]{1,0:T(8,128)} %get-tuple-element.195, bf16[1728,12,64]{0,2,1:T(8,128)(2,1)} %bitcast.244, f32[12,432,1728]{2,1,0:T(8,128)} %get-tuple-element.198, f32[1728]{0:T(1024)S(1)} %add.259, f32[12,432]{1,0:T(8,128)} %copy-done.27, ...), kind=kOutput, calls=%fused_computation.137 | convolution fusion | flops 1183444992 | bytes 40545792 | tf_op jit(solution)/shard_map/chqk,ckhd->chqd/dot_general | solution.py:113
  152.7 17.8 %multiply_convert_fusion.2 = (bf16[432,3072]{1,0:T(8,128)(2,1)}, f32[432,3072]{1,0:T(8,128)}, f32[432,3072]{1,0:T(8,128)}) fusion(f32[3072]{0:T(1024)S(1)} %copy-done.50, bf16[768,3072]{1,0:T(8,128)(2,1)} %param.30, f32[432,768]{1,0:T(8,128)S(1)} %get-tuple-element.202, f32[768]{0:T(1024)S(1)} %copy-done.52, f32[768]{0:T(1024)S(1)} %copy-done.45, ...), kind=kOutput, calls=%fused_computation.30 | convolution fusion | flops 2127679488 | bytes 19338624 | tf_op jit(solution)/shard_map/dot_general | solution.py:40
  170.5 8.2 convert_reduce_fusion
  178.7 3.1 multiply_reduce_fusion
  191.9 190.9 %while.21 = (s32[]{:T(128)}, bf16[1,432,768]{2,1,0:T(8,128)(2,1)}, bf16[1,432,768]{2,1,0:T(8,128)(2,1)}, bf16[1,432]{1,0:T(2,128)(2,1)S(1)}, f32[1,432,768]{2,1,...) while((s32[]{:T(128)}, bf16[1,432,768]{2,1,0:T(8,128)(2,1)}, ...), condition=%wide.region_10.11_spmd.clone, body=%wide.region_9.10_spmd.clone.sunk | while | flops 1459649024 | bytes 146635984 | solution.py:201
  200.4 3.0 fusion.144
  203.4 4.6 fusion.146
  208.0 2.9 copy.114
  217.2 6.4 multiply_convert_fusion.5
  223.7 2.7 convolution_multiply_fusion.6
  226.5 2.9 copy.113
  232.6 4.1 convolution_multiply_fusion.7
  241.5 11.9 %collective-permute-done.3 = bf16[1,432,768]{2,1,0:T(8,128)(2,1)} collective-permute-done((bf16[1,432,768]{2,1,0:T(8,128)(2,1)}, bf16[1,432,768]{2,1,0:T(8,128)(2,1)}, u32[]{:S(2)}, u32[]{:S(2)}) %collective-permute-start.3) | collective-permute-done | bytes 663584 | tf_op jit(solution)/shard_map/while/body/eval_jaxpr/ppermute | solution.py:18
  255.7 2.9 collective-permute-start.2
  264.9 3.0 fusion.144
  268.0 4.6 fusion.146
  272.5 2.9 copy.114
  275.5 2.7 fusion.147
  281.4 6.4 multiply_convert_fusion.5
  290.7 2.9 copy.113
  293.6 2.8 fusion.145
  296.4 2.9 collective-permute-start.3
  299.3 4.1 convolution_multiply_fusion.7
  303.4 2.9 bitcast_add_fusion.3
  308.6 9.2 collective-permute-done.3
  328.6 3.0 fusion.144
  331.6 4.6 fusion.146
  336.2 2.9 copy.114
  339.1 2.7 fusion.147
  345.8 6.4 multiply_convert_fusion.5
  355.1 2.9 copy.113
  358.0 2.8 fusion.145
  362.9 4.1 convolution_multiply_fusion.7
  367.0 2.9 bitcast_add_fusion.3
  372.2 8.3 collective-permute-done.3
  387.3 3.0 fusion.85
  390.4 3.5 fusion.23
  393.9 4.0 multiply_convert_fusion.1
  400.1 2.8 convolution_multiply_fusion.3
  402.8 3.0 copy.95
  405.8 8.4 fusion.66
  414.2 2.9 copy.98
  422.0 2.9 copy.96
  424.9 2.9 copy.97
  431.2 7.5 fusion.76
  438.7 8.2 collective-permute-done.5
  447.8 6.3 fusion.50
  454.8 6.7 fusion.49
  463.4 3.6 fusion.78
  468.3 48.5 %all-reduce.1 = (f32[768]{0:T(1024)}, f32[768]{0:T(1024)}, f32[2,768]{1,0:T(2,128)}, f32[768]{0:T(1024)}, f32[768]{0:T(1024)}, /*index=5*/f32[768]{0:T(1024)}, f32[3072]{0:T(1024)}, f32[768]{0:T(1024)}) all-reduce(f32[768]{0:T(1024)} %get-tuple-element.142, ...), channel_id=1, replica_groups=mesh['cube'=8,'blk'=4] {'cube','blk'}, use_global_device_ids=true, to_apply=%region_14.15 | all-reduce | flops 9216 | bytes 73728 | tf_op jit(solution)/shard_map/psum | solution.py:221
  517.4 4.0 add_bitcast_fusion
  521.3 371.1 %all-reduce.5.cloned.1.call-done = (f32[768,2304]{1,0:T(8,128)}, f32[768,768]{1,0:T(8,128)}, f32[768,3072]{1,0:T(8,128)}, f32[3072,768]{1,0:T(8,128)}) async-done(((f32[768,2304]{1,0:T(8,128)}, f32[768,768]{1,0:T(8,128)}, f32[768,3072]{1,0:T(8,128)}, f32[3072,768]{1,0:T(8,128)}), (f32[768,2304]{1,0:T(8,128)}, f32[768,768]{1,0:T(8,128)}, f32[768,3072]{1,0:T(8,128)}, ...) | async-done | bytes 28311568 | tf_op jit(solution)/shard_map/psum | solution.py:221
  892.5 6.6 copy.141
  900.5 9.3 %copy.143 = f32[768,3072]{1,0:T(8,128)} copy(f32[768,3072]{1,0:T(8,128)} %get-tuple-element.324) | data formatting | bytes 18874368
  909.8 3.7 copy.144
  (264 shorter events, 110.8 us)
Async XLA Ops:
  7.2 3.5 copy-start
  7.2 67.3 %all-gather.6.cloned.1.call-start = ((), (), s32[]{:S(2)}) async-start(), calls=%async_computation | async-start | bytes 3317760 | tf_op jit(solution)/shard_map/all_gather | solution.py:105
  8.7 5.0 copy-start.29
  10.7 5.9 copy-start.44
  16.6 113.4 %all-gather.8.cloned.1.call-start = ((), (), s32[]{:S(2)}) async-start(), calls=%async_computation.1 | async-start | bytes 3317760 | tf_op jit(solution)/shard_map/all_gather | solution.py:106
  16.7 6.1 copy-start.54
  19.7 872.7 %all-reduce.5.cloned.1.call-start = ((), (), s32[]{:S(2)}) async-start(), calls=%async_computation.2 | async-start | bytes 56623104 | tf_op jit(solution)/shard_map/psum | solution.py:221
  95.6 16.5 %copy-start.27 = (f32[12,432]{1,0:T(8,128)}, f32[12,432]{1,0:T(8,128)S(1)}, u32[]{:S(2)}) copy-start(f32[12,432]{1,0:T(8,128)S(1)} %get-tuple-element.197) | copy-start | bytes 62212
  134.5 16.9 %copy-start.8 = (bf16[1,432,768]{2,1,0:T(8,128)(2,1)S(1)}, bf16[1,432,768]{2,1,0:T(8,128)(2,1)}, u32[]{:S(2)}) copy-start(bf16[1,432,768]{2,1,0:T(8,128)(2,1)} %param.18) | copy-start | bytes 1990660
  134.5 16.9 %copy-start.49 = (bf16[768,768]{1,0:T(8,128)(2,1)S(1)}, bf16[768,768]{1,0:T(8,128)(2,1)}, u32[]{:S(2)}) copy-start(bf16[768,768]{1,0:T(8,128)(2,1)} %param.26) | copy-start | bytes 3538948
  134.5 16.9 %copy-start.51 = (f32[768]{0:T(1024)S(1)}, f32[768]{0:T(1024)}, u32[]{:S(2)}) copy-start(f32[768]{0:T(1024)} %param.27) | copy-start | bytes 9220
  151.4 19.1 %slice-start.5 = ((s8[4718592]{0:T(1024)(128)(4,1)}), s8[4194304]{0:T(1024)(128)(4,1)S(1)}, s32[]{:S(2)}) async-start(s8[4718592]{0:T(1024)(128)(4,1)} %bitcast.263), calls=%async_computation.8 | async-start | bytes 8388608
  151.4 27.3 %slice-start.3 = ((s8[4718592]{0:T(1024)(128)(4,1)}), s8[4194304]{0:T(1024)(128)(4,1)S(1)}, s32[]{:S(2)}) async-start(s8[4718592]{0:T(1024)(128)(4,1)} %bitcast.261), calls=%async_computation.6 | async-start | bytes 8388608
  152.3 29.5 %copy-start.13 = (f32[432,768]{1,0:T(8,128)}, f32[432,768]{1,0:T(8,128)S(1)}, u32[]{:S(2)}) copy-start(f32[432,768]{1,0:T(8,128)S(1)} %get-tuple-element.202) | copy-start | bytes 3981316
  152.6 29.2 %copy-start.42 = (f32[432]{0:T(512)}, f32[432]{0:T(512)S(1)}, u32[]{:S(2)}) copy-start(f32[432]{0:T(512)S(1)} %fusion.60) | copy-start | bytes 5188
  152.6 17.9 %copy-start.21 = (bf16[1,432,768]{2,1,0:T(8,128)(2,1)S(1)}, bf16[1,432,768]{2,1,0:T(8,128)(2,1)}, u32[]{:S(2)}) copy-start(bf16[1,432,768]{2,1,0:T(8,128)(2,1)} %param.19) | copy-start | bytes 1990660
  152.6 17.9 %copy-start.38 = (f32[432]{0:T(512)S(1)}, f32[432]{0:T(512)}, u32[]{:S(2)}) copy-start(f32[432]{0:T(512)} %subtract_convert_fusion) | copy-start | bytes 5188
  152.7 17.9 %slice-start.6 = ((s8[4718592]{0:T(1024)(128)(4,1)}), s8[524288]{0:T(1024)(128)(4,1)S(1)}, s32[]{:S(2)}) async-start(s8[4718592]{0:T(1024)(128)(4,1)} %bitcast.263), calls=%async_computation.9 | async-start | bytes 1048576
  152.7 26.0 %slice-start.4 = ((s8[4718592]{0:T(1024)(128)(4,1)}), s8[524288]{0:T(1024)(128)(4,1)S(1)}, s32[]{:S(2)}) async-start(s8[4718592]{0:T(1024)(128)(4,1)} %bitcast.261), calls=%async_computation.7 | async-start | bytes 1048576
  191.9 63.7 %collective-permute-start.2 = (bf16[1,432]{1,0:T(2,128)(2,1)S(1)}, bf16[1,432]{1,0:T(2,128)(2,1)S(1)}, u32[]{:S(2)}, u32[]{:S(2)}) collective-permute-start(bf16[1,432]{1,0:T(2,128)(2,1)S(1)} %copy.126), channel_id=1, source_target_pairs={{0,3},{1,0},{2,1},{3,2},{4,7},{5,4},{6,5},{7,6},{8,11},{9,8},{10,9... | collective-permute-start | bytes 2600 | tf_op jit(solution)/shard_map/while/body/eval_jaxpr/ppermute | solution.py:18
  194.7 60.9 %collective-permute-start = (bf16[1,432,768]{2,1,0:T(8,128)(2,1)}, bf16[1,432,768]{2,1,0:T(8,128)(2,1)}, u32[]{:S(2)}, u32[]{:S(2)}) collective-permute-start(bf16[1,432,768]{2,1,0:T(8,128)(2,1)} %copy.124), channel_id=1, source_target_pairs={{0,3},{1,0},{2,1},{3,2},{4,7},{5,4},{6,5},{7,6},{8,11},{9,8},{10,9... | collective-permute-start | bytes 1990664 | tf_op jit(solution)/shard_map/while/body/eval_jaxpr/ppermute | solution.py:18
  198.0 57.6 %collective-permute-start.1 = (bf16[1,432,768]{2,1,0:T(8,128)(2,1)}, bf16[1,432,768]{2,1,0:T(8,128)(2,1)}, u32[]{:S(2)}, u32[]{:S(2)}) collective-permute-start(bf16[1,432,768]{2,1,0:T(8,128)(2,1)} %copy.125), channel_id=1, source_target_pairs={{0,3},{1,0},{2,1},{3,2},{4,7},{5,4},{6,5},{7,6},{8,11},{9,8},{10,9... | collective-permute-start | bytes 1990664 | tf_op jit(solution)/shard_map/while/body/eval_jaxpr/ppermute | solution.py:18
  203.4 4.6 copy-start.1
  213.3 25.9 %collective-permute-start.4 = (bf16[1,432,768]{2,1,0:T(8,128)(2,1)}, bf16[1,432,768]{2,1,0:T(8,128)(2,1)}, u32[]{:S(2)}, u32[]{:S(2)}) collective-permute-start(bf16[1,432,768]{2,1,0:T(8,128)(2,1)} %fusion.147), channel_id=1, source_target_pairs={{0,3},{1,0},{2,1},{3,2},{4,7},{5,4},{6,5},{7,6},{8,11},{9,8},{10,9... | collective-permute-start | bytes 1990664 | tf_op jit(solution)/shard_map/while/body/eval_jaxpr/ppermute | solution.py:18
  217.2 6.4 copy-start.4
  231.8 21.6 %collective-permute-start.3 = (bf16[1,432,768]{2,1,0:T(8,128)(2,1)}, bf16[1,432,768]{2,1,0:T(8,128)(2,1)}, u32[]{:S(2)}, u32[]{:S(2)}) collective-permute-start(bf16[1,432,768]{2,1,0:T(8,128)(2,1)} %fusion.145), channel_id=1, source_target_pairs={{0,3},{1,0},{2,1},{3,2},{4,7},{5,4},{6,5},{7,6},{8,11},{9,8},{10,9... | collective-permute-start | bytes 1990664 | tf_op jit(solution)/shard_map/while/body/eval_jaxpr/ppermute | solution.py:18
  255.7 64.3 %collective-permute-start.2 = (bf16[1,432]{1,0:T(2,128)(2,1)S(1)}, bf16[1,432]{1,0:T(2,128)(2,1)S(1)}, u32[]{:S(2)}, u32[]{:S(2)}) collective-permute-start(bf16[1,432]{1,0:T(2,128)(2,1)S(1)} %copy.126), channel_id=1, source_target_pairs={{0,3},{1,0},{2,1},{3,2},{4,7},{5,4},{6,5},{7,6},{8,11},{9,8},{10,9... | collective-permute-start | bytes 2600 | tf_op jit(solution)/shard_map/while/body/eval_jaxpr/ppermute | solution.py:18
  260.6 59.5 %collective-permute-start = (bf16[1,432,768]{2,1,0:T(8,128)(2,1)}, bf16[1,432,768]{2,1,0:T(8,128)(2,1)}, u32[]{:S(2)}, u32[]{:S(2)}) collective-permute-start(bf16[1,432,768]{2,1,0:T(8,128)(2,1)} %copy.124), channel_id=1, source_target_pairs={{0,3},{1,0},{2,1},{3,2},{4,7},{5,4},{6,5},{7,6},{8,11},{9,8},{10,9... | collective-permute-start | bytes 1990664 | tf_op jit(solution)/shard_map/while/body/eval_jaxpr/ppermute | solution.py:18
  262.6 57.5 %collective-permute-start.1 = (bf16[1,432,768]{2,1,0:T(8,128)(2,1)}, bf16[1,432,768]{2,1,0:T(8,128)(2,1)}, u32[]{:S(2)}, u32[]{:S(2)}) collective-permute-start(bf16[1,432,768]{2,1,0:T(8,128)(2,1)} %copy.125), channel_id=1, source_target_pairs={{0,3},{1,0},{2,1},{3,2},{4,7},{5,4},{6,5},{7,6},{8,11},{9,8},{10,9... | collective-permute-start | bytes 1990664 | tf_op jit(solution)/shard_map/while/body/eval_jaxpr/ppermute | solution.py:18
  267.9 4.6 copy-start.1
  278.2 28.1 %collective-permute-start.4 = (bf16[1,432,768]{2,1,0:T(8,128)(2,1)}, bf16[1,432,768]{2,1,0:T(8,128)(2,1)}, u32[]{:S(2)}, u32[]{:S(2)}) collective-permute-start(bf16[1,432,768]{2,1,0:T(8,128)(2,1)} %fusion.147), channel_id=1, source_target_pairs={{0,3},{1,0},{2,1},{3,2},{4,7},{5,4},{6,5},{7,6},{8,11},{9,8},{10,9... | collective-permute-start | bytes 1990664 | tf_op jit(solution)/shard_map/while/body/eval_jaxpr/ppermute | solution.py:18
  281.4 6.4 copy-start.4
  293.6 5.7 copy-start.3
  296.4 21.4 %collective-permute-start.3 = (bf16[1,432,768]{2,1,0:T(8,128)(2,1)}, bf16[1,432,768]{2,1,0:T(8,128)(2,1)}, u32[]{:S(2)}, u32[]{:S(2)}) collective-permute-start(bf16[1,432,768]{2,1,0:T(8,128)(2,1)} %fusion.145), channel_id=1, source_target_pairs={{0,3},{1,0},{2,1},{3,2},{4,7},{5,4},{6,5},{7,6},{8,11},{9,8},{10,9... | collective-permute-start | bytes 1990664 | tf_op jit(solution)/shard_map/while/body/eval_jaxpr/ppermute | solution.py:18
  320.1 62.8 %collective-permute-start.2 = (bf16[1,432]{1,0:T(2,128)(2,1)S(1)}, bf16[1,432]{1,0:T(2,128)(2,1)S(1)}, u32[]{:S(2)}, u32[]{:S(2)}) collective-permute-start(bf16[1,432]{1,0:T(2,128)(2,1)S(1)} %copy.126), channel_id=1, source_target_pairs={{0,3},{1,0},{2,1},{3,2},{4,7},{5,4},{6,5},{7,6},{8,11},{9,8},{10,9... | collective-permute-start | bytes 2600 | tf_op jit(solution)/shard_map/while/body/eval_jaxpr/ppermute | solution.py:18
  324.2 58.6 %collective-permute-start = (bf16[1,432,768]{2,1,0:T(8,128)(2,1)}, bf16[1,432,768]{2,1,0:T(8,128)(2,1)}, u32[]{:S(2)}, u32[]{:S(2)}) collective-permute-start(bf16[1,432,768]{2,1,0:T(8,128)(2,1)} %copy.124), channel_id=1, source_target_pairs={{0,3},{1,0},{2,1},{3,2},{4,7},{5,4},{6,5},{7,6},{8,11},{9,8},{10,9... | collective-permute-start | bytes 1990664 | tf_op jit(solution)/shard_map/while/body/eval_jaxpr/ppermute | solution.py:18
  326.2 56.6 %collective-permute-start.1 = (bf16[1,432,768]{2,1,0:T(8,128)(2,1)}, bf16[1,432,768]{2,1,0:T(8,128)(2,1)}, u32[]{:S(2)}, u32[]{:S(2)}) collective-permute-start(bf16[1,432,768]{2,1,0:T(8,128)(2,1)} %copy.125), channel_id=1, source_target_pairs={{0,3},{1,0},{2,1},{3,2},{4,7},{5,4},{6,5},{7,6},{8,11},{9,8},{10,9... | collective-permute-start | bytes 1990664 | tf_op jit(solution)/shard_map/while/body/eval_jaxpr/ppermute | solution.py:18
  331.6 4.6 copy-start.1
  341.9 28.1 %collective-permute-start.4 = (bf16[1,432,768]{2,1,0:T(8,128)(2,1)}, bf16[1,432,768]{2,1,0:T(8,128)(2,1)}, u32[]{:S(2)}, u32[]{:S(2)}) collective-permute-start(bf16[1,432,768]{2,1,0:T(8,128)(2,1)} %fusion.147), channel_id=1, source_target_pairs={{0,3},{1,0},{2,1},{3,2},{4,7},{5,4},{6,5},{7,6},{8,11},{9,8},{10,9... | collective-permute-start | bytes 1990664 | tf_op jit(solution)/shard_map/while/body/eval_jaxpr/ppermute | solution.py:18
  345.8 6.4 copy-start.4
  358.0 5.0 copy-start.3
  360.8 19.8 %collective-permute-start.3 = (bf16[1,432,768]{2,1,0:T(8,128)(2,1)}, bf16[1,432,768]{2,1,0:T(8,128)(2,1)}, u32[]{:S(2)}, u32[]{:S(2)}) collective-permute-start(bf16[1,432,768]{2,1,0:T(8,128)(2,1)} %fusion.145), channel_id=1, source_target_pairs={{0,3},{1,0},{2,1},{3,2},{4,7},{5,4},{6,5},{7,6},{8,11},{9,8},{10,9... | collective-permute-start | bytes 1990664 | tf_op jit(solution)/shard_map/while/body/eval_jaxpr/ppermute | solution.py:18
  390.4 3.5 copy-start.24
  390.4 3.5 copy-start.35
  393.9 4.0 copy-start.5
  419.8 18.9 %collective-permute-start.6 = (bf16[1,432,768]{2,1,0:T(8,128)(2,1)}, bf16[1,432,768]{2,1,0:T(8,128)(2,1)}, u32[]{:S(2)}, u32[]{:S(2)}) collective-permute-start(bf16[1,432,768]{2,1,0:T(8,128)(2,1)} %add_convert_fusion.1), channel_id=1, source_target_pairs={{0,3},{1,0},{2,1},{3,2},{4,7},{5,4},{6,5},{7,6},{8,11},{9,8},{10,9... | collective-permute-start | bytes 1990664 | tf_op jit(solution)/shard_map/ppermute | solution.py:18
  427.8 3.3 copy-start.14
  427.8 3.3 copy-start.43
  427.8 3.3 copy-start.46
  429.9 17.1 %collective-permute-start.5 = (bf16[1,432,768]{2,1,0:T(8,128)(2,1)S(1)}, bf16[1,432,768]{2,1,0:T(8,128)(2,1)S(1)}, u32[]{:S(2)}, u32[]{:S(2)}) collective-permute-start(bf16[1,432,768]{2,1,0:T(8,128)(2,1)S(1)} %add_convert_fusion.2), channel_id=1, source_target_pairs={{0,3},{1,0},{2,1},{3,2},{4,7},{5,4},{6,5},{7,6},{8,11},{9,8},{10,9... | collective-permute-start | bytes 1990664 | tf_op jit(solution)/shard_map/ppermute | solution.py:18
  431.2 15.8 %copy-start.19 = (bf16[432,768]{1,0:T(8,128)(2,1)}, bf16[432,768]{1,0:T(8,128)(2,1)S(1)}, u32[]{:S(2)}) copy-start(bf16[432,768]{1,0:T(8,128)(2,1)S(1)} %get-tuple-element.186) | copy-start | bytes 1990660
  431.2 16.6 %copy-start.9 = (bf16[1,432,768]{2,1,0:T(8,128)(2,1)S(1)}, bf16[1,432,768]{2,1,0:T(8,128)(2,1)}, u32[]{:S(2)}) copy-start(bf16[1,432,768]{2,1,0:T(8,128)(2,1)} %param.18) | copy-start | bytes 1990660
  431.2 16.6 %copy-start.28 = (f32[768]{0:T(1024)S(1)}, f32[768]{0:T(1024)}, u32[]{:S(2)}) copy-start(f32[768]{0:T(1024)} %param.22) | copy-start | bytes 9220
  431.2 16.6 %copy-start.30 = (f32[432]{0:T(512)S(1)}, f32[432]{0:T(512)}, u32[]{:S(2)}) copy-start(f32[432]{0:T(512)} %copy-done.29) | copy-start | bytes 5188
  431.2 16.6 %copy-start.32 = (f32[432]{0:T(512)S(1)}, f32[432]{0:T(512)}, u32[]{:S(2)}) copy-start(f32[432]{0:T(512)} %copy-done.31) | copy-start | bytes 5188
  431.2 16.6 %copy-start.33 = (f32[768]{0:T(1024)S(1)}, f32[768]{0:T(1024)}, u32[]{:S(2)}) copy-start(f32[768]{0:T(1024)} %param.23) | copy-start | bytes 9220
  454.8 8.5 copy-start.10
  454.8 8.5 copy-start.20
  454.8 8.5 copy-start.26
  463.4 3.6 copy-start.37
  892.5 6.6 copy-start.22
  899.0 10.7 %slice-start = ((s8[9437184]{0:T(1024)(128)(4,1)}), s8[4194304]{0:T(1024)(128)(4,1)S(1)}, s32[]{:S(2)}) async-start(s8[9437184]{0:T(1024)(128)(4,1)} %bitcast.237), calls=%async_computation.3 | async-start | bytes 8388608
  900.5 9.3 %slice-start.1 = ((s8[9437184]{0:T(1024)(128)(4,1)}), s8[4194304]{0:T(1024)(128)(4,1)S(1)}, s32[]{:S(2)}) async-start(s8[9437184]{0:T(1024)(128)(4,1)} %bitcast.237), calls=%async_computation.4 | async-start | bytes 8388608
  900.5 9.3 %slice-start.2 = ((s8[9437184]{0:T(1024)(128)(4,1)}), s8[1048576]{0:T(1024)(128)(4,1)S(1)}, s32[]{:S(2)}) async-start(s8[9437184]{0:T(1024)(128)(4,1)} %bitcast.237), calls=%async_computation.5 | async-start | bytes 2097152
  (31 other events, 76.2 us)
Sparse Core Ops, SparseCore 0:
  16.7 57.7 all-gather.5
  76.1 53.8 all-gather.7
  454.2 438.1 all-reduce.4
where the time goes:
time: 927 us; the launch traced here: 920 us
  waiting for transfers between devices  464 us (50%)
  matrix products  180 us (19%)
  local copies, waits for them, and re-layouts  103 us (11%)
  other arithmetic  78.1 us (8%)
  blocking collectives  59.6 us (6%)
  starting transfers between devices  19.7 us (2%)
  between operations  15.2 us (2%)
    psum x1, waiting for transfers between devices, body(): lax.psum((grad_pre_gain, grad_pre_shift, grad_input_weight, grad_input_bi...  371 us
    psum x1, blocking collectives, body(): lax.psum((grad_pre_gain, grad_pre_shift, grad_input_weight, grad_input_bi...  48.5 us
    ppermute x17, waiting for transfers between devices, passed_along(): return lax.ppermute(value, axis, pairs)  38.6 us
    all_gather x1, waiting for transfers between devices, body(): key_part = lax.all_gather(key_cubes, 'blk', axis=1, tiled=True)  36.9 us
    dot_general x5, matrix products, score_block(): jnp.einsum('cqhd,ckhd->chqk', query_heads, split_heads(key_part), preferr...  28.6 us
    dot_general x4, matrix products, matmul_rows(): return jnp.dot(left_side, right_side, preferred_element_type=jnp.float32)  28.3 us
    reshape x9, local copies, waits for them, and re-layouts, merge_heads(): return tensor.reshape(tensor.shape[:-2] + (HEADS * HD,))  26.3 us
    while x51, local copies, waits for them, and re-layouts  26.2 us
  transfers between devices with their start and end apart: 20, of which 8 were waited for; matrix products, arithmetic and copies ran while one was open for 24% of the time, Pallas kernels for 0%

commit v1 on v0

v1 whole, which is shorter than its diff:
```python
import jax
import jax.numpy as jnp
from jax import lax
from jax.sharding import PartitionSpec as P

HEADS = 12
HD = 64
GROUPS = 12
MEMBERS = 4
LOCAL_HEADS = HEADS // MEMBERS
WIDTH = LOCAL_HEADS * HD

NEG_FILL = -32768.0
EPSILON = 1e-06
BF16 = jnp.bfloat16
F32 = jnp.float32


def over_cube(value, bit):
    count = lax.axis_size("cube")
    return lax.ppermute(value, "cube", [(i, i ^ (1 << bit)) for i in range(count)])


def over_blk(value, bit):
    return lax.ppermute(value, "blk", [(i, i ^ (1 << bit)) for i in range(MEMBERS)])


def chosen_pairs(is_home, cube_flip, blk_flip):
    pairs = []
    for c in range(lax.axis_size("cube")):
        for b in range(MEMBERS):
            if ((c & 1) == (b >> 1)) == is_home:
                pairs.append((c * MEMBERS + b, (c ^ cube_flip) * MEMBERS + (b ^ blk_flip)))
    return pairs


def sent_between(value, is_home, cube_flip, blk_flip):
    return lax.ppermute(value, ("cube", "blk"), chosen_pairs(is_home, cube_flip, blk_flip))


def exchanged(parts):
    far = over_blk(parts[3], 0)
    near = over_blk(parts[1], 0)
    core = over_cube(parts[2], 0)
    return [parts[0], near, core, over_cube(far, 0)]


def half_of(rows, which, axis=0):
    size = rows.shape[axis] // 2
    return lax.dynamic_slice_in_dim(rows, which * size, size, axis)


def added(first, second):
    return (first.astype(F32) + second.astype(F32)).astype(BF16)


def halved(rows, flag, send, axis=0):
    got = send(half_of(rows, 1 - flag, axis))
    return added(half_of(rows, flag, axis), got)


def joined(own, got, flag, axis=0):
    return jnp.where(
        flag == 0,
        jnp.concatenate([own, got], axis),
        jnp.concatenate([got, own], axis),
    )


def cube_bits():
    return list(range(1, lax.axis_size("cube").bit_length() - 1))


def flag_of(index, bit):
    return (index >> bit) & 1


def reduced_over_planes(first, second, cube):
    bits = cube_bits()
    for one, two in zip(bits, reversed(bits)):
        first = halved(first, flag_of(cube, one), lambda v, s=one: over_cube(v, s))
        second = halved(second, flag_of(cube, two), lambda v, s=two: over_cube(v, s))
    return first, second


def gathered_over_planes(first, second, cube, axis=0):
    bits = cube_bits()
    for one, two in zip(reversed(bits), bits):
        first = joined(first, over_cube(first, one), flag_of(cube, one), axis)
        second = joined(second, over_cube(second, two), flag_of(cube, two), axis)
    return first, second


def summed_everywhere(keep, send, cube, blk):
    half = added(keep, over_cube(send, 0))
    size = half.shape[0] // 2
    first, second = reduced_over_planes(half[:size], half[size:], cube)
    both = jnp.stack([first, second])
    both = halved(both, flag_of(blk, 0), lambda v: over_blk(v, 0), 1)
    both = halved(both, flag_of(blk, 1), lambda v: over_blk(v, 1), 1)
    both = joined(both, over_blk(both, 1), flag_of(blk, 1), 1)
    both = joined(both, over_blk(both, 0), flag_of(blk, 0), 1)
    first, second = gathered_over_planes(both[0], both[1], cube)
    got_first, got_second = over_cube(first, 0), over_cube(second, 0)
    mine = jnp.concatenate([first, second])
    other = jnp.concatenate([got_first, got_second])
    flag = cube & 1
    return jnp.where(flag == 0, mine, other), jnp.where(flag == 0, other, mine)


def layer_norm(values, gain_vec, shift_vec):
    centered = values - jnp.mean(values, axis=-1, keepdims=True)
    normed = centered * lax.rsqrt(jnp.mean(centered * centered, axis=-1, keepdims=True) + EPSILON)
    return normed * gain_vec + shift_vec


def gelu_exact(values):
    return jax.nn.gelu(values, approximate=False)


def matmul_rows(left_side, right_side):
    return jnp.dot(left_side, right_side, preferred_element_type=F32)


def matmul_back(left_side, right_side):
    return jnp.einsum("rf,df->rd", left_side, right_side, preferred_element_type=F32)


def weight_grad(left_side, right_side):
    return jnp.einsum("rd,rf->df", left_side, right_side, preferred_element_type=F32)


def column_sums(low_rows):
    return jnp.sum(low_rows, axis=0, dtype=F32)


def member_columns(matrix, member, axis):
    return lax.dynamic_slice_in_dim(matrix, member * WIDTH, WIDTH, axis)


def body(
    inputs,
    cotangent,
    absent_groups,
    token_group,
    pre_gain,
    pre_shift,
    input_weight,
    input_bias,
    output_weight,
    output_bias,
    mid_gain,
    mid_shift,
    up_weight,
    up_bias,
    down_weight,
    down_bias,
):
    _, rows, model = inputs.shape
    hidden_units = up_weight.shape[1]
    head_scale = HD ** (-0.5)
    cube, blk = lax.axis_index("cube"), lax.axis_index("blk")
    core = cube & 1
    at_home = core == (blk >> 1)
    member = 2 * core + (blk & 1)

    def moved(value):
        return jnp.where(at_home, value, sent_between(value, False, 1, 2))

    def from_group(value):
        value_moved = sent_between(value, False, 1, 2)
        near_home = sent_between(value, True, 0, 1)
        own = jnp.where(at_home, value, value_moved)
        near = jnp.where(at_home, near_home, sent_between(value_moved, False, 0, 1))
        return [own, near, over_cube(own, 0), over_cube(near, 0)]

    group_match = token_group[0][:, None] == jnp.arange(GROUPS, dtype=jnp.int32)[None, :]
    lacking = jnp.sum(jnp.where(group_match, absent_groups, 0), axis=1)
    valid_here = (1 - lacking).astype(BF16)[None, :]
    x_blocks = from_group(inputs[0])
    valid_blocks = from_group(valid_here)
    cot_own = moved(cotangent[0])
    x_all = jnp.concatenate(x_blocks).astype(F32)
    valid_all = jnp.concatenate(valid_blocks, axis=1)[0].astype(F32)
    key_bias = NEG_FILL * (1.0 - valid_all)
    residual_in = x_blocks[0].astype(F32)

    in_columns = jnp.concatenate(
        [member_columns(input_weight[:, s * model : (s + 1) * model], member, 1) for s in range(3)],
        axis=1,
    )
    bias_columns = member_columns(input_bias, member, 1)
    out_rows = [member_columns(output_weight, member ^ e, 0) for e in range(MEMBERS)]

    normed_low = layer_norm(x_all, pre_gain, pre_shift).astype(BF16)
    projected = matmul_rows(normed_low, in_columns)
    total_rows = projected.shape[0]
    heads_shape = (total_rows, LOCAL_HEADS, HD)
    query = (projected[:, :WIDTH] + bias_columns[0]).astype(BF16).reshape(heads_shape)
    key = projected[:, WIDTH : 2 * WIDTH].astype(BF16).reshape(heads_shape)
    value = (projected[:, 2 * WIDTH :] + bias_columns[1]).astype(BF16).reshape(heads_shape)

    def scores():
        raw = jnp.einsum("qhd,khd->hqk", query, key, preferred_element_type=F32)
        return raw * head_scale + key_bias

    peak = jnp.max(scores(), axis=2)
    weights = jnp.exp(scores() - peak[..., None])
    total = jnp.sum(weights, axis=2)
    attended_heads = (
        jnp.einsum("hqk,khd->hqd", weights.astype(BF16), value, preferred_element_type=F32)
        / total[..., None]
    )
    log_total = peak + jnp.log(total)
    attended_own = (
        jnp.transpose(attended_heads, (1, 0, 2)).reshape(MEMBERS, rows, WIDTH).astype(BF16)
    )
    attended = exchanged([attended_own[d] for d in range(MEMBERS)])

    hidden = residual_in + output_bias
    for part, weight_part in zip(attended, out_rows):
        hidden = hidden + matmul_rows(part, weight_part)
    normed_mid, mid_back = jax.vjp(layer_norm, hidden, mid_gain, mid_shift)
    normed_mid_low = normed_mid.astype(BF16)
    gate_pre = matmul_rows(normed_mid_low, up_weight) + up_bias
    activated, gelu_back = jax.vjp(gelu_exact, gate_pre)
    activated_low = activated.astype(BF16)
    result = hidden + matmul_rows(activated_low, down_weight) + down_bias
    valid_own = valid_all[:rows, None]
    layer_out = moved((valid_own * result).astype(BF16))
    grad_out = valid_own * cot_own.astype(F32)
    grad_down_low = grad_out.astype(BF16)
    grad_down_bias = column_sums(grad_down_low)
    (grad_gate,) = gelu_back(matmul_back(grad_down_low, down_weight))
    grad_gate_low = grad_gate.astype(BF16)

    down_halves = [
        weight_grad(half_of(activated_low, side, 1), grad_down_low).astype(BF16)
        for side in (core, 1 - core)
    ]
    grad_up_bias = column_sums(grad_gate_low)
    grad_mid, grad_mid_gain, grad_mid_shift = mid_back(matmul_back(grad_gate_low, up_weight))
    grad_hidden = grad_out + grad_mid
    grad_branch_low = grad_hidden.astype(BF16)
    grad_output_bias = column_sums(grad_branch_low)
    grad_attended = exchanged([matmul_back(grad_branch_low, part).astype(BF16) for part in out_rows])

    blocks = hidden_units // model

    def up_half(side):
        gate_half = half_of(grad_gate_low, side, 1)
        return [
            weight_grad(normed_mid_low, gate_half[:, s * model : (s + 1) * model]).astype(BF16)
            for s in range(blocks // 2)
        ]

    def out_half(side):
        parts = []
        for which in range(MEMBERS // 2):
            away = (2 * side + which) ^ member
            rows_here = lax.dynamic_index_in_dim(jnp.stack(attended), away, 0, keepdims=False)
            parts.append(weight_grad(rows_here, grad_branch_low).astype(BF16))
        return parts

    rest_halves = [jnp.concatenate(up_half(side) + out_half(side)) for side in (core, 1 - core)]
    down_sum = summed_everywhere(down_halves[0], down_halves[1], cube, blk)
    rest_sum = summed_everywhere(rest_halves[0], rest_halves[1], cube, blk)
    grad_down_weight = jnp.concatenate(down_sum).astype(F32)
    up_rows = blocks // 2 * model
    grad_up_weight = jnp.concatenate(
        [
            half[s * model : (s + 1) * model]
            for half in rest_sum
            for s in range(blocks // 2)
        ],
        axis=1,
    ).astype(F32)
    grad_output_weight = jnp.concatenate([half[up_rows:] for half in rest_sum]).astype(F32)

    grad_rows = jnp.concatenate(grad_attended).reshape(heads_shape)
    row_delta = jnp.einsum("qhd,hqd->hq", grad_rows.astype(F32), attended_heads)
    probs = jnp.exp(scores() - log_total[..., None])
    grad_probs = jnp.einsum("qhd,khd->hqk", grad_rows, value, preferred_element_type=F32)
    grad_scores = (probs * (grad_probs - row_delta[..., None])).astype(BF16)
    grad_query = jnp.einsum("hqk,khd->qhd", grad_scores, key, preferred_element_type=F32)
    grad_key = jnp.einsum("hqk,qhd->khd", grad_scores, query, preferred_element_type=F32)
    grad_value = jnp.einsum("hqk,qhd->khd", probs.astype(BF16), grad_rows, preferred_element_type=F32)
    grad_columns = jnp.concatenate(
        [
            (grad_query * head_scale).astype(BF16).reshape(total_rows, WIDTH),
            (grad_key * head_scale).astype(BF16).reshape(total_rows, WIDTH),
            grad_value.astype(BF16).reshape(total_rows, WIDTH),
        ],
        axis=1,
    )
    grad_in = weight_grad(normed_low, grad_columns)
    column_total = column_sums(grad_columns)

    partial = matmul_back(grad_columns, in_columns).astype(BF16).reshape(MEMBERS, rows, model)
    near_sum = added(partial[1], over_cube(partial[3], 0))
    own_sum = partial[0].astype(F32) + over_cube(partial[2], 0).astype(F32)
    grad_normed = own_sum + over_blk(near_sum, 0).astype(F32)
    _, pre_back = jax.vjp(layer_norm, residual_in, pre_gain, pre_shift)
    grad_pre, grad_pre_gain, grad_pre_shift = pre_back(grad_normed)
    grad_here = grad_hidden + grad_pre
    input_grad = jnp.where(
        at_home, grad_here, sent_between(grad_here.astype(BF16), False, 1, 2).astype(F32)
    )

    in_low = grad_in.astype(BF16)
    size = model // 2
    first, second = reduced_over_planes(in_low[:size], in_low[size:], cube)
    both = halved(jnp.stack([first, second]), flag_of(blk, 1), lambda v: over_blk(v, 1), 1)
    both = joined(both, over_blk(both, 1), flag_of(blk, 1), 1)
    both = jnp.stack([both, over_blk(both, 0)], axis=1)
    first, second = gathered_over_planes(both[0], both[1], cube, 1)
    mine = jnp.concatenate([first, second], axis=1)
    other = over_cube(mine, 0)
    pair = [mine[0], mine[1], other[0], other[1]]
    low_flag, high_flag = member & 1, member >> 1
    pair = [jnp.where(low_flag == 0, pair[e], pair[e ^ 1]) for e in range(MEMBERS)]
    pair = [jnp.where(high_flag == 0, pair[e], pair[e ^ 2]) for e in range(MEMBERS)]
    grad_input_weight = jnp.concatenate(
        [
            part[:, s * WIDTH : (s + 1) * WIDTH]
            for s in range(3)
            for part in pair
        ],
        axis=1,
    ).astype(F32)

    here_bias = jnp.stack([column_total[:WIDTH], column_total[2 * WIDTH :]])
    spread_bias = lax.dynamic_update_slice_in_dim(
        jnp.zeros((2, model), F32), here_bias, member * WIDTH, 1
    )
    vectors = jnp.concatenate(
        [
            jnp.stack(
                [
                    grad_pre_gain,
                    grad_pre_shift,
                    grad_output_bias,
                    grad_mid_gain,
                    grad_mid_shift,
                    grad_down_bias,
                ]
            ),
            spread_bias,
            grad_up_bias.reshape(blocks, model),
        ]
    )
    vectors = lax.psum(vectors, ("cube", "blk"))
    return (
        layer_out[None],
        input_grad[None],
        vectors[0],
        vectors[1],
        grad_input_weight,
        vectors[6:8],
        grad_output_weight,
        vectors[2],
        vectors[3],
        vectors[4],
        grad_up_weight,
        vectors[8:].reshape(-1),
        grad_down_weight,
        vectors[5],
    )


def solution(mesh):
    rows_spec = P("cube", "blk", None)
    return jax.shard_map(
        body,
        mesh=mesh,
        in_specs=(rows_spec, rows_spec, P("cube", None), P("cube", "blk")) + (P(),) * 12,
        out_specs=(rows_spec, rows_spec) + (P(),) * 12,
        check_vma=False,
    )
```

time: 927 us -> 561 us (0.61)
  waiting for transfers between devices: 464 us -> 125 us
  starting transfers between devices: 19.7 us -> 104 us
  local copies, waits for them, and re-layouts: 103 us -> 43.5 us
  matrix products: 180 us -> 153 us
  blocking collectives: 59.6 us -> 37.8 us
  between operations: 15.2 us -> 2.52 us
    psum x1 -> x0, waiting for transfers between devices: 371 us -> none  [body(): lax.psum((grad_pre_gain, grad_pre_shift, grad_input_weight, grad_input_bi...]
    ppermute x17 -> x66, waiting for transfers between devices: 38.6 us -> 125 us  [the longest x16 61.2 us: over_blk(): lax.ppermute(value, 'blk', [(i, i ^ 1 << bit) for i in range(MEMBERS)])]
    ppermute x17 -> x66, starting transfers between devices: 19.6 us -> 104 us  [the longest x41 67.7 us: over_cube(): lax.ppermute(value, 'cube', [(i, i ^ 1 << bit) for i in range(count)])]
    all_gather x2 -> x0, waiting for transfers between devices: 54.1 us -> none  [the longest x1 36.9 us: body(): key_part = lax.all_gather(key_cubes, 'blk', axis=1, tiled=True)]
    while x54 -> x0, local copies, waits for them, and re-layouts: 33.7 us -> none
    dot_general x34 -> x31, matrix products: 180 us -> 153 us  [the longest x7 23.2 us: matmul_rows(): return jnp.dot(left_side, right_side, preferred_element_type=F32)]
    reshape x10 -> x6, local copies, waits for them, and re-layouts: 28.5 us -> 2.39 us  [the longest x4 1.17 us: layer_norm(): return normed * gain_vec + shift_vec]
    convert_element_type x16 -> x20, other arithmetic: 37.7 us -> 20.1 us  [the longest x13 6.14 us: added(): return (first.astype(F32) + second.astype(F32)).astype(BF16)]
  transfers between devices with their start and end apart: 20 -> 66, of which waited for: 8 -> 32; matrix products, arithmetic and copies ran while one was open for 24% -> 31% of each run, Pallas kernels for 0% -> 0%
where the time goes in v1:
time: 561 us; the launch traced here: 550 us
  matrix products  153 us (27%)
  waiting for transfers between devices  125 us (22%)
  starting transfers between devices  104 us (19%)
  other arithmetic  83.4 us (15%)
  local copies, waits for them, and re-layouts  43.5 us (8%)
  blocking collectives  37.8 us (7%)
    ppermute x41, starting transfers between devices, over_cube(): lax.ppermute(value, 'cube', [(i, i ^ 1 << bit) for i in range(count)])  67.7 us
    ppermute x16, waiting for transfers between devices, over_blk(): lax.ppermute(value, 'blk', [(i, i ^ 1 << bit) for i in range(MEMBERS)])  61.2 us
    ppermute x41, waiting for transfers between devices, over_cube(): lax.ppermute(value, 'cube', [(i, i ^ 1 << bit) for i in range(count)])  42.9 us
    psum x1, blocking collectives, body(): vectors = lax.psum(vectors, ('cube', 'blk'))  37.8 us
    ppermute x9, starting transfers between devices, sent_between(): lax.ppermute(value, ('cube', 'blk'), chosen_pairs(is_home, cube_flip, blk...  26.1 us
    dot_general x7, matrix products, matmul_rows(): return jnp.dot(left_side, right_side, preferred_element_type=F32)  23.2 us
    dot_general x1, matrix products, body(): jnp.einsum('qhd,khd->hqk', grad_rows, value, preferred_element_type=F32)  22.3 us
    ppermute x9, waiting for transfers between devices, sent_between(): lax.ppermute(value, ('cube', 'blk'), chosen_pairs(is_home, cube_flip, blk...  21.3 us
  transfers between devices with their start and end apart: 66, of which 32 were waited for; matrix products, arithmetic and copies ran while one was open for 31% of the time, Pallas kernels for 0%

profile of v1, /device:TPU:1, one launch (start us, length us, event | category | flops | bytes accessed | tf_op | source)
XLA Modules:
  0.0 549.6 jit_solution(4204939533947078310)
XLA Ops:
  1.6 5.6 %collective-permute-start = (bf16[1,432]{1,0:T(2,128)(2,1)S(1)}, bf16[1,432]{1,0:T(2,128)(2,1)S(1)}, u32[]{:S(2)}, u32[]{:S(2)}) collective-permute-start(bf16[1,432]{1,0:T(2,128)(2,1)S(1)} %convert_element_type.358), channel_id=1, source_target_pairs={{2,4},{3,5},{4,2},{5,3},{10,12},{11,13},{12,10},{13,11},{18,20},{1... | collective-permute-start | bytes 2600 | tf_op jit(solution)/shard_map/ppermute | solution.py:38
  10.5 4.5 collective-permute-start.15
  16.0 2.2 fusion.128
  20.4 3.2 collective-permute-start.2
  23.6 12.5 %collective-permute-done.5 = bf16[432,768]{1,0:T(8,128)(2,1)} collective-permute-done((bf16[432,768]{1,0:T(8,128)(2,1)}, bf16[432,768]{1,0:T(8,128)(2,1)}, u32[]{:S(2)}, u32[]{:S(2)}) %collective-permute-start.5) | collective-permute-done | bytes 663584 | tf_op jit(solution)/shard_map/ppermute | solution.py:38
  41.4 8.8 %collective-permute-done.7 = bf16[432,768]{1,0:T(8,128)(2,1)S(1)} collective-permute-done((bf16[432,768]{1,0:T(8,128)(2,1)}, bf16[432,768]{1,0:T(8,128)(2,1)S(1)}, u32[]{:S(2)}, u32[]{:S(2)}) %collective-permute-start.7) | collective-permute-done | bytes 663584 | tf_op jit(solution)/shard_map/ppermute | solution.py:38
  54.4 5.1 fusion.10
  59.6 2.7 fusion.57
  62.6 15.3 %fusion.3 = (f32[3,1728]{1,0:T(4,128)S(1)}, f32[3,1728,1728]{1,2,0:T(8,128)}) fusion(f32[1728]{0:T(1024)S(1)} %multiply_reduce_fusion.3, bf16[1728,3,64]{0,2,1:T(8,128)(2,1)S(1)} %bitcast.133, bf16[1728,3,64]{0,2,1:T(8,128)(2,1)S(1)} %bitcast.128), kind=kOutput, calls=%fused_computation.7 | convolution fusion | flops 1173486592 | bytes 37186560 | tf_op jit(solution)/shard_map/qhd,khd->hqk/dot_general | solution.py:204
  77.9 16.0 %fusion = f32[3,1728]{1,0:T(4,128)S(1)} fusion(f32[3,1728,1728]{1,2,0:T(8,128)} %get-tuple-element.124, f32[3,1728]{1,0:T(4,128)S(1)} %get-tuple-element.123, f32[1728]{0:T(1024)S(1)} %multiply_reduce_fusion.3), kind=kLoop, calls=%fused_computation.4 | loop fusion | flops 35826624 | bytes 35880192 | tf_op jit(solution)/shard_map/reduce_sum | solution.py:209
  94.5 17.3 %fusion.32 = (bf16[1728,3,64]{0,2,1:T(8,128)(2,1)S(1)}, f32[3,1728,64]{1,2,0:T(8,128)}) fusion(f32[1728,3]{0,1:T(4,128)S(1)} %bitcast.156, bf16[1728,3,64]{0,2,1:T(8,128)(2,1)S(1)} %bitcast.147, f32[3,1728,1728]{1,2,0:T(8,128)} %get-tuple-element.124, f32[3,1728]{1,0:T(4,128)S(1)} %get-tuple-element.123, f32[1728]{0:T(1024)S(1)} %multiply_reduce_fusion.3), kind=kOutput, calls=%fused_computation.90 | convolution fusion | flops 1183113216 | bytes 38534400 | tf_op jit(solution)/shard_map/hqk,khd->hqd/dot_general | solution.py:211
  114.5 4.1 collective-permute-done.12
  120.4 2.3 collective-permute-done.10
  125.3 15.8 %multiply_convert_fusion.1 = (bf16[432,3072]{1,0:T(8,128)(2,1)S(1)}, f32[432,3072]{1,0:T(8,128)}, f32[432,3072]{1,0:T(8,128)}) fusion(f32[3072]{0:T(1024)S(1)} %copy-done.59, bf16[432,768]{1,0:T(8,128)(2,1)S(1)} %add_convert_fusion.6, bf16[768,3072]{1,0:T(8,128)(2,1)S(1)} %bitcast.174), kind=kOutput, calls=%fused_computation.23 | convolution fusion | flops 2126020608 | bytes 18665472 | tf_op jit(solution)/shard_map/dot_general | solution.py:122
  141.1 8.4 %convert_reduce_fusion.1 = (f32[3072]{0:T(1024)S(1)}, bf16[432,3072]{1,0:T(8,128)(2,1)S(1)}) fusion(f32[432,3072]{1,0:T(8,128)} %get-tuple-element.84, bf16[3072,768]{1,0:T(8,128)(2,1)S(1)} %bitcast.176, bf16[432,768]{1,0:T(8,128)(2,1)S(1)} %get-tuple-element.72, f32[432]{0:T(512)S(1)} %bitcast.161, f32[432,3072]{1,0:T(8,128)} %get-tuple-element.129, ...), kind=kOutput, calls=%fused_computation.21 | convolution fusion | flops 2061984768 | bytes 18679488 | tf_op jit(solution)/shard_map/rf,df->rd/dot_general | solution.py:126
  149.5 2.6 multiply_reduce_fusion
  159.9 2.9 convolution_convert_fusion
  162.8 3.1 fusion.35
  165.9 2.2 collective-permute-start.14
  181.1 3.4 collective-permute-done.18
  184.5 2.7 collective-permute-start.19
  190.1 20.0 %fusion.22 = bf16[3,64,1728]{2,1,0:T(8,128)(2,1)} fusion(bf16[1728,3,64]{0,2,1:T(8,128)(2,1)S(1)} %bitcast.138, f32[3,1728,1728]{1,2,0:T(8,128)} %get-tuple-element.124, f32[3,1728]{1,0:T(4,128)} %log_add_fusion, f32[1728]{0:T(1024)S(1)} %multiply_reduce_fusion.3), kind=kOutput, calls=%fused_computation.53 | convolution fusion | flops 1182781440 | bytes 37186560 | tf_op jit(solution)/shard_map/hqk,qhd->khd/dot_general | solution.py:287
  211.7 22.3 %multiply_convert_fusion = bf16[3,1728,1728]{1,2,0:T(8,128)(2,1)} fusion(f32[3,1728,1728]{1,2,0:T(8,128)} %get-tuple-element.124, f32[3,1728]{1,0:T(4,128)S(1)} %fusion.31, f32[3,1728]{1,0:T(4,128)S(1)} %copy-done.46, f32[1728]{0:T(1024)S(1)} %multiply_reduce_fusion.3, bf16[1728,3,64]{0,2,1:T(8,128)(2,1)S(1)} %bitcast.140, bf16[1728,3,64]{0,2,1:T(8,128)(2,1)} %bitcast.148), kind=kOutput, calls=%fused_computation | convolution fusion | flops 1200365568 | bytes 55123200 | tf_op jit(solution)/shard_map/qhd,khd->hqk/dot_general | solution.py:283
  234.0 11.5 %fusion.21 = bf16[3,64,1728]{2,1,0:T(8,128)(2,1)S(1)} fusion(bf16[1728,3,64]{0,2,1:T(8,128)(2,1)S(1)} %bitcast.134, bf16[3,1728,1728]{1,2,0:T(8,128)(2,1)} %multiply_convert_fusion), kind=kOutput, calls=%fused_computation.52 | convolution fusion | flops 1147281408 | bytes 19243008 | tf_op jit(solution)/shard_map/hqk,qhd->khd/dot_general | solution.py:286
  245.6 9.5 %fusion.20 = bf16[3,64,1728]{2,1,0:T(8,128)(2,1)S(1)} fusion(bf16[1728,3,64]{0,2,1:T(8,128)(2,1)S(1)} %bitcast.129, bf16[3,1728,1728]{1,2,0:T(8,128)(2,1)} %multiply_convert_fusion), kind=kOutput, calls=%fused_computation.51 | convolution fusion | flops 1147281408 | bytes 19243008 | tf_op jit(solution)/shard_map/hqk,khd->qhd/dot_general | solution.py:285
  255.2 2.5 convolution_convert_fusion.2
  264.4 6.9 %collective-permute-done.24 = bf16[192,576]{0,1:T(8,128)(2,1)S(1)} collective-permute-done((bf16[192,576]{0,1:T(8,128)(2,1)S(1)}, bf16[192,576]{0,1:T(8,128)(2,1)S(1)}, u32[]{:S(2)}, u32[]{:S(2)}) %collective-permute-start.24) | collective-permute-done | bytes 221216 | tf_op jit(solution)/shard_map/ppermute | solution.py:21
  272.7 5.8 %collective-permute-done.26 = bf16[192,576]{0,1:T(8,128)(2,1)S(1)} collective-permute-done((bf16[192,576]{0,1:T(8,128)(2,1)S(1)}, bf16[192,576]{0,1:T(8,128)(2,1)S(1)}, u32[]{:S(2)}, u32[]{:S(2)}) %collective-permute-start.26) | collective-permute-done | bytes 221216 | tf_op jit(solution)/shard_map/ppermute | solution.py:21
  280.0 2.5 collective-permute-done.25
  283.8 2.7 collective-permute-done.27
  287.5 13.9 %collective-permute-done.28 = bf16[2,48,576]{1,2,0:T(8,128)(2,1)S(1)} collective-permute-done((bf16[2,48,576]{1,2,0:T(8,128)(2,1)S(1)}, bf16[2,48,576]{1,2,0:T(8,128)(2,1)S(1)}, u32[]{:S(2)}, u32[]{:S(2)}) %collective-permute-start.28) | collective-permute-done | bytes 110624 | tf_op jit(solution)/shard_map/ppermute | solution.py:25
  301.8 14.8 %collective-permute-done.29 = bf16[2,48,576]{1,2,0:T(8,128)(2,1)S(1)} collective-permute-done((bf16[2,48,576]{1,2,0:T(8,128)(2,1)S(1)}, bf16[2,48,576]{1,2,0:T(8,128)(2,1)S(1)}, u32[]{:S(2)}, u32[]{:S(2)}) %collective-permute-start.29) | collective-permute-done | bytes 110624 | tf_op jit(solution)/shard_map/ppermute | solution.py:25
  316.9 2.3 add_convert_fusion.5
  321.0 4.0 collective-permute-done.30
  328.9 2.5 collective-permute-done.33
  331.4 3.2 collective-permute-start.36
  341.7 2.4 fusion.39
  345.7 3.2 fusion.125
  349.0 37.8 %psum.7 = f32[12,768]{1,0:T(8,128)S(1)} all-reduce(f32[12,768]{1,0:T(8,128)S(1)} %concatenate.180), channel_id=1, replica_groups=mesh['cube'=8,'blk'=4] {'cube','blk'}, use_global_device_ids=true, to_apply=%region_21.22 | all-reduce | flops 9216 | bytes 73728 | tf_op jit(solution)/shard_map/psum | solution.py:352
  387.4 3.0 fusion.124
  390.4 5.4 collective-permute-start.23
  397.0 2.1 copy.60
  399.1 2.2 copy.57
  405.3 3.2 add_convert_fusion.2
  411.7 2.3 select_bitcast_fusion
  414.1 8.5 %collective-permute-done.52 = bf16[384,768]{1,0:T(8,128)(2,1)S(1)} collective-permute-done((bf16[384,768]{1,0:T(8,128)(2,1)S(1)}, bf16[384,768]{1,0:T(8,128)(2,1)S(1)}, u32[]{:S(2)}, u32[]{:S(2)}) %collective-permute-start.52) | collective-permute-done | bytes 589856 | tf_op jit(solution)/shard_map/ppermute | solution.py:21
  425.9 2.4 add_convert_fusion
  435.0 3.5 collective-permute-done.56
  446.1 2.2 collective-permute-done.37
  456.7 3.2 collective-permute-done.59
  460.1 3.6 collective-permute-start.60
  465.7 2.4 collective-permute-done.60
  469.4 3.2 collective-permute-done.42
  473.5 3.4 collective-permute-start.62
  476.9 4.7 collective-permute-done.43
  482.7 6.5 %collective-permute-start.63 = (bf16[384,768]{1,0:T(8,128)(2,1)S(1)}, bf16[384,768]{1,0:T(8,128)(2,1)S(1)}, u32[]{:S(2)}, u32[]{:S(2)}) collective-permute-start(bf16[384,768]{1,0:T(8,128)(2,1)S(1)} %maximum_select_fusion.13), channel_id=1, source_target_pairs={{0,16},{4,20},{8,24},{12,28},{16,0},{20,4},{24,8},{28,12},{1,17},{... | collective-permute-start | bytes 1769480 | tf_op jit(solution)/shard_map/ppermute | solution.py:21
  489.7 8.6 %collective-permute-start.64 = (bf16[768,768]{1,0:T(8,128)(2,1)S(1)}, bf16[768,768]{1,0:T(8,128)(2,1)}, u32[]{:S(2)}, u32[]{:S(2)}) collective-permute-start(bf16[768,768]{1,0:T(8,128)(2,1)S(1)} %maximum_select_fusion.2), channel_id=1, source_target_pairs={{0,4},{4,0},{8,12},{12,8},{16,20},{20,16},{24,28},{28,24},{1,5},{5... | collective-permute-start | bytes 3538952 | tf_op jit(solution)/shard_map/ppermute | solution.py:21
  501.2 8.7 %collective-permute-start.65 = (bf16[768,768]{1,0:T(8,128)(2,1)S(1)}, bf16[768,768]{1,0:T(8,128)(2,1)}, u32[]{:S(2)}, u32[]{:S(2)}) collective-permute-start(bf16[768,768]{1,0:T(8,128)(2,1)S(1)} %maximum_select_fusion.3), channel_id=1, source_target_pairs={{0,4},{4,0},{8,12},{12,8},{16,20},{20,16},{24,28},{28,24},{1,5},{5... | collective-permute-start | bytes 3538952 | tf_op jit(solution)/shard_map/ppermute | solution.py:21
  515.8 5.9 %copy.62 = f32[768,2304]{1,0:T(8,128)} copy(bf16[768,2304]{0,1:T(8,128)(2,1)} %slice_dynamic-update-slice_fusion) | data formatting | bytes 10616832
  523.1 3.2 collective-permute-done.46
  526.3 2.3 maximum_select_fusion
  528.6 4.3 collective-permute-start.49
  537.2 4.5 maximum_convert_fusion.1
  545.1 4.3 maximum_convert_fusion
  (402 shorter events, 135.2 us)
Async XLA Ops:
  1.6 18.8 %collective-permute-start = (bf16[1,432]{1,0:T(2,128)(2,1)S(1)}, bf16[1,432]{1,0:T(2,128)(2,1)S(1)}, u32[]{:S(2)}, u32[]{:S(2)}) collective-permute-start(bf16[1,432]{1,0:T(2,128)(2,1)S(1)} %convert_element_type.358), channel_id=1, source_target_pairs={{2,4},{3,5},{4,2},{5,3},{10,12},{11,13},{12,10},{13,11},{18,20},{1... | collective-permute-start | bytes 2600 | tf_op jit(solution)/shard_map/ppermute | solution.py:38
  7.2 30.8 %collective-permute-start.1 = (bf16[1,432]{1,0:T(2,128)(2,1)S(1)}, bf16[1,432]{1,0:T(2,128)(2,1)S(1)}, u32[]{:S(2)}, u32[]{:S(2)}) collective-permute-start(bf16[1,432]{1,0:T(2,128)(2,1)S(1)} %convert_element_type.358), channel_id=1, source_target_pairs={{0,1},{1,0},{6,7},{7,6},{8,9},{9,8},{14,15},{15,14},{16,17},{17,16... | collective-permute-start | bytes 2600 | tf_op jit(solution)/shard_map/ppermute | solution.py:38
  7.8 33.5 %collective-permute-start.6 = (bf16[432,768]{1,0:T(8,128)(2,1)}, bf16[432,768]{1,0:T(8,128)(2,1)S(1)}, u32[]{:S(2)}, u32[]{:S(2)}) collective-permute-start(bf16[432,768]{1,0:T(8,128)(2,1)} %bitcast.152), channel_id=1, source_target_pairs={{0,1},{1,0},{6,7},{7,6},{8,9},{9,8},{14,15},{15,14},{16,17},{17,16... | collective-permute-start | bytes 1990664 | tf_op jit(solution)/shard_map/ppermute | solution.py:38
  8.6 27.5 %collective-permute-start.5 = (bf16[432,768]{1,0:T(8,128)(2,1)}, bf16[432,768]{1,0:T(8,128)(2,1)}, u32[]{:S(2)}, u32[]{:S(2)}) collective-permute-start(bf16[432,768]{1,0:T(8,128)(2,1)} %bitcast.153), channel_id=1, source_target_pairs={{2,4},{3,5},{4,2},{5,3},{10,12},{11,13},{12,10},{13,11},{18,20},{1... | collective-permute-start | bytes 1990664 | tf_op jit(solution)/shard_map/ppermute | solution.py:38
  10.5 39.8 %collective-permute-start.15 = (bf16[432,768]{1,0:T(8,128)(2,1)}, bf16[432,768]{1,0:T(8,128)(2,1)}, u32[]{:S(2)}, u32[]{:S(2)}) collective-permute-start(bf16[432,768]{1,0:T(8,128)(2,1)} %bitcast.154), channel_id=1, source_target_pairs={{2,4},{3,5},{4,2},{5,3},{10,12},{11,13},{12,10},{13,11},{18,20},{1... | collective-permute-start | bytes 1990664 | tf_op jit(solution)/shard_map/ppermute | solution.py:38
  20.4 17.7 %collective-permute-start.2 = (bf16[1,432]{1,0:T(2,128)(2,1)S(1)}, bf16[1,432]{1,0:T(2,128)(2,1)S(1)}, u32[]{:S(2)}, u32[]{:S(2)}) collective-permute-start(bf16[1,432]{1,0:T(2,128)(2,1)S(1)} %collective-permute-done), channel_id=1, source_target_pairs={{2,3},{3,2},{4,5},{5,4},{10,11},{11,10},{12,13},{13,12},{18,19},{1... | collective-permute-start | bytes 2600 | tf_op jit(solution)/shard_map/ppermute | solution.py:38
  36.0 14.1 %collective-permute-start.7 = (bf16[432,768]{1,0:T(8,128)(2,1)}, bf16[432,768]{1,0:T(8,128)(2,1)S(1)}, u32[]{:S(2)}, u32[]{:S(2)}) collective-permute-start(bf16[432,768]{1,0:T(8,128)(2,1)} %collective-permute-done.5), channel_id=1, source_target_pairs={{2,3},{3,2},{4,5},{5,4},{10,11},{11,10},{12,13},{13,12},{18,19},{1... | collective-permute-start | bytes 1990664 | tf_op jit(solution)/shard_map/ppermute | solution.py:38
  41.2 12.5 %collective-permute-start.8 = (bf16[432,768]{1,0:T(8,128)(2,1)S(1)}, bf16[432,768]{1,0:T(8,128)(2,1)S(1)}, u32[]{:S(2)}, u32[]{:S(2)}) collective-permute-start(bf16[432,768]{1,0:T(8,128)(2,1)S(1)} %get-tuple-element.82), channel_id=1, source_target_pairs={{0,4},{4,0},{8,12},{12,8},{16,20},{20,16},{24,28},{28,24},{1,5},{5... | collective-permute-start | bytes 1990664 | tf_op jit(solution)/shard_map/ppermute | solution.py:21
  50.2 3.4 collective-permute-start.9
  112.1 6.4 %collective-permute-start.12 = (bf16[432,192]{0,1:T(8,128)(2,1)S(1)}, bf16[432,192]{0,1:T(8,128)(2,1)S(1)}, u32[]{:S(2)}, u32[]{:S(2)}) collective-permute-start(bf16[432,192]{0,1:T(8,128)(2,1)S(1)} %bitcast.159), channel_id=1, source_target_pairs={{0,1},{1,0},{2,3},{3,2},{4,5},{5,4},{6,7},{7,6},{8,9},{9,8},{10,11... | collective-permute-start | bytes 497672 | tf_op jit(solution)/shard_map/ppermute | solution.py:25
  112.2 7.9 %collective-permute-start.11 = (bf16[432,192]{0,1:T(8,128)(2,1)S(1)}, bf16[432,192]{0,1:T(8,128)(2,1)S(1)}, u32[]{:S(2)}, u32[]{:S(2)}) collective-permute-start(bf16[432,192]{0,1:T(8,128)(2,1)S(1)} %bitcast.158), channel_id=1, source_target_pairs={{0,4},{4,0},{8,12},{12,8},{16,20},{20,16},{24,28},{28,24},{1,5},{5... | collective-permute-start | bytes 497672 | tf_op jit(solution)/shard_map/ppermute | solution.py:21
  112.4 10.3 %collective-permute-start.10 = (bf16[432,192]{0,1:T(8,128)(2,1)S(1)}, bf16[432,192]{0,1:T(8,128)(2,1)S(1)}, u32[]{:S(2)}, u32[]{:S(2)}) collective-permute-start(bf16[432,192]{0,1:T(8,128)(2,1)S(1)} %bitcast.157), channel_id=1, source_target_pairs={{0,1},{1,0},{2,3},{3,2},{4,5},{5,4},{6,7},{7,6},{8,9},{9,8},{10,11... | collective-permute-start | bytes 497672 | tf_op jit(solution)/shard_map/ppermute | solution.py:25
  118.5 4.6 collective-permute-start.13
  165.9 159.8 %collective-permute-start.14 = (bf16[432,768]{1,0:T(8,128)(2,1)}, bf16[432,768]{1,0:T(8,128)(2,1)}, u32[]{:S(2)}, u32[]{:S(2)}) collective-permute-start(bf16[432,768]{1,0:T(8,128)(2,1)} %fusion.35), channel_id=1, source_target_pairs={{2,4},{3,5},{4,2},{5,3},{10,12},{11,13},{12,10},{13,11},{18,20},{1... | collective-permute-start | bytes 1990664 | tf_op jit(solution)/shard_map/ppermute | solution.py:38
  168.1 20.1 %collective-permute-start.16 = (bf16[432,192]{0,1:T(8,128)(2,1)}, bf16[432,192]{0,1:T(8,128)(2,1)}, u32[]{:S(2)}, u32[]{:S(2)}) collective-permute-start(bf16[432,192]{0,1:T(8,128)(2,1)} %convolution_convert_fusion.14), channel_id=1, source_target_pairs={{0,1},{1,0},{2,3},{3,2},{4,5},{5,4},{6,7},{7,6},{8,9},{9,8},{10,11... | collective-permute-start | bytes 497672 | tf_op jit(solution)/shard_map/ppermute | solution.py:25
  169.6 18.6 %collective-permute-start.17 = (bf16[432,192]{0,1:T(8,128)(2,1)}, bf16[432,192]{0,1:T(8,128)(2,1)}, u32[]{:S(2)}, u32[]{:S(2)}) collective-permute-start(bf16[432,192]{0,1:T(8,128)(2,1)} %convolution_convert_fusion.13), channel_id=1, source_target_pairs={{0,4},{4,0},{8,12},{12,8},{16,20},{20,16},{24,28},{28,24},{1,5},{5... | collective-permute-start | bytes 497672 | tf_op jit(solution)/shard_map/ppermute | solution.py:21
  169.6 14.8 %collective-permute-start.18 = (bf16[432,192]{0,1:T(8,128)(2,1)}, bf16[432,192]{0,1:T(8,128)(2,1)}, u32[]{:S(2)}, u32[]{:S(2)}) collective-permute-start(bf16[432,192]{0,1:T(8,128)(2,1)} %convolution_convert_fusion.12), channel_id=1, source_target_pairs={{0,1},{1,0},{2,3},{3,2},{4,5},{5,4},{6,7},{7,6},{8,9},{9,8},{10,11... | collective-permute-start | bytes 497672 | tf_op jit(solution)/shard_map/ppermute | solution.py:25
  177.7 227.6 %collective-permute-start.51 = (bf16[1536,768]{1,0:T(8,128)(2,1)}, bf16[1536,768]{1,0:T(8,128)(2,1)}, u32[]{:S(2)}, u32[]{:S(2)}) collective-permute-start(bf16[1536,768]{1,0:T(8,128)(2,1)} %convolution_convert_fusion), channel_id=1, source_target_pairs={{0,4},{4,0},{8,12},{12,8},{16,20},{20,16},{24,28},{28,24},{1,5},{5... | collective-permute-start | bytes 7077896 | tf_op jit(solution)/shard_map/ppermute | solution.py:21
  184.5 4.1 collective-permute-start.19
  259.3 57.7 %collective-permute-start.21 = (bf16[432,768]{1,0:T(8,128)(2,1)}, bf16[432,768]{1,0:T(8,128)(2,1)}, u32[]{:S(2)}, u32[]{:S(2)}) collective-permute-start(bf16[432,768]{1,0:T(8,128)(2,1)} %get-tuple-element.104), channel_id=1, source_target_pairs={{0,4},{4,0},{8,12},{12,8},{16,20},{20,16},{24,28},{28,24},{1,5},{5... | collective-permute-start | bytes 1990664 | tf_op jit(solution)/shard_map/ppermute | solution.py:21
  259.6 80.0 %collective-permute-start.20 = (bf16[432,768]{1,0:T(8,128)(2,1)}, bf16[432,768]{1,0:T(8,128)(2,1)S(1)}, u32[]{:S(2)}, u32[]{:S(2)}) collective-permute-start(bf16[432,768]{1,0:T(8,128)(2,1)} %get-tuple-element.103), channel_id=1, source_target_pairs={{0,4},{4,0},{8,12},{12,8},{16,20},{20,16},{24,28},{28,24},{1,5},{5... | collective-permute-start | bytes 1990664 | tf_op jit(solution)/shard_map/ppermute | solution.py:21
  263.0 8.3 %collective-permute-start.24 = (bf16[192,576]{0,1:T(8,128)(2,1)S(1)}, bf16[192,576]{0,1:T(8,128)(2,1)S(1)}, u32[]{:S(2)}, u32[]{:S(2)}) collective-permute-start(bf16[192,576]{0,1:T(8,128)(2,1)S(1)} %constant_dynamic-slice_fusion.13), channel_id=1, source_target_pairs={{0,8},{4,12},{8,0},{12,4},{16,24},{20,28},{24,16},{28,20},{1,9},{5... | collective-permute-start | bytes 663560 | tf_op jit(solution)/shard_map/ppermute | solution.py:21
  271.2 7.3 %collective-permute-start.26 = (bf16[192,576]{0,1:T(8,128)(2,1)S(1)}, bf16[192,576]{0,1:T(8,128)(2,1)S(1)}, u32[]{:S(2)}, u32[]{:S(2)}) collective-permute-start(bf16[192,576]{0,1:T(8,128)(2,1)S(1)} %constant_dynamic-slice_fusion.11), channel_id=1, source_target_pairs={{0,16},{4,20},{8,24},{12,28},{16,0},{20,4},{24,8},{28,12},{1,17},{... | collective-permute-start | bytes 663560 | tf_op jit(solution)/shard_map/ppermute | solution.py:21
  278.5 4.0 collective-permute-start.25
  282.5 4.0 collective-permute-start.27
  286.8 14.6 %collective-permute-start.28 = (bf16[2,48,576]{1,2,0:T(8,128)(2,1)S(1)}, bf16[2,48,576]{1,2,0:T(8,128)(2,1)S(1)}, u32[]{:S(2)}, u32[]{:S(2)}) collective-permute-start(bf16[2,48,576]{1,2,0:T(8,128)(2,1)S(1)} %fusion.58), channel_id=1, source_target_pairs={{0,2},{1,3},{2,0},{3,1},{4,6},{5,7},{6,4},{7,5},{8,10},{9,11},{10,... | collective-permute-start | bytes 331784 | tf_op jit(solution)/shard_map/ppermute | solution.py:25
  301.5 15.0 %collective-permute-start.29 = (bf16[2,48,576]{1,2,0:T(8,128)(2,1)S(1)}, bf16[2,48,576]{1,2,0:T(8,128)(2,1)S(1)}, u32[]{:S(2)}, u32[]{:S(2)}) collective-permute-start(bf16[2,48,576]{1,2,0:T(8,128)(2,1)S(1)} %add_convert_fusion.15), channel_id=1, source_target_pairs={{0,2},{1,3},{2,0},{3,1},{4,6},{5,7},{6,4},{7,5},{8,10},{9,11},{10,... | collective-permute-start | bytes 331784 | tf_op jit(solution)/shard_map/ppermute | solution.py:25
  316.8 8.2 %collective-permute-start.30 = (bf16[2,96,576]{1,2,0:T(8,128)(2,1)S(1)}, bf16[2,96,576]{1,2,0:T(8,128)(2,1)S(1)}, u32[]{:S(2)}, u32[]{:S(2)}) collective-permute-start(bf16[2,96,576]{1,2,0:T(8,128)(2,1)S(1)} %maximum_select_fusion.16), channel_id=1, source_target_pairs={{0,1},{1,0},{2,3},{3,2},{4,5},{5,4},{6,7},{7,6},{8,9},{9,8},{10,11... | collective-permute-start | bytes 663560 | tf_op jit(solution)/shard_map/ppermute | solution.py:25
  319.2 21.6 %collective-permute-start.22 = (bf16[432,768]{1,0:T(8,128)(2,1)}, bf16[432,768]{1,0:T(8,128)(2,1)S(1)}, u32[]{:S(2)}, u32[]{:S(2)}) collective-permute-start(bf16[432,768]{1,0:T(8,128)(2,1)} %add_convert_fusion.5), channel_id=1, source_target_pairs={{0,1},{1,0},{2,3},{3,2},{4,5},{5,4},{6,7},{7,6},{8,9},{9,8},{10,11... | collective-permute-start | bytes 1990664 | tf_op jit(solution)/shard_map/ppermute | solution.py:25
  325.1 6.3 %collective-permute-start.33 = (bf16[2,96,576]{1,2,0:T(8,128)(2,1)S(1)}, bf16[2,96,576]{1,2,0:T(8,128)(2,1)S(1)}, u32[]{:S(2)}, u32[]{:S(2)}) collective-permute-start(bf16[2,96,576]{1,2,0:T(8,128)(2,1)S(1)} %get-tuple-element.118), channel_id=1, source_target_pairs={{0,8},{4,12},{8,0},{12,4},{16,24},{20,28},{24,16},{28,20},{1,9},{5... | collective-permute-start | bytes 663560 | tf_op jit(solution)/shard_map/ppermute | solution.py:21
  325.7 10.5 %collective-permute-start.31 = (bf16[2,96,576]{1,2,0:T(8,128)(2,1)S(1)}, bf16[2,96,576]{1,2,0:T(8,128)(2,1)}, u32[]{:S(2)}, u32[]{:S(2)}) collective-permute-start(bf16[2,96,576]{1,2,0:T(8,128)(2,1)S(1)} %get-tuple-element.117), channel_id=1, source_target_pairs={{0,16},{4,20},{8,24},{12,28},{16,0},{20,4},{24,8},{28,12},{1,17},{... | collective-permute-start | bytes 663560 | tf_op jit(solution)/shard_map/ppermute | solution.py:21
  331.4 94.5 %collective-permute-start.36 = (bf16[1920,768]{1,0:T(8,128)(2,1)}, bf16[1920,768]{1,0:T(8,128)(2,1)}, u32[]{:S(2)}, u32[]{:S(2)}) collective-permute-start(bf16[1920,768]{1,0:T(8,128)(2,1)} %pad_maximum_fusion), channel_id=1, source_target_pairs={{0,4},{4,0},{8,12},{12,8},{16,20},{20,16},{24,28},{28,24},{1,5},{5... | collective-permute-start | bytes 8847368 | tf_op jit(solution)/shard_map/ppermute | solution.py:21
  336.2 60.9 %collective-permute-start.34 = (bf16[2,192,576]{2,1,0:T(8,128)(2,1)}, bf16[2,192,576]{2,1,0:T(8,128)(2,1)}, u32[]{:S(2)}, u32[]{:S(2)}) collective-permute-start(bf16[2,192,576]{2,1,0:T(8,128)(2,1)} %copy.59), channel_id=1, source_target_pairs={{0,16},{4,20},{8,24},{12,28},{16,0},{20,4},{24,8},{28,12},{1,17},{... | collective-permute-start | bytes 1327112 | tf_op jit(solution)/shard_map/ppermute | solution.py:21
  339.6 59.6 %collective-permute-start.32 = (bf16[2,192,576]{2,1,0:T(8,128)(2,1)}, bf16[2,192,576]{2,1,0:T(8,128)(2,1)}, u32[]{:S(2)}, u32[]{:S(2)}) collective-permute-start(bf16[2,192,576]{2,1,0:T(8,128)(2,1)} %copy.56), channel_id=1, source_target_pairs={{0,8},{4,12},{8,0},{12,4},{16,24},{20,28},{24,16},{28,20},{1,9},{5... | collective-permute-start | bytes 1327112 | tf_op jit(solution)/shard_map/ppermute | solution.py:21
  390.4 21.3 %collective-permute-start.23 = (bf16[432,768]{1,0:T(8,128)(2,1)}, bf16[432,768]{1,0:T(8,128)(2,1)}, u32[]{:S(2)}, u32[]{:S(2)}) collective-permute-start(bf16[432,768]{1,0:T(8,128)(2,1)} %get-tuple-element.75), channel_id=1, source_target_pairs={{2,4},{3,5},{4,2},{5,3},{10,12},{11,13},{12,10},{13,11},{18,20},{1... | collective-permute-start | bytes 1990664 | tf_op jit(solution)/shard_map/ppermute | solution.py:38
  408.7 13.8 %collective-permute-start.52 = (bf16[384,768]{1,0:T(8,128)(2,1)S(1)}, bf16[384,768]{1,0:T(8,128)(2,1)S(1)}, u32[]{:S(2)}, u32[]{:S(2)}) collective-permute-start(bf16[384,768]{1,0:T(8,128)(2,1)S(1)} %constant_dynamic-slice_fusion.4), channel_id=1, source_target_pairs={{0,8},{4,12},{8,0},{12,4},{16,24},{20,28},{24,16},{28,20},{1,9},{5... | collective-permute-start | bytes 1769480 | tf_op jit(solution)/shard_map/ppermute | solution.py:21
  410.9 22.6 %collective-permute-start.35 = (bf16[2,768,576]{1,2,0:T(8,128)(2,1)S(1)}, bf16[2,768,576]{1,2,0:T(8,128)(2,1)S(1)}, u32[]{:S(2)}, u32[]{:S(2)}) collective-permute-start(bf16[2,768,576]{1,2,0:T(8,128)(2,1)S(1)} %pad_maximum_fusion.4), channel_id=1, source_target_pairs={{0,4},{4,0},{8,12},{12,8},{16,20},{20,16},{24,28},{28,24},{1,5},{5... | collective-permute-start | bytes 5308424 | tf_op jit(solution)/shard_map/ppermute | solution.py:21
  411.0 14.5 %collective-permute-start.54 = (bf16[384,768]{1,0:T(8,128)(2,1)S(1)}, bf16[384,768]{1,0:T(8,128)(2,1)S(1)}, u32[]{:S(2)}, u32[]{:S(2)}) collective-permute-start(bf16[384,768]{1,0:T(8,128)(2,1)S(1)} %constant_dynamic-slice_fusion.2), channel_id=1, source_target_pairs={{0,16},{4,20},{8,24},{12,28},{16,0},{20,4},{24,8},{28,12},{1,17},{... | collective-permute-start | bytes 1769480 | tf_op jit(solution)/shard_map/ppermute | solution.py:21
  422.7 9.5 %collective-permute-start.53 = (bf16[192,768]{1,0:T(8,128)(2,1)S(1)}, bf16[192,768]{1,0:T(8,128)(2,1)S(1)}, u32[]{:S(2)}, u32[]{:S(2)}) collective-permute-start(bf16[192,768]{1,0:T(8,128)(2,1)S(1)} %constant_dynamic-slice_fusion.3), channel_id=1, source_target_pairs={{0,16},{4,20},{8,24},{12,28},{16,0},{20,4},{24,8},{28,12},{1,17},{... | collective-permute-start | bytes 884744 | tf_op jit(solution)/shard_map/ppermute | solution.py:21
  425.7 6.7 %collective-permute-start.55 = (bf16[192,768]{1,0:T(8,128)(2,1)S(1)}, bf16[192,768]{1,0:T(8,128)(2,1)S(1)}, u32[]{:S(2)}, u32[]{:S(2)}) collective-permute-start(bf16[192,768]{1,0:T(8,128)(2,1)S(1)} %constant_dynamic-slice_fusion.1), channel_id=1, source_target_pairs={{0,8},{4,12},{8,0},{12,4},{16,24},{20,28},{24,16},{28,20},{1,9},{5... | collective-permute-start | bytes 884744 | tf_op jit(solution)/shard_map/ppermute | solution.py:21
  428.6 19.6 %collective-permute-start.37 = (bf16[480,768]{1,0:T(8,128)(2,1)S(1)}, bf16[480,768]{1,0:T(8,128)(2,1)S(1)}, u32[]{:S(2)}, u32[]{:S(2)}) collective-permute-start(bf16[480,768]{1,0:T(8,128)(2,1)S(1)} %constant_dynamic-slice_fusion.9), channel_id=1, source_target_pairs={{0,8},{4,12},{8,0},{12,4},{16,24},{20,28},{24,16},{28,20},{1,9},{5... | collective-permute-start | bytes 2211848 | tf_op jit(solution)/shard_map/ppermute | solution.py:21
  430.1 19.6 %collective-permute-start.39 = (bf16[480,768]{1,0:T(8,128)(2,1)S(1)}, bf16[480,768]{1,0:T(8,128)(2,1)S(1)}, u32[]{:S(2)}, u32[]{:S(2)}) collective-permute-start(bf16[480,768]{1,0:T(8,128)(2,1)S(1)} %constant_dynamic-slice_fusion.7), channel_id=1, source_target_pairs={{0,16},{4,20},{8,24},{12,28},{16,0},{20,4},{24,8},{28,12},{1,17},{... | collective-permute-start | bytes 2211848 | tf_op jit(solution)/shard_map/ppermute | solution.py:21
  432.6 5.9 %collective-permute-start.56 = (bf16[2,96,768]{2,1,0:T(8,128)(2,1)S(1)}, bf16[2,96,768]{2,1,0:T(8,128)(2,1)S(1)}, u32[]{:S(2)}, u32[]{:S(2)}) collective-permute-start(bf16[2,96,768]{2,1,0:T(8,128)(2,1)S(1)} %fusion.64), channel_id=1, source_target_pairs={{0,1},{1,0},{2,3},{3,2},{4,5},{5,4},{6,7},{7,6},{8,9},{9,8},{10,11... | collective-permute-start | bytes 884744 | tf_op jit(solution)/shard_map/ppermute | solution.py:25
  438.6 5.9 %collective-permute-start.57 = (bf16[2,48,768]{2,1,0:T(8,128)(2,1)S(1)}, bf16[2,48,768]{2,1,0:T(8,128)(2,1)S(1)}, u32[]{:S(2)}, u32[]{:S(2)}) collective-permute-start(bf16[2,48,768]{2,1,0:T(8,128)(2,1)S(1)} %constant_dynamic-slice_fusion), channel_id=1, source_target_pairs={{0,2},{1,3},{2,0},{3,1},{4,6},{5,7},{6,4},{7,5},{8,10},{9,11},{10,... | collective-permute-start | bytes 442376 | tf_op jit(solution)/shard_map/ppermute | solution.py:25
  444.5 9.0 %collective-permute-start.58 = (bf16[2,48,768]{2,1,0:T(8,128)(2,1)S(1)}, bf16[2,48,768]{2,1,0:T(8,128)(2,1)S(1)}, u32[]{:S(2)}, u32[]{:S(2)}) collective-permute-start(bf16[2,48,768]{2,1,0:T(8,128)(2,1)S(1)} %add_convert_fusion.19), channel_id=1, source_target_pairs={{0,2},{1,3},{2,0},{3,1},{4,6},{5,7},{6,4},{7,5},{8,10},{9,11},{10,... | collective-permute-start | bytes 442376 | tf_op jit(solution)/shard_map/ppermute | solution.py:25
  448.5 6.4 %collective-permute-start.38 = (bf16[240,768]{1,0:T(8,128)(2,1)S(1)}, bf16[240,768]{1,0:T(8,128)(2,1)S(1)}, u32[]{:S(2)}, u32[]{:S(2)}) collective-permute-start(bf16[240,768]{1,0:T(8,128)(2,1)S(1)} %constant_dynamic-slice_fusion.8), channel_id=1, source_target_pairs={{0,16},{4,20},{8,24},{12,28},{16,0},{20,4},{24,8},{28,12},{1,17},{... | collective-permute-start | bytes 1105928 | tf_op jit(solution)/shard_map/ppermute | solution.py:21
  449.9 6.4 %collective-permute-start.40 = (bf16[240,768]{1,0:T(8,128)(2,1)S(1)}, bf16[240,768]{1,0:T(8,128)(2,1)S(1)}, u32[]{:S(2)}, u32[]{:S(2)}) collective-permute-start(bf16[240,768]{1,0:T(8,128)(2,1)S(1)} %constant_dynamic-slice_fusion.6), channel_id=1, source_target_pairs={{0,8},{4,12},{8,0},{12,4},{16,24},{20,28},{24,16},{28,20},{1,9},{5... | collective-permute-start | bytes 1105928 | tf_op jit(solution)/shard_map/ppermute | solution.py:21
  453.5 6.3 %collective-permute-start.59 = (bf16[2,96,768]{2,1,0:T(8,128)(2,1)S(1)}, bf16[2,96,768]{2,1,0:T(8,128)(2,1)S(1)}, u32[]{:S(2)}, u32[]{:S(2)}) collective-permute-start(bf16[2,96,768]{2,1,0:T(8,128)(2,1)S(1)} %maximum_select_fusion.17), channel_id=1, source_target_pairs={{0,1},{1,0},{2,3},{3,2},{4,5},{5,4},{6,7},{7,6},{8,9},{9,8},{10,11... | collective-permute-start | bytes 884744 | tf_op jit(solution)/shard_map/ppermute | solution.py:25
  456.5 8.3 %collective-permute-start.41 = (bf16[2,120,768]{2,1,0:T(8,128)(2,1)S(1)}, bf16[2,120,768]{2,1,0:T(8,128)(2,1)S(1)}, u32[]{:S(2)}, u32[]{:S(2)}) collective-permute-start(bf16[2,120,768]{2,1,0:T(8,128)(2,1)S(1)} %fusion.55), channel_id=1, source_target_pairs={{0,1},{1,0},{2,3},{3,2},{4,5},{5,4},{6,7},{7,6},{8,9},{9,8},{10,11... | collective-permute-start | bytes 1105928 | tf_op jit(solution)/shard_map/ppermute | solution.py:25
  460.1 8.1 %collective-permute-start.60 = (bf16[192,768]{1,0:T(8,128)(2,1)S(1)}, bf16[192,768]{1,0:T(8,128)(2,1)S(1)}, u32[]{:S(2)}, u32[]{:S(2)}) collective-permute-start(bf16[192,768]{1,0:T(8,128)(2,1)S(1)} %get-tuple-element.116), channel_id=1, source_target_pairs={{0,16},{4,20},{8,24},{12,28},{16,0},{20,4},{24,8},{28,12},{1,17},{... | collective-permute-start | bytes 884744 | tf_op jit(solution)/shard_map/ppermute | solution.py:21
  464.9 7.7 %collective-permute-start.42 = (bf16[2,60,768]{2,1,0:T(8,128)(2,1)S(1)}, bf16[2,60,768]{2,1,0:T(8,128)(2,1)S(1)}, u32[]{:S(2)}, u32[]{:S(2)}) collective-permute-start(bf16[2,60,768]{2,1,0:T(8,128)(2,1)S(1)} %constant_dynamic-slice_fusion.5), channel_id=1, source_target_pairs={{0,2},{1,3},{2,0},{3,1},{4,6},{5,7},{6,4},{7,5},{8,10},{9,11},{10,... | collective-permute-start | bytes 552968 | tf_op jit(solution)/shard_map/ppermute | solution.py:25
  468.3 20.9 %collective-permute-start.61 = (bf16[384,768]{1,0:T(8,128)(2,1)S(1)}, bf16[384,768]{1,0:T(8,128)(2,1)S(1)}, u32[]{:S(2)}, u32[]{:S(2)}) collective-permute-start(bf16[384,768]{1,0:T(8,128)(2,1)S(1)} %maximum_select_fusion.12), channel_id=1, source_target_pairs={{0,8},{4,12},{8,0},{12,4},{16,24},{20,28},{24,16},{28,20},{1,9},{5... | collective-permute-start | bytes 1769480 | tf_op jit(solution)/shard_map/ppermute | solution.py:21
  472.7 8.9 %collective-permute-start.43 = (bf16[2,60,768]{2,1,0:T(8,128)(2,1)S(1)}, bf16[2,60,768]{2,1,0:T(8,128)(2,1)S(1)}, u32[]{:S(2)}, u32[]{:S(2)}) collective-permute-start(bf16[2,60,768]{2,1,0:T(8,128)(2,1)S(1)} %add_convert_fusion.18), channel_id=1, source_target_pairs={{0,2},{1,3},{2,0},{3,1},{4,6},{5,7},{6,4},{7,5},{8,10},{9,11},{10,... | collective-permute-start | bytes 552968 | tf_op jit(solution)/shard_map/ppermute | solution.py:25
  473.5 9.0 %collective-permute-start.62 = (bf16[192,768]{1,0:T(8,128)(2,1)S(1)}, bf16[192,768]{1,0:T(8,128)(2,1)S(1)}, u32[]{:S(2)}, u32[]{:S(2)}) collective-permute-start(bf16[192,768]{1,0:T(8,128)(2,1)S(1)} %get-tuple-element.115), channel_id=1, source_target_pairs={{0,8},{4,12},{8,0},{12,4},{16,24},{20,28},{24,16},{28,20},{1,9},{5... | collective-permute-start | bytes 884744 | tf_op jit(solution)/shard_map/ppermute | solution.py:21
  481.7 16.6 %collective-permute-start.44 = (bf16[2,120,768]{2,1,0:T(8,128)(2,1)S(1)}, bf16[2,120,768]{2,1,0:T(8,128)(2,1)S(1)}, u32[]{:S(2)}, u32[]{:S(2)}) collective-permute-start(bf16[2,120,768]{2,1,0:T(8,128)(2,1)S(1)} %maximum_select_fusion.14), channel_id=1, source_target_pairs={{0,1},{1,0},{2,3},{3,2},{4,5},{5,4},{6,7},{7,6},{8,9},{9,8},{10,11... | collective-permute-start | bytes 1105928 | tf_op jit(solution)/shard_map/ppermute | solution.py:25
  482.7 18.1 %collective-permute-start.63 = (bf16[384,768]{1,0:T(8,128)(2,1)S(1)}, bf16[384,768]{1,0:T(8,128)(2,1)S(1)}, u32[]{:S(2)}, u32[]{:S(2)}) collective-permute-start(bf16[384,768]{1,0:T(8,128)(2,1)S(1)} %maximum_select_fusion.13), channel_id=1, source_target_pairs={{0,16},{4,20},{8,24},{12,28},{16,0},{20,4},{24,8},{28,12},{1,17},{... | collective-permute-start | bytes 1769480 | tf_op jit(solution)/shard_map/ppermute | solution.py:21
  489.7 32.1 %collective-permute-start.64 = (bf16[768,768]{1,0:T(8,128)(2,1)S(1)}, bf16[768,768]{1,0:T(8,128)(2,1)}, u32[]{:S(2)}, u32[]{:S(2)}) collective-permute-start(bf16[768,768]{1,0:T(8,128)(2,1)S(1)} %maximum_select_fusion.2), channel_id=1, source_target_pairs={{0,4},{4,0},{8,12},{12,8},{16,20},{20,16},{24,28},{28,24},{1,5},{5... | collective-permute-start | bytes 3538952 | tf_op jit(solution)/shard_map/ppermute | solution.py:21
  498.7 11.3 %collective-permute-start.45 = (bf16[240,768]{1,0:T(8,128)(2,1)S(1)}, bf16[240,768]{1,0:T(8,128)(2,1)S(1)}, u32[]{:S(2)}, u32[]{:S(2)}) collective-permute-start(bf16[240,768]{1,0:T(8,128)(2,1)S(1)} %get-tuple-element.110), channel_id=1, source_target_pairs={{0,16},{4,20},{8,24},{12,28},{16,0},{20,4},{24,8},{28,12},{1,17},{... | collective-permute-start | bytes 1105928 | tf_op jit(solution)/shard_map/ppermute | solution.py:21
  498.7 14.1 %collective-permute-start.47 = (bf16[240,768]{1,0:T(8,128)(2,1)S(1)}, bf16[240,768]{1,0:T(8,128)(2,1)S(1)}, u32[]{:S(2)}, u32[]{:S(2)}) collective-permute-start(bf16[240,768]{1,0:T(8,128)(2,1)S(1)} %get-tuple-element.109), channel_id=1, source_target_pairs={{0,8},{4,12},{8,0},{12,4},{16,24},{20,28},{24,16},{28,20},{1,9},{5... | collective-permute-start | bytes 1105928 | tf_op jit(solution)/shard_map/ppermute | solution.py:21
  501.2 33.7 %collective-permute-start.65 = (bf16[768,768]{1,0:T(8,128)(2,1)S(1)}, bf16[768,768]{1,0:T(8,128)(2,1)}, u32[]{:S(2)}, u32[]{:S(2)}) collective-permute-start(bf16[768,768]{1,0:T(8,128)(2,1)S(1)} %maximum_select_fusion.3), channel_id=1, source_target_pairs={{0,4},{4,0},{8,12},{12,8},{16,20},{20,16},{24,28},{28,24},{1,5},{5... | collective-permute-start | bytes 3538952 | tf_op jit(solution)/shard_map/ppermute | solution.py:21
  511.1 15.2 %collective-permute-start.46 = (bf16[480,768]{1,0:T(8,128)(2,1)}, bf16[480,768]{1,0:T(8,128)(2,1)}, u32[]{:S(2)}, u32[]{:S(2)}) collective-permute-start(bf16[480,768]{1,0:T(8,128)(2,1)} %maximum_select_fusion.7), channel_id=1, source_target_pairs={{0,8},{4,12},{8,0},{12,4},{16,24},{20,28},{24,16},{28,20},{1,9},{5... | collective-permute-start | bytes 2211848 | tf_op jit(solution)/shard_map/ppermute | solution.py:21
  513.1 19.9 %collective-permute-start.48 = (bf16[480,768]{1,0:T(8,128)(2,1)S(1)}, bf16[480,768]{1,0:T(8,128)(2,1)}, u32[]{:S(2)}, u32[]{:S(2)}) collective-permute-start(bf16[480,768]{1,0:T(8,128)(2,1)S(1)} %maximum_select_fusion.8), channel_id=1, source_target_pairs={{0,16},{4,20},{8,24},{12,28},{16,0},{20,4},{24,8},{28,12},{1,17},{... | collective-permute-start | bytes 2211848 | tf_op jit(solution)/shard_map/ppermute | solution.py:21
  528.6 13.0 %collective-permute-start.49 = (bf16[960,768]{1,0:T(8,128)(2,1)S(1)}, bf16[960,768]{1,0:T(8,128)(2,1)S(1)}, u32[]{:S(2)}, u32[]{:S(2)}) collective-permute-start(bf16[960,768]{1,0:T(8,128)(2,1)S(1)} %maximum_select_fusion), channel_id=1, source_target_pairs={{0,4},{4,0},{8,12},{12,8},{16,20},{20,16},{24,28},{28,24},{1,5},{5... | collective-permute-start | bytes 4423688 | tf_op jit(solution)/shard_map/ppermute | solution.py:21
  534.8 6.9 %collective-permute-start.50 = (bf16[960,768]{1,0:T(8,128)(2,1)S(1)}, bf16[960,768]{1,0:T(8,128)(2,1)S(1)}, u32[]{:S(2)}, u32[]{:S(2)}) collective-permute-start(bf16[960,768]{1,0:T(8,128)(2,1)S(1)} %maximum_select_fusion.1), channel_id=1, source_target_pairs={{0,4},{4,0},{8,12},{12,8},{16,20},{20,16},{24,28},{28,24},{1,5},{5... | collective-permute-start | bytes 4423688 | tf_op jit(solution)/shard_map/ppermute | solution.py:21
  (73 other events, 854.6 us)

commit v2 on v1

--- a/solution.py
+++ b/solution.py
@@ -1,6 +1,9 @@
+import functools
 import jax
 import jax.numpy as jnp
 from jax import lax
+from jax.experimental import pallas as pl
+from jax.experimental.pallas import tpu as pltpu
 from jax.sharding import PartitionSpec as P
 
 HEADS = 12
@@ -9,11 +12,364 @@
 MEMBERS = 4
 LOCAL_HEADS = HEADS // MEMBERS
 WIDTH = LOCAL_HEADS * HD
-
 NEG_FILL = -32768.0
 EPSILON = 1e-06
 BF16 = jnp.bfloat16
 F32 = jnp.float32
+TILE = 256
+LANES = 128
+VMEM = pltpu.VMEM
+
+
+def dot(left, right):
+    return jnp.dot(left, right, preferred_element_type=F32)
+
+
+def dot_nt(left, right):
+    return lax.dot_general(left, right, (((1,), (1,)), ((), ())), preferred_element_type=F32)
+
+
+def dot_tn(left, right):
+    return lax.dot_general(left, right, (((0,), (0,)), ((), ())), preferred_element_type=F32)
+
+
+def params(limit=60 << 20, **more):
+    return pltpu.CompilerParams(vmem_limit_bytes=limit, **more)
+
+
+def whole(*shape):
+    return pl.BlockSpec(shape, lambda *_: (0,) * len(shape))
+
+
+def normalized(values):
+    centered = values - jnp.mean(values, axis=-1, keepdims=True)
+    inverse = lax.rsqrt(jnp.mean(centered * centered, axis=-1, keepdims=True) + EPSILON)
+    return centered * inverse, inverse
+
+
+def project_kernel(x0, x1, x2, x3, mask, gain, shift, w, wt, bias, bias_col, normed, qa, ka, va, qn, kt, vt):
+    rows = x0.shape[0]
+    total = MEMBERS * rows
+    padded = qa.shape[2]
+    step = rows // 3
+    for d, x in enumerate((x0, x1, x2, x3)):
+
+        def some(i, carry, d=d, x=x):
+            here = x[pl.ds(i * step, step), :].astype(F32)
+            unit, _ = normalized(here)
+            normed[pl.ds(d * rows + i * step, step), :] = (unit * gain[...] + shift[...]).astype(BF16)
+            return carry
+
+        lax.fori_loop(0, 3, some, 0)
+    for d in range(MEMBERS):
+        here = pl.ds(d * rows, rows)
+        natural = dot(normed[here, :], w[...]) + bias[...]
+        lane = lax.broadcasted_iota(jnp.int32, (rows, HD), 1)
+        low_mask = NEG_FILL * (1.0 - mask[here, :])
+        key_tail = jnp.where(lane == 0, low_mask, jnp.where(lane < 4, 1.0, 0.0)).astype(BF16)
+        value_tail = jnp.where(lane < 3, 1.0, 0.0).astype(BF16)
+        for h in range(LOCAL_HEADS):
+            at = h * HD
+            qn[h, here, :] = (natural[:, at : at + HD] * HD ** (-0.5)).astype(BF16)
+            ka[h, here, :HD] = natural[:, WIDTH + at : WIDTH + at + HD].astype(BF16)
+            ka[h, here, HD:] = key_tail
+            va[h, here, :HD] = natural[:, 2 * WIDTH + at : 2 * WIDTH + at + HD].astype(BF16)
+            va[h, here, HD:] = value_tail
+    turned = dot_nt(wt[...], normed[...]) + bias_col[...]
+    row = lax.broadcasted_iota(jnp.int32, (HD, padded), 0)
+    query_tail = jnp.where(row == 0, 1.0, 0.0).astype(BF16)
+    for h in range(LOCAL_HEADS):
+        at = h * HD
+        qn[h, total:, :] = jnp.zeros((padded - total, HD), BF16)
+        qa[h, :HD, :total] = (turned[at : at + HD] * HD ** (-0.5)).astype(BF16)
+        qa[h, :HD, total:] = jnp.zeros((HD, padded - total), BF16)
+        qa[h, HD:, :] = query_tail
+        kt[h] = turned[WIDTH + at : WIDTH + at + HD].astype(BF16)
+        vt[h] = turned[2 * WIDTH + at : 2 * WIDTH + at + HD].astype(BF16)
+
+
+def project(x_blocks, mask, gain, shift, w, bias):
+    rows, model = x_blocks[0].shape
+    total = MEMBERS * rows
+    padded = -(-total // TILE) * TILE
+    n = LOCAL_HEADS
+    outs = [
+        jax.ShapeDtypeStruct((total, model), BF16),
+        jax.ShapeDtypeStruct((n, 2 * HD, padded), BF16),
+        jax.ShapeDtypeStruct((n, total, 2 * HD), BF16),
+        jax.ShapeDtypeStruct((n, total, 2 * HD), BF16),
+        jax.ShapeDtypeStruct((n, padded, HD), BF16),
+        jax.ShapeDtypeStruct((n, HD, total), BF16),
+        jax.ShapeDtypeStruct((n, HD, total), BF16),
+    ]
+    flops = 4 * total * model * 3 * WIDTH
+    return pl.pallas_call(
+        project_kernel,
+        out_shape=outs,
+        in_specs=[pl.BlockSpec(memory_space=VMEM)] * 11,
+        out_specs=[pl.BlockSpec(memory_space=VMEM)] * len(outs),
+        compiler_params=params(),
+        cost_estimate=pl.CostEstimate(flops=flops, bytes_accessed=12 << 20, transcendentals=0),
+        name="project",
+    )(*x_blocks, mask, gain[None, :], shift[None, :], w, w.T, bias[None, :], bias[:, None])
+
+
+def forward_kernel(qa, ka, vt, low, turned, logs, held):
+    head = pl.program_id(0)
+    total = ka.shape[1]
+    tiles = qa.shape[2] // TILE
+
+    def some(i, carry):
+        here = pl.ds(pl.multiple_of(i * TILE, TILE), TILE)
+        scores = dot(ka[0], qa[0, :, here])
+        peak = jnp.max(scores, axis=0, keepdims=True)
+        weights = jnp.exp(scores - peak)
+        sums = jnp.sum(weights, axis=0, keepdims=True)
+        mixed = dot(vt[0], weights.astype(BF16)) * (1.0 / sums)
+        turned[0, :, here] = mixed
+        logs[0, :, here] = peak + jnp.log(sums)
+        held[here, :] = mixed.T.astype(BF16)
+        return carry
+
+    lax.fori_loop(0, tiles, some, 0)
+    for h in range(LOCAL_HEADS):
+
+        @pl.when(head == h)
+        def _(h=h):
+            low[:, h * HD : (h + 1) * HD] = held[:total, :]
+
+
+def attend(qa, ka, vt):
+    n, total, _ = ka.shape
+    padded = qa.shape[2]
+    per_head = lambda *shape: pl.BlockSpec((1,) + shape, lambda h: (h, 0, 0))
+    return pl.pallas_call(
+        forward_kernel,
+        grid=(n,),
+        out_shape=[
+            jax.ShapeDtypeStruct((total, WIDTH), BF16),
+            jax.ShapeDtypeStruct((n, HD, padded), F32),
+            jax.ShapeDtypeStruct((n, 1, padded), F32),
+        ],
+        in_specs=[per_head(2 * HD, padded), per_head(total, 2 * HD), per_head(HD, total)],
+        out_specs=[whole(total, WIDTH), per_head(HD, padded), per_head(1, padded)],
+        scratch_shapes=[VMEM((padded, HD), BF16)],
+        compiler_params=params(),
+        cost_estimate=pl.CostEstimate(flops=16 * n * total * total * HD, bytes_accessed=8 << 20, transcendentals=n * total * total),
+        name="attend",
+    )(qa, ka, vt)
+
+
+def three_parts(row):
+    high = row.astype(BF16).astype(F32)
+    rest = row - high
+    middle = rest.astype(BF16).astype(F32)
+    return high, middle, rest - middle
+
+
+def backward_kernel(qa, ka, va, qn, kt, turned, logs, g0, g1, g2, g3, out, held_g, held_q, sum_k, sum_v):
+    head = pl.program_id(0)
+    rows = g0.shape[0]
+    total = ka.shape[1]
+    padded = qa.shape[2]
+    tiles = padded // TILE
+    for h in range(LOCAL_HEADS):
+
+        @pl.when(head == h)
+        def _(h=h):
+            for d, part in enumerate((g0, g1, g2, g3)):
+                held_g[d * rows : (d + 1) * rows, :] = part[:, h * HD : (h + 1) * HD]
+
+    held_g[total:, :] = jnp.zeros((padded - total, HD), BF16)
+    sum_k[...] = jnp.zeros_like(sum_k)
+    sum_v[...] = jnp.zeros_like(sum_v)
+    row = lax.broadcasted_iota(jnp.int32, (HD, TILE), 0)
+
+    def some(i, carry):
+        here = pl.ds(pl.multiple_of(i * TILE, TILE), TILE)
+        grad = held_g[here, :]
+        grad_turned = grad.astype(F32).T
+        delta = jnp.sum(grad_turned * turned[0, :, here], axis=0, keepdims=True)
+        high, middle, least = three_parts(-logs[0, :, here])
+        tail = jnp.where(row == 0, 1.0, jnp.where(row == 1, high, jnp.where(row == 2, middle, jnp.where(row == 3, least, 0.0))))
+        query = jnp.concatenate([qa[0, :HD, here], tail.astype(BF16)], axis=0)
+        probs = jnp.exp(dot(ka[0], query))
+        high, middle, least = three_parts(-delta)
+        tail = jnp.where(row == 0, high, jnp.where(row == 1, middle, jnp.where(row == 2, least, 0.0)))
+        grad_tail = jnp.concatenate([grad_turned, tail], axis=0).astype(BF16)
+        grad_scores = (probs * dot(va[0], grad_tail)).astype(BF16)
+        sum_v[...] += dot(probs.astype(BF16), grad)
+        sum_k[...] += dot(grad_scores, qn[0, here, :])
+        query_grad = dot(kt[0], grad_scores) * HD ** (-0.5)
+        held_q[here, :] = query_grad.T.astype(BF16)
+        return carry
+
+    lax.fori_loop(0, tiles, some, 0)
+    for h in range(LOCAL_HEADS):
+
+        @pl.when(head == h)
+        def _(h=h):
+            at = h * HD
+            out[:, at : at + HD] = held_q[:total, :]
+            out[:, WIDTH + at : WIDTH + at + HD] = sum_k[...].astype(BF16)
+            out[:, 2 * WIDTH + at : 2 * WIDTH + at + HD] = sum_v[...].astype(BF16)
+
+
+def attend_back(qa, ka, va, qn, kt, turned, logs, grads):
+    n, total, _ = ka.shape
+    padded = qa.shape[2]
+    rows = grads[0].shape[0]
+    per_head = lambda *shape: pl.BlockSpec((1,) + shape, lambda h: (h, 0, 0))
+    return pl.pallas_call(
+        backward_kernel,
+        grid=(n,),
+        out_shape=jax.ShapeDtypeStruct((total, 3 * WIDTH), BF16),
+        in_specs=[
+            per_head(2 * HD, padded),
+            per_head(total, 2 * HD),
+            per_head(total, 2 * HD),
+            per_head(padded, HD),
+            per_head(HD, total),
+            per_head(HD, padded),
+            per_head(1, padded),
+        ]
+        + [whole(rows, WIDTH)] * MEMBERS,
+        out_specs=whole(total, 3 * WIDTH),
+        scratch_shapes=[
+            VMEM((padded, HD), BF16),
+            VMEM((padded, HD), BF16),
+            VMEM((total, HD), F32),
+            VMEM((total, HD), F32),
+        ],
+        compiler_params=params(),
+        cost_estimate=pl.CostEstimate(flops=40 * n * total * total * HD, bytes_accessed=12 << 20, transcendentals=n * total * total),
+        name="attend_back",
+    )(qa, ka, va, qn, kt, turned, logs, *grads)
+
+
+def middle_kernel(
+    side, x, a0, a1, a2, a3, wo, out_bias, gain, shift, cot, valid, down_bias, up, up_bias, down,
+    layer, down_send, down_keep, rest_send, rest_keep, grad_up_bias, grad_hidden, g0, g1, g2, g3, vectors,
+    hidden, normed, grad_down, total_out, total_grad,
+):
+    step = pl.program_id(0)
+    last = pl.num_programs(0) - 1
+    half = pl.num_programs(0) // 2
+    model = x.shape[1]
+
+    @pl.when(step == 0)
+    def _():
+        value = x[...].astype(F32) + out_bias[...]
+        for e, part in enumerate((a0, a1, a2, a3)):
+            value += dot(part[...], wo[e])
+        hidden[...] = value
+        unit, _ = normalized(value)
+        normed[...] = (unit * gain[...] + shift[...]).astype(BF16)
+        low = (valid[...] * cot[...].astype(F32)).astype(BF16)
+        grad_down[...] = low
+        vectors[3:4, :] = jnp.sum(low.astype(F32), axis=0, keepdims=True)
+        total_out[...] = value + down_bias[...]
+        total_grad[...] = jnp.zeros_like(total_grad)
+
+    gate = dot(normed[...], up[...]) + up_bias[0]
+    below = 0.5 * (1.0 + lax.erf(gate * (0.5**0.5)))
+    active = (gate * below).astype(BF16)
+    slope = below + gate * (jnp.exp(-0.5 * gate * gate) * (0.5 / jnp.pi) ** 0.5)
+    low = grad_down[...]
+    grad_gate = (dot_nt(low, down[...]) * slope).astype(BF16)
+    total_out[...] += dot(active, down[...])
+    total_grad[...] += dot_nt(grad_gate, up[...])
+    grad_up_bias[0] = jnp.sum(grad_gate.astype(F32), axis=0, keepdims=True)
+    of_down = dot_tn(active, low).astype(BF16)
+    of_up = dot_tn(normed[...], grad_gate).astype(BF16)
+    for i in range(2 * half):
+
+        @pl.when(step == i)
+        def _(i=i):
+            if i < half:
+                down_send[...] = of_down
+                rest_send[i * model : (i + 1) * model, :] = of_up
+            else:
+                down_keep[...] = of_down
+                rest_keep[(i - half) * model : (i - half + 1) * model, :] = of_up
+
+    @pl.when(step == last)
+    def _():
+        unit, inverse = normalized(hidden[...])
+        layer[...] = (valid[...] * total_out[...]).astype(BF16)
+        grad = total_grad[...]
+        vectors[0:1, :] = jnp.sum(grad * unit, axis=0, keepdims=True)
+        vectors[1:2, :] = jnp.sum(grad, axis=0, keepdims=True)
+        scaled = grad * gain[...]
+        inner = scaled - jnp.mean(scaled, axis=-1, keepdims=True)
+        inner = inner - unit * jnp.mean(scaled * unit, axis=-1, keepdims=True)
+        grad = grad_down[...].astype(F32) + inverse * inner
+        grad_hidden[...] = grad
+        branch = grad.astype(BF16)
+        vectors[2:3, :] = jnp.sum(branch.astype(F32), axis=0, keepdims=True)
+        parts = (a0, a1, a2, a3)
+        for e, given in enumerate((g0, g1, g2, g3)):
+            given[...] = dot_nt(branch, wo[e]).astype(BF16)
+            place = half * model + (side[1] ^ (e & 1)) * WIDTH
+            held = rest_keep if e < 2 else rest_send
+            held[pl.ds(pl.multiple_of(place, WIDTH), WIDTH), :] = dot_tn(parts[e][...], branch).astype(BF16)
+
+
+def middle(core, near, x, attended, wo, out_bias, gain, shift, cot, valid, down_bias, up, up_bias, down):
+    rows, model = x.shape
+    blocks = up.shape[1] // model
+    half = blocks // 2
+
+    def block_of(i, side):
+        return lax.rem(i, half) + half * jnp.where(i < half, 1 - side[0], side[0])
+
+    whole_s = lambda *shape: pl.BlockSpec(shape, lambda i, side: (0,) * len(shape))
+    rest_rows = half * model + 2 * WIDTH
+    shaped = jax.ShapeDtypeStruct
+    outs = [
+        (shaped((rows, model), BF16), whole_s(rows, model)),
+        (shaped((half * model, model), BF16), pl.BlockSpec((model, model), lambda i, side: (jnp.minimum(i, half - 1), 0))),
+        (shaped((half * model, model), BF16), pl.BlockSpec((model, model), lambda i, side: (jnp.maximum(i - half, 0), 0))),
+        (shaped((rest_rows, model), BF16), whole_s(rest_rows, model)),
+        (shaped((rest_rows, model), BF16), whole_s(rest_rows, model)),
+        (shaped((blocks, 1, model), F32), pl.BlockSpec((1, 1, model), lambda i, side: (block_of(i, side), 0, 0))),
+        (shaped((rows, model), F32), whole_s(rows, model)),
+    ]
+    outs += [(shaped((rows, WIDTH), BF16), whole_s(rows, WIDTH))] * MEMBERS
+    outs += [(shaped((4, model), F32), whole_s(4, model))]
+    return pl.pallas_call(
+        middle_kernel,
+        out_shape=[o[0] for o in outs],
+        grid_spec=pltpu.PrefetchScalarGridSpec(
+            num_scalar_prefetch=1,
+            grid=(blocks,),
+            in_specs=[whole_s(rows, model)]
+            + [whole_s(rows, WIDTH)] * MEMBERS
+            + [whole_s(MEMBERS, WIDTH, model)]
+            + [whole_s(1, model)] * 3
+            + [whole_s(rows, model), whole_s(rows, 1), whole_s(1, model)]
+            + [
+                pl.BlockSpec((model, model), lambda i, side: (0, block_of(i, side))),
+                pl.BlockSpec((1, 1, model), lambda i, side: (block_of(i, side), 0, 0)),
+                pl.BlockSpec((model, model), lambda i, side: (block_of(i, side), 0)),
+            ],
+            out_specs=[o[1] for o in outs],
+            scratch_shapes=[
+                VMEM((rows, model), F32),
+                VMEM((rows, model), BF16),
+                VMEM((rows, model), BF16),
+                VMEM((rows, model), F32),
+                VMEM((rows, model), F32),
+            ],
+        ),
+        compiler_params=params(),
+        cost_estimate=pl.CostEstimate(flops=12 * rows * model * model * blocks, bytes_accessed=25 << 20, transcendentals=2 * rows * model * blocks),
+        name="middle",
+    )(
+        jnp.stack([core, near]).astype(jnp.int32),
+        x, *attended, wo, out_bias[None], gain[None], shift[None], cot, valid, down_bias[None],
+        up, up_bias.reshape(blocks, 1, model), down,
+    )
 
 
 def over_cube(value, bit):
@@ -112,14 +468,6 @@
     centered = values - jnp.mean(values, axis=-1, keepdims=True)
     normed = centered * lax.rsqrt(jnp.mean(centered * centered, axis=-1, keepdims=True) + EPSILON)
     return normed * gain_vec + shift_vec
-
-
-def gelu_exact(values):
-    return jax.nn.gelu(values, approximate=False)
-
-
-def matmul_rows(left_side, right_side):
-    return jnp.dot(left_side, right_side, preferred_element_type=F32)
 
 
 def matmul_back(left_side, right_side):
@@ -158,7 +506,6 @@
 ):
     _, rows, model = inputs.shape
     hidden_units = up_weight.shape[1]
-    head_scale = HD ** (-0.5)
     cube, blk = lax.axis_index("cube"), lax.axis_index("blk")
     core = cube & 1
     at_home = core == (blk >> 1)
@@ -180,91 +527,51 @@
     x_blocks = from_group(inputs[0])
     valid_blocks = from_group(valid_here)
     cot_own = moved(cotangent[0])
-    x_all = jnp.concatenate(x_blocks).astype(F32)
-    valid_all = jnp.concatenate(valid_blocks, axis=1)[0].astype(F32)
-    key_bias = NEG_FILL * (1.0 - valid_all)
-    residual_in = x_blocks[0].astype(F32)
+    valid_all = jnp.concatenate(valid_blocks, axis=1).astype(F32).reshape(-1, 1)
 
     in_columns = jnp.concatenate(
         [member_columns(input_weight[:, s * model : (s + 1) * model], member, 1) for s in range(3)],
         axis=1,
     )
     bias_columns = member_columns(input_bias, member, 1)
-    out_rows = [member_columns(output_weight, member ^ e, 0) for e in range(MEMBERS)]
-
-    normed_low = layer_norm(x_all, pre_gain, pre_shift).astype(BF16)
-    projected = matmul_rows(normed_low, in_columns)
-    total_rows = projected.shape[0]
-    heads_shape = (total_rows, LOCAL_HEADS, HD)
-    query = (projected[:, :WIDTH] + bias_columns[0]).astype(BF16).reshape(heads_shape)
-    key = projected[:, WIDTH : 2 * WIDTH].astype(BF16).reshape(heads_shape)
-    value = (projected[:, 2 * WIDTH :] + bias_columns[1]).astype(BF16).reshape(heads_shape)
-
-    def scores():
-        raw = jnp.einsum("qhd,khd->hqk", query, key, preferred_element_type=F32)
-        return raw * head_scale + key_bias
-
-    peak = jnp.max(scores(), axis=2)
-    weights = jnp.exp(scores() - peak[..., None])
-    total = jnp.sum(weights, axis=2)
-    attended_heads = (
-        jnp.einsum("hqk,khd->hqd", weights.astype(BF16), value, preferred_element_type=F32)
-        / total[..., None]
-    )
-    log_total = peak + jnp.log(total)
-    attended_own = (
-        jnp.transpose(attended_heads, (1, 0, 2)).reshape(MEMBERS, rows, WIDTH).astype(BF16)
-    )
-    attended = exchanged([attended_own[d] for d in range(MEMBERS)])
-
-    hidden = residual_in + output_bias
-    for part, weight_part in zip(attended, out_rows):
-        hidden = hidden + matmul_rows(part, weight_part)
-    normed_mid, mid_back = jax.vjp(layer_norm, hidden, mid_gain, mid_shift)
-    normed_mid_low = normed_mid.astype(BF16)
-    gate_pre = matmul_rows(normed_mid_low, up_weight) + up_bias
-    activated, gelu_back = jax.vjp(gelu_exact, gate_pre)
-    activated_low = activated.astype(BF16)
-    result = hidden + matmul_rows(activated_low, down_weight) + down_bias
-    valid_own = valid_all[:rows, None]
-    layer_out = moved((valid_own * result).astype(BF16))
-    grad_out = valid_own * cot_own.astype(F32)
-    grad_down_low = grad_out.astype(BF16)
-    grad_down_bias = column_sums(grad_down_low)
-    (grad_gate,) = gelu_back(matmul_back(grad_down_low, down_weight))
-    grad_gate_low = grad_gate.astype(BF16)
-
-    down_halves = [
-        weight_grad(half_of(activated_low, side, 1), grad_down_low).astype(BF16)
-        for side in (core, 1 - core)
-    ]
-    grad_up_bias = column_sums(grad_gate_low)
-    grad_mid, grad_mid_gain, grad_mid_shift = mid_back(matmul_back(grad_gate_low, up_weight))
-    grad_hidden = grad_out + grad_mid
-    grad_branch_low = grad_hidden.astype(BF16)
-    grad_output_bias = column_sums(grad_branch_low)
-    grad_attended = exchanged([matmul_back(grad_branch_low, part).astype(BF16) for part in out_rows])
-
+    bias_columns = jnp.concatenate([bias_columns[0], jnp.zeros((WIDTH,), F32), bias_columns[1]])
+    out_rows = jnp.stack([member_columns(output_weight, member ^ e, 0) for e in range(MEMBERS)])
+
+    normed_low, qa, ka, va, qn, kt, vt = project(
+        x_blocks, valid_all, pre_gain, pre_shift, in_columns, bias_columns
+    )
+    attended_own, turned, logs = attend(qa, ka, vt)
+    attended = exchanged([attended_own[d * rows : (d + 1) * rows] for d in range(MEMBERS)])
+    (
+        layer_here,
+        down_send,
+        down_keep,
+        rest_send,
+        rest_keep,
+        grad_up_bias,
+        grad_hidden,
+        *grad_attended,
+        middle_vectors,
+    ) = middle(
+        core,
+        blk & 1,
+        x_blocks[0],
+        attended,
+        out_rows,
+        output_bias,
+        mid_gain,
+        mid_shift,
+        cot_own,
+        valid_all[:rows],
+        down_bias,
+        up_weight,
+        up_bias,
+        down_weight,
+    )
+    layer_out = moved(layer_here)
     blocks = hidden_units // model
-
-    def up_half(side):
-        gate_half = half_of(grad_gate_low, side, 1)
-        return [
-            weight_grad(normed_mid_low, gate_half[:, s * model : (s + 1) * model]).astype(BF16)
-            for s in range(blocks // 2)
-        ]
-
-    def out_half(side):
-        parts = []
-        for which in range(MEMBERS // 2):
-            away = (2 * side + which) ^ member
-            rows_here = lax.dynamic_index_in_dim(jnp.stack(attended), away, 0, keepdims=False)
-            parts.append(weight_grad(rows_here, grad_branch_low).astype(BF16))
-        return parts
-
-    rest_halves = [jnp.concatenate(up_half(side) + out_half(side)) for side in (core, 1 - core)]
-    down_sum = summed_everywhere(down_halves[0], down_halves[1], cube, blk)
-    rest_sum = summed_everywhere(rest_halves[0], rest_halves[1], cube, blk)
+    down_sum = summed_everywhere(down_keep, down_send, cube, blk)
+    rest_sum = summed_everywhere(rest_keep, rest_send, cube, blk)
     grad_down_weight = jnp.concatenate(down_sum).astype(F32)
     up_rows = blocks // 2 * model
     grad_up_weight = jnp.concatenate(
@@ -277,22 +584,7 @@
     ).astype(F32)
     grad_output_weight = jnp.concatenate([half[up_rows:] for half in rest_sum]).astype(F32)
 
-    grad_rows = jnp.concatenate(grad_attended).reshape(heads_shape)
-    row_delta = jnp.einsum("qhd,hqd->hq", grad_rows.astype(F32), attended_heads)
-    probs = jnp.exp(scores() - log_total[..., None])
-    grad_probs = jnp.einsum("qhd,khd->hqk", grad_rows, value, preferred_element_type=F32)
-    grad_scores = (probs * (grad_probs - row_delta[..., None])).astype(BF16)
-    grad_query = jnp.einsum("hqk,khd->qhd", grad_scores, key, preferred_element_type=F32)
-    grad_key = jnp.einsum("hqk,qhd->khd", grad_scores, query, preferred_element_type=F32)
-    grad_value = jnp.einsum("hqk,qhd->khd", probs.astype(BF16), grad_rows, preferred_element_type=F32)
-    grad_columns = jnp.concatenate(
-        [
-            (grad_query * head_scale).astype(BF16).reshape(total_rows, WIDTH),
-            (grad_key * head_scale).astype(BF16).reshape(total_rows, WIDTH),
-            grad_value.astype(BF16).reshape(total_rows, WIDTH),
-        ],
-        axis=1,
-    )
+    grad_columns = attend_back(qa, ka, va, qn, kt, turned, logs, exchanged(grad_attended))
     grad_in = weight_grad(normed_low, grad_columns)
     column_total = column_sums(grad_columns)
 
@@ -300,7 +592,7 @@
     near_sum = added(partial[1], over_cube(partial[3], 0))
     own_sum = partial[0].astype(F32) + over_cube(partial[2], 0).astype(F32)
     grad_normed = own_sum + over_blk(near_sum, 0).astype(F32)
-    _, pre_back = jax.vjp(layer_norm, residual_in, pre_gain, pre_shift)
+    _, pre_back = jax.vjp(layer_norm, x_blocks[0].astype(F32), pre_gain, pre_shift)
     grad_pre, grad_pre_gain, grad_pre_shift = pre_back(grad_normed)
     grad_here = grad_hidden + grad_pre
     input_grad = jnp.where(
@@ -335,16 +627,8 @@
     )
     vectors = jnp.concatenate(
         [
-            jnp.stack(
-                [
-                    grad_pre_gain,
-                    grad_pre_shift,
-                    grad_output_bias,
-                    grad_mid_gain,
-                    grad_mid_shift,
-                    grad_down_bias,
-                ]
-            ),
+            jnp.stack([grad_pre_gain, grad_pre_shift]),
+            middle_vectors,
             spread_bias,
             grad_up_bias.reshape(blocks, model),
         ]
@@ -358,9 +642,9 @@
         grad_input_weight,
         vectors[6:8],
         grad_output_weight,
+        vectors[4],
         vectors[2],
         vectors[3],
-        vectors[4],
         grad_up_weight,
         vectors[8:].reshape(-1),
         grad_down_weight,

time: 561 us -> 490 us (0.87)
  matrix products: 153 us -> 5.38 us
  Pallas kernels: 0 us -> 100 us
  other arithmetic: 83.4 us -> 58.6 us
    dot_general x13 -> x0, matrix products: 119 us -> none  [the longest x7 23.2 us: matmul_rows(): return jnp.dot(left_side, right_side, preferred_element_type=F32)]
    pallas_call x0 -> x4, Pallas kernels: none -> 100 us  [the longest x1 33.7 us: attend_back(): pl.pallas_call(backward_kernel, grid=(n,), out_shape=jax.ShapeDtypeStruct...]
    reduce_sum x1 -> x0, other arithmetic: 16 us -> none  [body(): total = jnp.sum(weights, axis=2)]
    dot_general x11 -> x1, matrix products: 16.5 us -> 1.93 us  [weight_grad(): jnp.einsum('rd,rf->df', left_side, right_side, preferred_element_type=F32)]
    dot_general x7 -> x1, matrix products: 17.7 us -> 3.46 us  [matmul_back(): jnp.einsum('rf,df->rd', left_side, right_side, preferred_element_type=F32)]
    unnamed x156 -> x84, local copies, waits for them, and re-layouts: 18.4 us -> 21.8 us
  transfers between devices with their start and end apart: 66 -> 66, of which waited for: 32 -> 29; matrix products, arithmetic and copies ran while one was open for 31% -> 21% of each run, Pallas kernels for 0% -> 15%
where the time goes in v2:
time: 490 us; the launch traced here: 481 us
  waiting for transfers between devices  126 us (26%)
  starting transfers between devices  101 us (21%)
  Pallas kernels  100 us (20%)
  other arithmetic  58.6 us (12%)
  local copies, waits for them, and re-layouts  49 us (10%)
  blocking collectives  38.9 us (8%)
  matrix products  5.38 us (1%)
    ppermute x41, starting transfers between devices, over_cube(): lax.ppermute(value, 'cube', [(i, i ^ 1 << bit) for i in range(count)])  62.2 us
    ppermute x16, waiting for transfers between devices, over_blk(): lax.ppermute(value, 'blk', [(i, i ^ 1 << bit) for i in range(MEMBERS)])  57.9 us
    ppermute x41, waiting for transfers between devices, over_cube(): lax.ppermute(value, 'cube', [(i, i ^ 1 << bit) for i in range(count)])  47 us
    psum x1, blocking collectives, body(): vectors = lax.psum(vectors, ('cube', 'blk'))  38.9 us
    pallas_call x1, Pallas kernels, attend_back(): pl.pallas_call(backward_kernel, grid=(n,), out_shape=jax.ShapeDtypeStruct...  33.7 us
    ppermute x9, starting transfers between devices, sent_between(): lax.ppermute(value, ('cube', 'blk'), chosen_pairs(is_home, cube_flip, blk...  30 us
    pallas_call x1, Pallas kernels, attend(): pl.pallas_call(forward_kernel, grid=(n,), out_shape=[jax.ShapeDtypeStruct...  27.9 us
    pallas_call x1, Pallas kernels, middle(): pl.pallas_call(middle_kernel, out_shape=[o[0] for o in outs], grid_spec=p...  27.3 us
  transfers between devices with their start and end apart: 66, of which 29 were waited for; matrix products, arithmetic and copies ran while one was open for 21% of the time, Pallas kernels for 15%

profile of v2, /device:TPU:1, one launch (start us, length us, event | category | flops | bytes accessed | tf_op | source)
XLA Modules:
  0.0 481.2 jit_solution(10145449358606256264)
XLA Ops:
  0.6 5.6 %collective-permute-start = (bf16[432,768]{1,0:T(8,128)(2,1)}, bf16[432,768]{1,0:T(8,128)(2,1)}, u32[]{:S(2)}, u32[]{:S(2)}) collective-permute-start(bf16[432,768]{1,0:T(8,128)(2,1)} %bitcast.79), channel_id=1, source_target_pairs={{2,4},{3,5},{4,2},{5,3},{10,12},{11,13},{12,10},{13,11},{18,20},{1... | collective-permute-start | bytes 1990664 | tf_op jit(solution)/shard_map/ppermute | solution.py:394
  11.2 4.5 collective-permute-start.14
  15.8 2.2 fusion.32
  18.4 7.4 %collective-permute-done = bf16[432,768]{1,0:T(8,128)(2,1)} collective-permute-done((bf16[432,768]{1,0:T(8,128)(2,1)}, bf16[432,768]{1,0:T(8,128)(2,1)}, u32[]{:S(2)}, u32[]{:S(2)}) %collective-permute-start) | collective-permute-done | bytes 663584 | tf_op jit(solution)/shard_map/ppermute | solution.py:394
  25.7 2.9 collective-permute-start.2
  34.5 8.9 %collective-permute-done.2 = bf16[432,768]{1,0:T(8,128)(2,1)} collective-permute-done((bf16[432,768]{1,0:T(8,128)(2,1)}, bf16[432,768]{1,0:T(8,128)(2,1)}, u32[]{:S(2)}, u32[]{:S(2)}) %collective-permute-start.2) | collective-permute-done | bytes 663584 | tf_op jit(solution)/shard_map/ppermute | solution.py:394
  47.5 2.3 collective-permute-done.7
  55.2 11.3 %project.1 = (bf16[1728,768]{1,0:T(8,128)(2,1)}, bf16[3,128,1792]{2,1,0:T(8,128)(2,1)}, bf16[3,1728,128]{2,1,0:T(8,128)(2,1)}, bf16[3,1728,128]{2,1,0:T(8,128)(2...) custom-call(bf16[432,768]{1,0:T(8,128)(2,1)} %copy-done, ...), custom_call_target="tpu_custom_call" | custom-call | flops 3057647616 | bytes 12582912 | tf_op jit(solution)/shard_map/project/pallas_call | solution.py:106
  66.5 27.9 %attend.1 = (bf16[1728,192]{1,0:T(8,128)(2,1)}, f32[3,64,1792]{2,1,0:T(8,128)}, f32[3,1,1792]{2,1,0:T(1,128)}) custom-call(bf16[3,128,1792]{2,1,0:T(8,128)(2,1)} %get-tuple-element.36.qa, bf16[3,1728,128]{2,1,0:T(8,128)(2,1)} %get-tuple-element.37.ka, bf16[3,64,1728]{2,1,0:T(8,128)(2,1)} %get-tuple-element.38.vt), custom_call_target="tpu_custom_call" | custom-call | flops 9172942848 | bytes 8388608 | tf_op jit(solution)/shard_map/attend/pallas_call | solution.py:146
  94.5 2.0 fusion.39
  104.4 2.0 broadcast_select_fusion.8.cot
  106.4 2.9 collective-permute-done.10.a1
  110.1 27.3 %middle.1 = (bf16[432,768]{1,0:T(8,128)(2,1)}, bf16[1536,768]{1,0:T(8,128)(2,1)}, bf16[1536,768]{1,0:T(8,128)(2,1)}, bf16[1920,768]{1,0:T(8,128)(2,1)}, bf16[192...) custom-call(s32[2]{0:T(128)} %pad_add_fusion.side, ...), custom_call_target="tpu_custom_call" | custom-call | flops 12230590464 | bytes 26214400 | tf_op jit(solution)/shard_map/middle/pallas_call | solution.py:340
  140.7 3.2 collective-permute-done.18
  143.8 2.9 collective-permute-start.19
  147.5 6.4 %collective-permute-start.15 = (bf16[432,768]{1,0:T(8,128)(2,1)}, bf16[432,768]{1,0:T(8,128)(2,1)}, u32[]{:S(2)}, u32[]{:S(2)}) collective-permute-start(bf16[432,768]{1,0:T(8,128)(2,1)} %get-tuple-element.40), channel_id=1, source_target_pairs={{2,4},{3,5},{4,2},{5,3},{10,12},{11,13},{12,10},{13,11},{18,20},{1... | collective-permute-start | bytes 1990664 | tf_op jit(solution)/shard_map/ppermute | solution.py:394
  154.8 33.7 %attend_back.1 = bf16[1728,576]{1,0:T(8,128)(2,1)} custom-call(bf16[3,128,1792]{2,1,0:T(8,128)(2,1)} %get-tuple-element.36.qa, bf16[3,1728,128]{2,1,0:T(8,128)(2,1)} %get-tuple-element.37.ka, bf16[3,1728,128]{2,1,0:T(8,128)(2,1)} %get-tuple-element.42.va, bf16[3,1792,64]{2,1,0:T(8,128)(2,1)} %get-tuple-element.43.qn, ...), custom_call_target="tpu_custom_call" | custom-call | flops 22932357120 | bytes 12582912 | tf_op jit(solution)/shard_map/attend_back/pallas_call | solution.py:223
  188.5 2.2 convert_reduce_fusion
  190.8 3.5 convolution_convert_fusion
  201.4 3.3 collective-permute-done.24
  207.8 2.5 collective-permute-done.25
  210.3 2.5 collective-permute-start.27
  213.0 2.4 collective-permute-done.27
  217.8 15.5 %collective-permute-done.28 = bf16[2,48,576]{1,2,0:T(8,128)(2,1)} collective-permute-done((bf16[2,48,576]{1,2,0:T(8,128)(2,1)}, bf16[2,48,576]{1,2,0:T(8,128)(2,1)}, u32[]{:S(2)}, u32[]{:S(2)}) %collective-permute-start.28) | collective-permute-done | bytes 110624 | tf_op jit(solution)/shard_map/ppermute | solution.py:381
  235.6 11.5 %collective-permute-done.29 = bf16[2,48,576]{1,2,0:T(8,128)(2,1)S(1)} collective-permute-done((bf16[2,48,576]{1,2,0:T(8,128)(2,1)S(1)}, bf16[2,48,576]{1,2,0:T(8,128)(2,1)S(1)}, u32[]{:S(2)}, u32[]{:S(2)}) %collective-permute-start.29) | collective-permute-done | bytes 110624 | tf_op jit(solution)/shard_map/ppermute | solution.py:381
  247.6 2.2 add_convert_fusion.4
  251.5 4.2 collective-permute-done.30
  257.2 2.0 collective-permute-start.33
  259.2 2.0 select_bitcast_fusion.5
  261.2 2.8 collective-permute-done.33
  264.0 3.2 collective-permute-start.36
  271.8 2.3 fusion.7
  274.1 2.3 fusion.31
  277.7 38.9 %psum.7 = f32[12,768]{1,0:T(8,128)S(1)} all-reduce(f32[12,768]{1,0:T(8,128)S(1)} %concatenate.193), channel_id=1, replica_groups=mesh['cube'=8,'blk'=4] {'cube','blk'}, use_global_device_ids=true, to_apply=%region_8.9 | all-reduce | flops 9216 | bytes 73728 | tf_op jit(solution)/shard_map/psum | solution.py:636
  317.7 4.5 collective-permute-start.23
  324.2 2.1 copy.90
  327.0 2.0 maximum_select_fusion.5
  329.0 2.3 add_convert_fusion.1
  331.4 2.0 collective-permute-start.52
  335.3 2.7 collective-permute-done.23
  338.0 2.4 select_bitcast_fusion
  340.5 5.7 %collective-permute-done.52 = bf16[384,768]{1,0:T(8,128)(2,1)S(1)} collective-permute-done((bf16[384,768]{1,0:T(8,128)(2,1)S(1)}, bf16[384,768]{1,0:T(8,128)(2,1)S(1)}, u32[]{:S(2)}, u32[]{:S(2)}) %collective-permute-start.52) | collective-permute-done | bytes 589856 | tf_op jit(solution)/shard_map/ppermute | solution.py:377
  350.0 2.7 add_convert_fusion
  352.7 2.8 collective-permute-done.53
  357.3 2.1 collective-permute-start.37
  359.6 4.0 collective-permute-done.56
  370.6 3.7 collective-permute-done.37
  379.2 4.3 collective-permute-done.38
  383.8 1.9 collective-permute-start.41
  386.7 8.1 %collective-permute-done.41 = bf16[2,120,768]{2,1,0:T(8,128)(2,1)S(1)} collective-permute-done((bf16[2,120,768]{2,1,0:T(8,128)(2,1)S(1)}, bf16[2,120,768]{2,1,0:T(8,128)(2,1)S(1)}, u32[]{:S(2)}, u32[]{:S(2)}) %collective-permute-start.41) | collective-permute-done | bytes 368672 | tf_op jit(solution)/shard_map/ppermute | solution.py:381
  396.0 2.9 collective-permute-start.61
  398.9 5.3 %collective-permute-done.42 = bf16[2,60,768]{2,1,0:T(8,128)(2,1)S(1)} collective-permute-done((bf16[2,60,768]{2,1,0:T(8,128)(2,1)S(1)}, bf16[2,60,768]{2,1,0:T(8,128)(2,1)S(1)}, u32[]{:S(2)}, u32[]{:S(2)}) %collective-permute-start.42) | collective-permute-done | bytes 184352 | tf_op jit(solution)/shard_map/ppermute | solution.py:381
  405.1 5.4 %collective-permute-start.62 = (bf16[192,768]{1,0:T(8,128)(2,1)S(1)}, bf16[192,768]{1,0:T(8,128)(2,1)S(1)}, u32[]{:S(2)}, u32[]{:S(2)}) collective-permute-start(bf16[192,768]{1,0:T(8,128)(2,1)S(1)} %get-tuple-element.180), channel_id=1, source_target_pairs={{0,8},{4,12},{8,0},{12,4},{16,24},{20,28},{24,16},{28,20},{1,9},{5... | collective-permute-start | bytes 884744 | tf_op jit(solution)/shard_map/ppermute | solution.py:377
  413.1 5.1 %collective-permute-done.62 = bf16[192,768]{1,0:T(8,128)(2,1)S(1)} collective-permute-done((bf16[192,768]{1,0:T(8,128)(2,1)S(1)}, bf16[192,768]{1,0:T(8,128)(2,1)S(1)}, u32[]{:S(2)}, u32[]{:S(2)}) %collective-permute-start.62) | collective-permute-done | bytes 294944 | tf_op jit(solution)/shard_map/ppermute | solution.py:377
  420.7 9.5 %collective-permute-start.47 = (bf16[240,768]{1,0:T(8,128)(2,1)S(1)}, bf16[240,768]{1,0:T(8,128)(2,1)S(1)}, u32[]{:S(2)}, u32[]{:S(2)}) collective-permute-start(bf16[240,768]{1,0:T(8,128)(2,1)S(1)} %get-tuple-element.178), channel_id=1, source_target_pairs={{0,8},{4,12},{8,0},{12,4},{16,24},{20,28},{24,16},{28,20},{1,9},{5... | collective-permute-start | bytes 1105928 | tf_op jit(solution)/shard_map/ppermute | solution.py:377
  432.3 3.1 collective-permute-start.65
  435.4 4.9 %collective-permute-done.45 = bf16[240,768]{1,0:T(8,128)(2,1)S(1)} collective-permute-done((bf16[240,768]{1,0:T(8,128)(2,1)S(1)}, bf16[240,768]{1,0:T(8,128)(2,1)S(1)}, u32[]{:S(2)}, u32[]{:S(2)}) %collective-permute-start.45) | collective-permute-done | bytes 368672 | tf_op jit(solution)/shard_map/ppermute | solution.py:377
  441.5 3.1 collective-permute-start.46
  446.8 6.1 %copy.92 = f32[768,2304]{1,0:T(8,128)} copy(bf16[768,2304]{0,1:T(8,128)(2,1)} %slice_dynamic-update-slice_fusion) | data formatting | bytes 10616832
  454.2 6.1 %collective-permute-done.46 = bf16[480,768]{1,0:T(8,128)(2,1)} collective-permute-done((bf16[480,768]{1,0:T(8,128)(2,1)}, bf16[480,768]{1,0:T(8,128)(2,1)}, u32[]{:S(2)}, u32[]{:S(2)}) %collective-permute-start.46) | collective-permute-done | bytes 737312 | tf_op jit(solution)/shard_map/ppermute | solution.py:377
  460.4 2.1 maximum_select_fusion
  462.5 2.0 collective-permute-start.49
  468.8 4.5 maximum_convert_fusion.1
  476.7 4.3 maximum_convert_fusion
  (294 shorter events, 104.7 us)
Async XLA Ops:
  0.6 25.1 %collective-permute-start = (bf16[432,768]{1,0:T(8,128)(2,1)}, bf16[432,768]{1,0:T(8,128)(2,1)}, u32[]{:S(2)}, u32[]{:S(2)}) collective-permute-start(bf16[432,768]{1,0:T(8,128)(2,1)} %bitcast.79), channel_id=1, source_target_pairs={{2,4},{3,5},{4,2},{5,3},{10,12},{11,13},{12,10},{13,11},{18,20},{1... | collective-permute-start | bytes 1990664 | tf_op jit(solution)/shard_map/ppermute | solution.py:394
  7.1 40.4 %collective-permute-start.6 = (bf16[1,432]{1,0:T(2,128)(2,1)S(1)}, bf16[1,432]{1,0:T(2,128)(2,1)S(1)}, u32[]{:S(2)}, u32[]{:S(2)}) collective-permute-start(bf16[1,432]{1,0:T(2,128)(2,1)S(1)} %convert_element_type.251), channel_id=1, source_target_pairs={{0,1},{1,0},{6,7},{7,6},{8,9},{9,8},{14,15},{15,14},{16,17},{17,16... | collective-permute-start | bytes 2600 | tf_op jit(solution)/shard_map/ppermute | solution.py:394
  7.7 37.8 %collective-permute-start.5 = (bf16[1,432]{1,0:T(2,128)(2,1)S(1)}, bf16[1,432]{1,0:T(2,128)(2,1)S(1)}, u32[]{:S(2)}, u32[]{:S(2)}) collective-permute-start(bf16[1,432]{1,0:T(2,128)(2,1)S(1)} %convert_element_type.251), channel_id=1, source_target_pairs={{2,4},{3,5},{4,2},{5,3},{10,12},{11,13},{12,10},{13,11},{18,20},{1... | collective-permute-start | bytes 2600 | tf_op jit(solution)/shard_map/ppermute | solution.py:394
  9.7 24.8 %collective-permute-start.1 = (bf16[432,768]{1,0:T(8,128)(2,1)}, bf16[432,768]{1,0:T(8,128)(2,1)}, u32[]{:S(2)}, u32[]{:S(2)}) collective-permute-start(bf16[432,768]{1,0:T(8,128)(2,1)} %bitcast.80), channel_id=1, source_target_pairs={{0,1},{1,0},{6,7},{7,6},{8,9},{9,8},{14,15},{15,14},{16,17},{17,16... | collective-permute-start | bytes 1990664 | tf_op jit(solution)/shard_map/ppermute | solution.py:394
  11.2 93.2 %collective-permute-start.14 = (bf16[432,768]{1,0:T(8,128)(2,1)}, bf16[432,768]{1,0:T(8,128)(2,1)}, u32[]{:S(2)}, u32[]{:S(2)}) collective-permute-start(bf16[432,768]{1,0:T(8,128)(2,1)} %bitcast.78), channel_id=1, source_target_pairs={{2,4},{3,5},{4,2},{5,3},{10,12},{11,13},{12,10},{13,11},{18,20},{1... | collective-permute-start | bytes 1990664 | tf_op jit(solution)/shard_map/ppermute | solution.py:394
  25.7 17.7 %collective-permute-start.2 = (bf16[432,768]{1,0:T(8,128)(2,1)}, bf16[432,768]{1,0:T(8,128)(2,1)}, u32[]{:S(2)}, u32[]{:S(2)}) collective-permute-start(bf16[432,768]{1,0:T(8,128)(2,1)} %collective-permute-done), channel_id=1, source_target_pairs={{2,3},{3,2},{4,5},{5,4},{10,11},{11,10},{12,13},{13,12},{18,19},{1... | collective-permute-start | bytes 1990664 | tf_op jit(solution)/shard_map/ppermute | solution.py:394
  34.5 20.8 %collective-permute-start.3 = (bf16[432,768]{1,0:T(8,128)(2,1)S(1)}, bf16[432,768]{1,0:T(8,128)(2,1)}, u32[]{:S(2)}, u32[]{:S(2)}) collective-permute-start(bf16[432,768]{1,0:T(8,128)(2,1)S(1)} %get-tuple-element.143.x0.x), channel_id=1, source_target_pairs={{0,4},{4,0},{8,12},{12,8},{16,20},{20,16},{24,28},{28,24},{1,5},{5... | collective-permute-start | bytes 1990664 | tf_op jit(solution)/shard_map/ppermute | solution.py:377
  44.6 10.7 %collective-permute-start.4 = (bf16[432,768]{1,0:T(8,128)(2,1)S(1)}, bf16[432,768]{1,0:T(8,128)(2,1)}, u32[]{:S(2)}, u32[]{:S(2)}) collective-permute-start(bf16[432,768]{1,0:T(8,128)(2,1)S(1)} %broadcast_select_fusion.9.x1), channel_id=1, source_target_pairs={{0,4},{4,0},{8,12},{12,8},{16,20},{20,16},{24,28},{28,24},{1,5},{5... | collective-permute-start | bytes 1990664 | tf_op jit(solution)/shard_map/ppermute | solution.py:377
  45.5 4.3 collective-permute-start.7
  47.5 6.5 %collective-permute-start.8 = (bf16[1,432]{1,0:T(2,128)(2,1)S(1)}, bf16[1,432]{1,0:T(2,128)(2,1)S(1)}, u32[]{:S(2)}, u32[]{:S(2)}) collective-permute-start(bf16[1,432]{1,0:T(2,128)(2,1)S(1)} %get-tuple-element.145), channel_id=1, source_target_pairs={{0,4},{4,0},{8,12},{12,8},{16,20},{20,16},{24,28},{28,24},{1,5},{5... | collective-permute-start | bytes 2600 | tf_op jit(solution)/shard_map/ppermute | solution.py:377
  96.6 7.2 %collective-permute-start.12 = (bf16[432,192]{1,0:T(8,128)(2,1)S(1)}, bf16[432,192]{1,0:T(8,128)(2,1)S(1)}, u32[]{:S(2)}, u32[]{:S(2)}) collective-permute-start(bf16[432,192]{1,0:T(8,128)(2,1)S(1)} %get-tuple-element.172), channel_id=1, source_target_pairs={{0,1},{1,0},{2,3},{3,2},{4,5},{5,4},{6,7},{7,6},{8,9},{9,8},{10,11... | collective-permute-start | bytes 497672 | tf_op jit(solution)/shard_map/ppermute | solution.py:381
  101.5 4.9 %collective-permute-start.11 = (bf16[432,192]{1,0:T(8,128)(2,1)S(1)}, bf16[432,192]{1,0:T(8,128)(2,1)S(1)}, u32[]{:S(2)}, u32[]{:S(2)}) collective-permute-start(bf16[432,192]{1,0:T(8,128)(2,1)S(1)} %get-tuple-element.173), channel_id=1, source_target_pairs={{0,4},{4,0},{8,12},{12,8},{16,20},{20,16},{24,28},{28,24},{1,5},{5... | collective-permute-start | bytes 497672 | tf_op jit(solution)/shard_map/ppermute | solution.py:377
  102.3 7.1 %collective-permute-start.10 = (bf16[432,192]{1,0:T(8,128)(2,1)S(1)}, bf16[432,192]{1,0:T(8,128)(2,1)S(1)}, u32[]{:S(2)}, u32[]{:S(2)}) collective-permute-start(bf16[432,192]{1,0:T(8,128)(2,1)S(1)} %get-tuple-element.174), channel_id=1, source_target_pairs={{0,1},{1,0},{2,3},{3,2},{4,5},{5,4},{6,7},{7,6},{8,9},{9,8},{10,11... | collective-permute-start | bytes 497672 | tf_op jit(solution)/shard_map/ppermute | solution.py:381
  103.7 5.6 %collective-permute-start.13 = (bf16[432,192]{1,0:T(8,128)(2,1)S(1)}, bf16[432,192]{1,0:T(8,128)(2,1)S(1)}, u32[]{:S(2)}, u32[]{:S(2)}) collective-permute-start(bf16[432,192]{1,0:T(8,128)(2,1)S(1)} %collective-permute-done.12), channel_id=1, source_target_pairs={{0,4},{4,0},{8,12},{12,8},{16,20},{20,16},{24,28},{28,24},{1,5},{5... | collective-permute-start | bytes 497672 | tf_op jit(solution)/shard_map/ppermute | solution.py:377
  137.4 6.4 %collective-permute-start.18 = (bf16[432,192]{1,0:T(8,128)(2,1)}, bf16[432,192]{1,0:T(8,128)(2,1)S(1)}, u32[]{:S(2)}, u32[]{:S(2)}) collective-permute-start(bf16[432,192]{1,0:T(8,128)(2,1)} %get-tuple-element.50), channel_id=1, source_target_pairs={{0,1},{1,0},{2,3},{3,2},{4,5},{5,4},{6,7},{7,6},{8,9},{9,8},{10,11... | collective-permute-start | bytes 497672 | tf_op jit(solution)/shard_map/ppermute | solution.py:381
  139.3 14.7 %collective-permute-start.16 = (bf16[432,192]{1,0:T(8,128)(2,1)}, bf16[432,192]{1,0:T(8,128)(2,1)S(1)}, u32[]{:S(2)}, u32[]{:S(2)}) collective-permute-start(bf16[432,192]{1,0:T(8,128)(2,1)} %get-tuple-element.48), channel_id=1, source_target_pairs={{0,1},{1,0},{2,3},{3,2},{4,5},{5,4},{6,7},{7,6},{8,9},{9,8},{10,11... | collective-permute-start | bytes 497672 | tf_op jit(solution)/shard_map/ppermute | solution.py:381
  139.3 14.7 %collective-permute-start.17 = (bf16[432,192]{1,0:T(8,128)(2,1)}, bf16[432,192]{1,0:T(8,128)(2,1)S(1)}, u32[]{:S(2)}, u32[]{:S(2)}) collective-permute-start(bf16[432,192]{1,0:T(8,128)(2,1)} %get-tuple-element.49), channel_id=1, source_target_pairs={{0,4},{4,0},{8,12},{12,8},{16,20},{20,16},{24,28},{28,24},{1,5},{5... | collective-permute-start | bytes 497672 | tf_op jit(solution)/shard_map/ppermute | solution.py:377
  143.8 10.2 %collective-permute-start.19 = (bf16[432,192]{1,0:T(8,128)(2,1)S(1)}, bf16[432,192]{1,0:T(8,128)(2,1)S(1)}, u32[]{:S(2)}, u32[]{:S(2)}) collective-permute-start(bf16[432,192]{1,0:T(8,128)(2,1)S(1)} %collective-permute-done.18), channel_id=1, source_target_pairs={{0,4},{4,0},{8,12},{12,8},{16,20},{20,16},{24,28},{28,24},{1,5},{5... | collective-permute-start | bytes 497672 | tf_op jit(solution)/shard_map/ppermute | solution.py:377
  147.5 109.7 %collective-permute-start.15 = (bf16[432,768]{1,0:T(8,128)(2,1)}, bf16[432,768]{1,0:T(8,128)(2,1)}, u32[]{:S(2)}, u32[]{:S(2)}) collective-permute-start(bf16[432,768]{1,0:T(8,128)(2,1)} %get-tuple-element.40), channel_id=1, source_target_pairs={{2,4},{3,5},{4,2},{5,3},{10,12},{11,13},{12,10},{13,11},{18,20},{1... | collective-permute-start | bytes 1990664 | tf_op jit(solution)/shard_map/ppermute | solution.py:394
  153.9 175.0 %collective-permute-start.51 = (bf16[1536,768]{1,0:T(8,128)(2,1)}, bf16[1536,768]{1,0:T(8,128)(2,1)}, u32[]{:S(2)}, u32[]{:S(2)}) collective-permute-start(bf16[1536,768]{1,0:T(8,128)(2,1)} %get-tuple-element.57), channel_id=1, source_target_pairs={{0,4},{4,0},{8,12},{12,8},{16,20},{20,16},{24,28},{28,24},{1,5},{5... | collective-permute-start | bytes 7077896 | tf_op jit(solution)/shard_map/ppermute | solution.py:377
  196.5 8.2 %collective-permute-start.24 = (bf16[192,576]{0,1:T(8,128)(2,1)S(1)}, bf16[192,576]{0,1:T(8,128)(2,1)S(1)}, u32[]{:S(2)}, u32[]{:S(2)}) collective-permute-start(bf16[192,576]{0,1:T(8,128)(2,1)S(1)} %constant_dynamic-slice_fusion.13), channel_id=1, source_target_pairs={{0,8},{4,12},{8,0},{12,4},{16,24},{20,28},{24,16},{28,20},{1,9},{5... | collective-permute-start | bytes 663560 | tf_op jit(solution)/shard_map/ppermute | solution.py:377
  197.9 8.3 %collective-permute-start.26 = (bf16[192,576]{0,1:T(8,128)(2,1)S(1)}, bf16[192,576]{0,1:T(8,128)(2,1)S(1)}, u32[]{:S(2)}, u32[]{:S(2)}) collective-permute-start(bf16[192,576]{0,1:T(8,128)(2,1)S(1)} %constant_dynamic-slice_fusion.11), channel_id=1, source_target_pairs={{0,16},{4,20},{8,24},{12,28},{16,0},{20,4},{24,8},{28,12},{1,17},{... | collective-permute-start | bytes 663560 | tf_op jit(solution)/shard_map/ppermute | solution.py:377
  200.4 71.3 %collective-permute-start.20 = (bf16[432,768]{1,0:T(8,128)(2,1)}, bf16[432,768]{1,0:T(8,128)(2,1)}, u32[]{:S(2)}, u32[]{:S(2)}) collective-permute-start(bf16[432,768]{1,0:T(8,128)(2,1)} %get-tuple-element.162), channel_id=1, source_target_pairs={{0,4},{4,0},{8,12},{12,8},{16,20},{20,16},{24,28},{28,24},{1,5},{5... | collective-permute-start | bytes 1990664 | tf_op jit(solution)/shard_map/ppermute | solution.py:377
  204.7 42.9 %collective-permute-start.21 = (bf16[432,768]{1,0:T(8,128)(2,1)}, bf16[432,768]{1,0:T(8,128)(2,1)}, u32[]{:S(2)}, u32[]{:S(2)}) collective-permute-start(bf16[432,768]{1,0:T(8,128)(2,1)} %get-tuple-element.163), channel_id=1, source_target_pairs={{0,4},{4,0},{8,12},{12,8},{16,20},{20,16},{24,28},{28,24},{1,5},{5... | collective-permute-start | bytes 1990664 | tf_op jit(solution)/shard_map/ppermute | solution.py:377
  210.3 5.1 %collective-permute-start.27 = (bf16[96,576]{0,1:T(8,128)(2,1)S(1)}, bf16[96,576]{0,1:T(8,128)(2,1)S(1)}, u32[]{:S(2)}, u32[]{:S(2)}) collective-permute-start(bf16[96,576]{0,1:T(8,128)(2,1)S(1)} %constant_dynamic-slice_fusion.10), channel_id=1, source_target_pairs={{0,8},{4,12},{8,0},{12,4},{16,24},{20,28},{24,16},{28,20},{1,9},{5... | collective-permute-start | bytes 331784 | tf_op jit(solution)/shard_map/ppermute | solution.py:377
  217.1 16.2 %collective-permute-start.28 = (bf16[2,48,576]{1,2,0:T(8,128)(2,1)}, bf16[2,48,576]{1,2,0:T(8,128)(2,1)}, u32[]{:S(2)}, u32[]{:S(2)}) collective-permute-start(bf16[2,48,576]{1,2,0:T(8,128)(2,1)} %fusion.14), channel_id=1, source_target_pairs={{0,2},{1,3},{2,0},{3,1},{4,6},{5,7},{6,4},{7,5},{8,10},{9,11},{10,... | collective-permute-start | bytes 331784 | tf_op jit(solution)/shard_map/ppermute | solution.py:381
  234.4 12.8 %collective-permute-start.29 = (bf16[2,48,576]{1,2,0:T(8,128)(2,1)S(1)}, bf16[2,48,576]{1,2,0:T(8,128)(2,1)S(1)}, u32[]{:S(2)}, u32[]{:S(2)}) collective-permute-start(bf16[2,48,576]{1,2,0:T(8,128)(2,1)S(1)} %add_convert_fusion.13), channel_id=1, source_target_pairs={{0,2},{1,3},{2,0},{3,1},{4,6},{5,7},{6,4},{7,5},{8,10},{9,11},{10,... | collective-permute-start | bytes 331784 | tf_op jit(solution)/shard_map/ppermute | solution.py:381
  247.5 8.2 %collective-permute-start.30 = (bf16[2,96,576]{1,2,0:T(8,128)(2,1)S(1)}, bf16[2,96,576]{1,2,0:T(8,128)(2,1)S(1)}, u32[]{:S(2)}, u32[]{:S(2)}) collective-permute-start(bf16[2,96,576]{1,2,0:T(8,128)(2,1)S(1)} %maximum_select_fusion.16), channel_id=1, source_target_pairs={{0,1},{1,0},{2,3},{3,2},{4,5},{5,4},{6,7},{7,6},{8,9},{9,8},{10,11... | collective-permute-start | bytes 663560 | tf_op jit(solution)/shard_map/ppermute | solution.py:381
  249.8 22.0 %collective-permute-start.22 = (bf16[432,768]{1,0:T(8,128)(2,1)}, bf16[432,768]{1,0:T(8,128)(2,1)S(1)}, u32[]{:S(2)}, u32[]{:S(2)}) collective-permute-start(bf16[432,768]{1,0:T(8,128)(2,1)} %add_convert_fusion.4), channel_id=1, source_target_pairs={{0,1},{1,0},{2,3},{3,2},{4,5},{5,4},{6,7},{7,6},{8,9},{9,8},{10,11... | collective-permute-start | bytes 1990664 | tf_op jit(solution)/shard_map/ppermute | solution.py:381
  255.8 12.9 %collective-permute-start.31 = (bf16[2,96,576]{1,2,0:T(8,128)(2,1)S(1)}, bf16[2,96,576]{1,2,0:T(8,128)(2,1)S(1)}, u32[]{:S(2)}, u32[]{:S(2)}) collective-permute-start(bf16[2,96,576]{1,2,0:T(8,128)(2,1)S(1)} %get-tuple-element.182), channel_id=1, source_target_pairs={{0,16},{4,20},{8,24},{12,28},{16,0},{20,4},{24,8},{28,12},{1,17},{... | collective-permute-start | bytes 663560 | tf_op jit(solution)/shard_map/ppermute | solution.py:377
  257.2 6.8 %collective-permute-start.33 = (bf16[2,96,576]{1,2,0:T(8,128)(2,1)S(1)}, bf16[2,96,576]{1,2,0:T(8,128)(2,1)S(1)}, u32[]{:S(2)}, u32[]{:S(2)}) collective-permute-start(bf16[2,96,576]{1,2,0:T(8,128)(2,1)S(1)} %get-tuple-element.183), channel_id=1, source_target_pairs={{0,8},{4,12},{8,0},{12,4},{16,24},{20,28},{24,16},{28,20},{1,9},{5... | collective-permute-start | bytes 663560 | tf_op jit(solution)/shard_map/ppermute | solution.py:377
  264.0 86.0 %collective-permute-start.36 = (bf16[1920,768]{1,0:T(8,128)(2,1)}, bf16[1920,768]{1,0:T(8,128)(2,1)}, u32[]{:S(2)}, u32[]{:S(2)}) collective-permute-start(bf16[1920,768]{1,0:T(8,128)(2,1)} %get-tuple-element.55), channel_id=1, source_target_pairs={{0,4},{4,0},{8,12},{12,8},{16,20},{20,16},{24,28},{28,24},{1,5},{5... | collective-permute-start | bytes 8847368 | tf_op jit(solution)/shard_map/ppermute | solution.py:377
  270.2 52.7 %collective-permute-start.32 = (bf16[2,192,576]{2,1,0:T(8,128)(2,1)}, bf16[2,192,576]{2,1,0:T(8,128)(2,1)}, u32[]{:S(2)}, u32[]{:S(2)}) collective-permute-start(bf16[2,192,576]{2,1,0:T(8,128)(2,1)} %copy.86), channel_id=1, source_target_pairs={{0,8},{4,12},{8,0},{12,4},{16,24},{20,28},{24,16},{28,20},{1,9},{5... | collective-permute-start | bytes 1327112 | tf_op jit(solution)/shard_map/ppermute | solution.py:377
  271.7 52.5 %collective-permute-start.34 = (bf16[2,192,576]{2,1,0:T(8,128)(2,1)}, bf16[2,192,576]{2,1,0:T(8,128)(2,1)}, u32[]{:S(2)}, u32[]{:S(2)}) collective-permute-start(bf16[2,192,576]{2,1,0:T(8,128)(2,1)} %copy.89), channel_id=1, source_target_pairs={{0,16},{4,20},{8,24},{12,28},{16,0},{20,4},{24,8},{28,12},{1,17},{... | collective-permute-start | bytes 1327112 | tf_op jit(solution)/shard_map/ppermute | solution.py:377
  317.7 20.3 %collective-permute-start.23 = (bf16[432,768]{1,0:T(8,128)(2,1)}, bf16[432,768]{1,0:T(8,128)(2,1)}, u32[]{:S(2)}, u32[]{:S(2)}) collective-permute-start(bf16[432,768]{1,0:T(8,128)(2,1)} %fusion.23), channel_id=1, source_target_pairs={{2,4},{3,5},{4,2},{5,3},{10,12},{11,13},{12,10},{13,11},{18,20},{1... | collective-permute-start | bytes 1990664 | tf_op jit(solution)/shard_map/ppermute | solution.py:394
  331.4 14.7 %collective-permute-start.52 = (bf16[384,768]{1,0:T(8,128)(2,1)S(1)}, bf16[384,768]{1,0:T(8,128)(2,1)S(1)}, u32[]{:S(2)}, u32[]{:S(2)}) collective-permute-start(bf16[384,768]{1,0:T(8,128)(2,1)S(1)} %constant_dynamic-slice_fusion.4), channel_id=1, source_target_pairs={{0,8},{4,12},{8,0},{12,4},{16,24},{20,28},{24,16},{28,20},{1,9},{5... | collective-permute-start | bytes 1769480 | tf_op jit(solution)/shard_map/ppermute | solution.py:377
  333.6 30.3 %collective-permute-start.35 = (bf16[2,768,576]{1,2,0:T(8,128)(2,1)S(1)}, bf16[2,768,576]{1,2,0:T(8,128)(2,1)S(1)}, u32[]{:S(2)}, u32[]{:S(2)}) collective-permute-start(bf16[2,768,576]{1,2,0:T(8,128)(2,1)S(1)} %pad_maximum_fusion.2), channel_id=1, source_target_pairs={{0,4},{4,0},{8,12},{12,8},{16,20},{20,16},{24,28},{28,24},{1,5},{5... | collective-permute-start | bytes 5308424 | tf_op jit(solution)/shard_map/ppermute | solution.py:377
  333.7 14.6 %collective-permute-start.54 = (bf16[384,768]{1,0:T(8,128)(2,1)S(1)}, bf16[384,768]{1,0:T(8,128)(2,1)S(1)}, u32[]{:S(2)}, u32[]{:S(2)}) collective-permute-start(bf16[384,768]{1,0:T(8,128)(2,1)S(1)} %constant_dynamic-slice_fusion.2), channel_id=1, source_target_pairs={{0,16},{4,20},{8,24},{12,28},{16,0},{20,4},{24,8},{28,12},{1,17},{... | collective-permute-start | bytes 1769480 | tf_op jit(solution)/shard_map/ppermute | solution.py:377
  346.3 9.2 %collective-permute-start.53 = (bf16[192,768]{1,0:T(8,128)(2,1)S(1)}, bf16[192,768]{1,0:T(8,128)(2,1)S(1)}, u32[]{:S(2)}, u32[]{:S(2)}) collective-permute-start(bf16[192,768]{1,0:T(8,128)(2,1)S(1)} %constant_dynamic-slice_fusion.3), channel_id=1, source_target_pairs={{0,16},{4,20},{8,24},{12,28},{16,0},{20,4},{24,8},{28,12},{1,17},{... | collective-permute-start | bytes 884744 | tf_op jit(solution)/shard_map/ppermute | solution.py:377
  348.6 7.9 %collective-permute-start.55 = (bf16[192,768]{1,0:T(8,128)(2,1)S(1)}, bf16[192,768]{1,0:T(8,128)(2,1)S(1)}, u32[]{:S(2)}, u32[]{:S(2)}) collective-permute-start(bf16[192,768]{1,0:T(8,128)(2,1)S(1)} %constant_dynamic-slice_fusion.1), channel_id=1, source_target_pairs={{0,8},{4,12},{8,0},{12,4},{16,24},{20,28},{24,16},{28,20},{1,9},{5... | collective-permute-start | bytes 884744 | tf_op jit(solution)/shard_map/ppermute | solution.py:377
  356.6 7.0 %collective-permute-start.56 = (bf16[2,96,768]{2,1,0:T(8,128)(2,1)S(1)}, bf16[2,96,768]{2,1,0:T(8,128)(2,1)S(1)}, u32[]{:S(2)}, u32[]{:S(2)}) collective-permute-start(bf16[2,96,768]{2,1,0:T(8,128)(2,1)S(1)} %fusion.20), channel_id=1, source_target_pairs={{0,1},{1,0},{2,3},{3,2},{4,5},{5,4},{6,7},{7,6},{8,9},{9,8},{10,11... | collective-permute-start | bytes 884744 | tf_op jit(solution)/shard_map/ppermute | solution.py:381
  357.3 17.0 %collective-permute-start.37 = (bf16[480,768]{1,0:T(8,128)(2,1)S(1)}, bf16[480,768]{1,0:T(8,128)(2,1)S(1)}, u32[]{:S(2)}, u32[]{:S(2)}) collective-permute-start(bf16[480,768]{1,0:T(8,128)(2,1)S(1)} %constant_dynamic-slice_fusion.9), channel_id=1, source_target_pairs={{0,8},{4,12},{8,0},{12,4},{16,24},{20,28},{24,16},{28,20},{1,9},{5... | collective-permute-start | bytes 2211848 | tf_op jit(solution)/shard_map/ppermute | solution.py:377
  359.4 16.7 %collective-permute-start.39 = (bf16[480,768]{1,0:T(8,128)(2,1)S(1)}, bf16[480,768]{1,0:T(8,128)(2,1)S(1)}, u32[]{:S(2)}, u32[]{:S(2)}) collective-permute-start(bf16[480,768]{1,0:T(8,128)(2,1)S(1)} %constant_dynamic-slice_fusion.7), channel_id=1, source_target_pairs={{0,16},{4,20},{8,24},{12,28},{16,0},{20,4},{24,8},{28,12},{1,17},{... | collective-permute-start | bytes 2211848 | tf_op jit(solution)/shard_map/ppermute | solution.py:377
  363.7 6.3 %collective-permute-start.57 = (bf16[2,48,768]{2,1,0:T(8,128)(2,1)S(1)}, bf16[2,48,768]{2,1,0:T(8,128)(2,1)S(1)}, u32[]{:S(2)}, u32[]{:S(2)}) collective-permute-start(bf16[2,48,768]{2,1,0:T(8,128)(2,1)S(1)} %constant_dynamic-slice_fusion), channel_id=1, source_target_pairs={{0,2},{1,3},{2,0},{3,1},{4,6},{5,7},{6,4},{7,5},{8,10},{9,11},{10,... | collective-permute-start | bytes 442376 | tf_op jit(solution)/shard_map/ppermute | solution.py:381
  370.0 8.2 %collective-permute-start.58 = (bf16[2,48,768]{2,1,0:T(8,128)(2,1)S(1)}, bf16[2,48,768]{2,1,0:T(8,128)(2,1)S(1)}, u32[]{:S(2)}, u32[]{:S(2)}) collective-permute-start(bf16[2,48,768]{2,1,0:T(8,128)(2,1)S(1)} %add_convert_fusion.17), channel_id=1, source_target_pairs={{0,2},{1,3},{2,0},{3,1},{4,6},{5,7},{6,4},{7,5},{8,10},{9,11},{10,... | collective-permute-start | bytes 442376 | tf_op jit(solution)/shard_map/ppermute | solution.py:381
  374.5 9.0 %collective-permute-start.38 = (bf16[240,768]{1,0:T(8,128)(2,1)S(1)}, bf16[240,768]{1,0:T(8,128)(2,1)S(1)}, u32[]{:S(2)}, u32[]{:S(2)}) collective-permute-start(bf16[240,768]{1,0:T(8,128)(2,1)S(1)} %constant_dynamic-slice_fusion.8), channel_id=1, source_target_pairs={{0,16},{4,20},{8,24},{12,28},{16,0},{20,4},{24,8},{28,12},{1,17},{... | collective-permute-start | bytes 1105928 | tf_op jit(solution)/shard_map/ppermute | solution.py:377
  376.3 7.3 %collective-permute-start.40 = (bf16[240,768]{1,0:T(8,128)(2,1)S(1)}, bf16[240,768]{1,0:T(8,128)(2,1)S(1)}, u32[]{:S(2)}, u32[]{:S(2)}) collective-permute-start(bf16[240,768]{1,0:T(8,128)(2,1)S(1)} %constant_dynamic-slice_fusion.6), channel_id=1, source_target_pairs={{0,8},{4,12},{8,0},{12,4},{16,24},{20,28},{24,16},{28,20},{1,9},{5... | collective-permute-start | bytes 1105928 | tf_op jit(solution)/shard_map/ppermute | solution.py:377
  378.3 7.4 %collective-permute-start.59 = (bf16[2,96,768]{2,1,0:T(8,128)(2,1)S(1)}, bf16[2,96,768]{2,1,0:T(8,128)(2,1)S(1)}, u32[]{:S(2)}, u32[]{:S(2)}) collective-permute-start(bf16[2,96,768]{2,1,0:T(8,128)(2,1)S(1)} %maximum_select_fusion.17), channel_id=1, source_target_pairs={{0,1},{1,0},{2,3},{3,2},{4,5},{5,4},{6,7},{7,6},{8,9},{9,8},{10,11... | collective-permute-start | bytes 884744 | tf_op jit(solution)/shard_map/ppermute | solution.py:381
  383.8 11.0 %collective-permute-start.41 = (bf16[2,120,768]{2,1,0:T(8,128)(2,1)S(1)}, bf16[2,120,768]{2,1,0:T(8,128)(2,1)S(1)}, u32[]{:S(2)}, u32[]{:S(2)}) collective-permute-start(bf16[2,120,768]{2,1,0:T(8,128)(2,1)S(1)} %fusion.12), channel_id=1, source_target_pairs={{0,1},{1,0},{2,3},{3,2},{4,5},{5,4},{6,7},{7,6},{8,9},{9,8},{10,11... | collective-permute-start | bytes 1105928 | tf_op jit(solution)/shard_map/ppermute | solution.py:381
  386.0 9.9 %collective-permute-start.60 = (bf16[192,768]{1,0:T(8,128)(2,1)S(1)}, bf16[192,768]{1,0:T(8,128)(2,1)S(1)}, u32[]{:S(2)}, u32[]{:S(2)}) collective-permute-start(bf16[192,768]{1,0:T(8,128)(2,1)S(1)} %get-tuple-element.181), channel_id=1, source_target_pairs={{0,16},{4,20},{8,24},{12,28},{16,0},{20,4},{24,8},{28,12},{1,17},{... | collective-permute-start | bytes 884744 | tf_op jit(solution)/shard_map/ppermute | solution.py:377
  395.0 9.2 %collective-permute-start.42 = (bf16[2,60,768]{2,1,0:T(8,128)(2,1)S(1)}, bf16[2,60,768]{2,1,0:T(8,128)(2,1)S(1)}, u32[]{:S(2)}, u32[]{:S(2)}) collective-permute-start(bf16[2,60,768]{2,1,0:T(8,128)(2,1)S(1)} %constant_dynamic-slice_fusion.5), channel_id=1, source_target_pairs={{0,2},{1,3},{2,0},{3,1},{4,6},{5,7},{6,4},{7,5},{8,10},{9,11},{10,... | collective-permute-start | bytes 552968 | tf_op jit(solution)/shard_map/ppermute | solution.py:381
  396.0 22.4 %collective-permute-start.61 = (bf16[384,768]{1,0:T(8,128)(2,1)S(1)}, bf16[384,768]{1,0:T(8,128)(2,1)S(1)}, u32[]{:S(2)}, u32[]{:S(2)}) collective-permute-start(bf16[384,768]{1,0:T(8,128)(2,1)S(1)} %maximum_select_fusion.12), channel_id=1, source_target_pairs={{0,8},{4,12},{8,0},{12,4},{16,24},{20,28},{24,16},{28,20},{1,9},{5... | collective-permute-start | bytes 1769480 | tf_op jit(solution)/shard_map/ppermute | solution.py:377
  404.3 7.8 %collective-permute-start.43 = (bf16[2,60,768]{2,1,0:T(8,128)(2,1)S(1)}, bf16[2,60,768]{2,1,0:T(8,128)(2,1)S(1)}, u32[]{:S(2)}, u32[]{:S(2)}) collective-permute-start(bf16[2,60,768]{2,1,0:T(8,128)(2,1)S(1)} %add_convert_fusion.16), channel_id=1, source_target_pairs={{0,2},{1,3},{2,0},{3,1},{4,6},{5,7},{6,4},{7,5},{8,10},{9,11},{10,... | collective-permute-start | bytes 552968 | tf_op jit(solution)/shard_map/ppermute | solution.py:381
  405.1 13.0 %collective-permute-start.62 = (bf16[192,768]{1,0:T(8,128)(2,1)S(1)}, bf16[192,768]{1,0:T(8,128)(2,1)S(1)}, u32[]{:S(2)}, u32[]{:S(2)}) collective-permute-start(bf16[192,768]{1,0:T(8,128)(2,1)S(1)} %get-tuple-element.180), channel_id=1, source_target_pairs={{0,8},{4,12},{8,0},{12,4},{16,24},{20,28},{24,16},{28,20},{1,9},{5... | collective-permute-start | bytes 884744 | tf_op jit(solution)/shard_map/ppermute | solution.py:377
  412.2 8.1 %collective-permute-start.44 = (bf16[2,120,768]{2,1,0:T(8,128)(2,1)S(1)}, bf16[2,120,768]{2,1,0:T(8,128)(2,1)S(1)}, u32[]{:S(2)}, u32[]{:S(2)}) collective-permute-start(bf16[2,120,768]{2,1,0:T(8,128)(2,1)S(1)} %maximum_select_fusion.14), channel_id=1, source_target_pairs={{0,1},{1,0},{2,3},{3,2},{4,5},{5,4},{6,7},{7,6},{8,9},{9,8},{10,11... | collective-permute-start | bytes 1105928 | tf_op jit(solution)/shard_map/ppermute | solution.py:381
  418.3 13.5 %collective-permute-start.63 = (bf16[384,768]{1,0:T(8,128)(2,1)S(1)}, bf16[384,768]{1,0:T(8,128)(2,1)S(1)}, u32[]{:S(2)}, u32[]{:S(2)}) collective-permute-start(bf16[384,768]{1,0:T(8,128)(2,1)S(1)} %maximum_select_fusion.13), channel_id=1, source_target_pairs={{0,16},{4,20},{8,24},{12,28},{16,0},{20,4},{24,8},{28,12},{1,17},{... | collective-permute-start | bytes 1769480 | tf_op jit(solution)/shard_map/ppermute | solution.py:377
  418.9 34.0 %collective-permute-start.64 = (bf16[768,768]{1,0:T(8,128)(2,1)S(1)}, bf16[768,768]{1,0:T(8,128)(2,1)}, u32[]{:S(2)}, u32[]{:S(2)}) collective-permute-start(bf16[768,768]{1,0:T(8,128)(2,1)S(1)} %maximum_select_fusion.2), channel_id=1, source_target_pairs={{0,4},{4,0},{8,12},{12,8},{16,20},{20,16},{24,28},{28,24},{1,5},{5... | collective-permute-start | bytes 3538952 | tf_op jit(solution)/shard_map/ppermute | solution.py:377
  420.7 23.9 %collective-permute-start.47 = (bf16[240,768]{1,0:T(8,128)(2,1)S(1)}, bf16[240,768]{1,0:T(8,128)(2,1)S(1)}, u32[]{:S(2)}, u32[]{:S(2)}) collective-permute-start(bf16[240,768]{1,0:T(8,128)(2,1)S(1)} %get-tuple-element.178), channel_id=1, source_target_pairs={{0,8},{4,12},{8,0},{12,4},{16,24},{20,28},{24,16},{28,20},{1,9},{5... | collective-permute-start | bytes 1105928 | tf_op jit(solution)/shard_map/ppermute | solution.py:377
  430.2 10.1 %collective-permute-start.45 = (bf16[240,768]{1,0:T(8,128)(2,1)S(1)}, bf16[240,768]{1,0:T(8,128)(2,1)S(1)}, u32[]{:S(2)}, u32[]{:S(2)}) collective-permute-start(bf16[240,768]{1,0:T(8,128)(2,1)S(1)} %get-tuple-element.179), channel_id=1, source_target_pairs={{0,16},{4,20},{8,24},{12,28},{16,0},{20,4},{24,8},{28,12},{1,17},{... | collective-permute-start | bytes 1105928 | tf_op jit(solution)/shard_map/ppermute | solution.py:377
  432.3 34.2 %collective-permute-start.65 = (bf16[768,768]{1,0:T(8,128)(2,1)S(1)}, bf16[768,768]{1,0:T(8,128)(2,1)}, u32[]{:S(2)}, u32[]{:S(2)}) collective-permute-start(bf16[768,768]{1,0:T(8,128)(2,1)S(1)} %maximum_select_fusion.3), channel_id=1, source_target_pairs={{0,4},{4,0},{8,12},{12,8},{16,20},{20,16},{24,28},{28,24},{1,5},{5... | collective-permute-start | bytes 3538952 | tf_op jit(solution)/shard_map/ppermute | solution.py:377
  441.5 18.9 %collective-permute-start.46 = (bf16[480,768]{1,0:T(8,128)(2,1)}, bf16[480,768]{1,0:T(8,128)(2,1)}, u32[]{:S(2)}, u32[]{:S(2)}) collective-permute-start(bf16[480,768]{1,0:T(8,128)(2,1)} %maximum_select_fusion.7), channel_id=1, source_target_pairs={{0,8},{4,12},{8,0},{12,4},{16,24},{20,28},{24,16},{28,20},{1,9},{5... | collective-permute-start | bytes 2211848 | tf_op jit(solution)/shard_map/ppermute | solution.py:377
  444.9 19.7 %collective-permute-start.48 = (bf16[480,768]{1,0:T(8,128)(2,1)S(1)}, bf16[480,768]{1,0:T(8,128)(2,1)}, u32[]{:S(2)}, u32[]{:S(2)}) collective-permute-start(bf16[480,768]{1,0:T(8,128)(2,1)S(1)} %maximum_select_fusion.8), channel_id=1, source_target_pairs={{0,16},{4,20},{8,24},{12,28},{16,0},{20,4},{24,8},{28,12},{1,17},{... | collective-permute-start | bytes 2211848 | tf_op jit(solution)/shard_map/ppermute | solution.py:377
  462.5 10.8 %collective-permute-start.49 = (bf16[960,768]{1,0:T(8,128)(2,1)S(1)}, bf16[960,768]{1,0:T(8,128)(2,1)S(1)}, u32[]{:S(2)}, u32[]{:S(2)}) collective-permute-start(bf16[960,768]{1,0:T(8,128)(2,1)S(1)} %maximum_select_fusion), channel_id=1, source_target_pairs={{0,4},{4,0},{8,12},{12,8},{16,20},{20,16},{24,28},{28,24},{1,5},{5... | collective-permute-start | bytes 4423688 | tf_op jit(solution)/shard_map/ppermute | solution.py:377
  466.4 6.9 %collective-permute-start.50 = (bf16[960,768]{1,0:T(8,128)(2,1)S(1)}, bf16[960,768]{1,0:T(8,128)(2,1)S(1)}, u32[]{:S(2)}, u32[]{:S(2)}) collective-permute-start(bf16[960,768]{1,0:T(8,128)(2,1)S(1)} %maximum_select_fusion.1), channel_id=1, source_target_pairs={{0,4},{4,0},{8,12},{12,8},{16,20},{20,16},{24,28},{28,24},{1,5},{5... | collective-permute-start | bytes 4423688 | tf_op jit(solution)/shard_map/ppermute | solution.py:377
  (35 other events, 276.9 us)

commit v3 on v2

v3 whole, which is shorter than its diff:
```python
import functools
import jax
import jax.numpy as jnp
from jax import lax
from jax.experimental import pallas as pl
from jax.experimental.pallas import tpu as pltpu
from jax.sharding import PartitionSpec as P

HEADS = 12
HD = 64
GROUPS = 12
MEMBERS = 4
LOCAL_HEADS = HEADS // MEMBERS
WIDTH = LOCAL_HEADS * HD
NEG_FILL = -32768.0
EPSILON = 1e-06
BF16 = jnp.bfloat16
F32 = jnp.float32
TILE = 256
LANES = 128
VMEM = pltpu.VMEM
QUICK = pl.CostEstimate(flops=1, bytes_accessed=1, transcendentals=0)


def dot(left, right):
    return jnp.dot(left, right, preferred_element_type=F32)


def dot_nt(left, right):
    return lax.dot_general(left, right, (((1,), (1,)), ((), ())), preferred_element_type=F32)


def dot_tn(left, right):
    return lax.dot_general(left, right, (((0,), (0,)), ((), ())), preferred_element_type=F32)


def params(limit=60 << 20, **more):
    return pltpu.CompilerParams(vmem_limit_bytes=limit, **more)


def whole(*shape):
    return pl.BlockSpec(shape, lambda *_: (0,) * len(shape))


def normalized(values):
    centered = values - jnp.mean(values, axis=-1, keepdims=True)
    inverse = lax.rsqrt(jnp.mean(centered * centered, axis=-1, keepdims=True) + EPSILON)
    return centered * inverse, inverse


def mask_column(x, rows):
    return x[rows:, :rows].astype(F32).T[:, :1]


def project_kernel(x0, x1, x2, x3, gain, shift, w, wt, bias, bias_col, normed, qa, ka, va, qn, kt, vt):
    rows = normed.shape[0] // MEMBERS
    total = MEMBERS * rows
    padded = qa.shape[2]
    step = rows // 3
    for d, x in enumerate((x0, x1, x2, x3)):

        def some(i, carry, d=d, x=x):
            here = x[pl.ds(i * step, step), :].astype(F32)
            unit, _ = normalized(here)
            normed[pl.ds(d * rows + i * step, step), :] = (unit * gain[...][None] + shift[...][None]).astype(BF16)
            return carry

        lax.fori_loop(0, 3, some, 0)
    for d, x in enumerate((x0, x1, x2, x3)):
        here = pl.ds(d * rows, rows)
        natural = dot(normed[here, :], w[...]) + bias[...][None]
        lane = lax.broadcasted_iota(jnp.int32, (rows, HD), 1)
        low_mask = NEG_FILL * (1.0 - mask_column(x, rows))
        key_tail = jnp.where(lane == 0, low_mask, jnp.where(lane < 4, 1.0, 0.0)).astype(BF16)
        value_tail = jnp.where(lane < 3, 1.0, 0.0).astype(BF16)
        for h in range(LOCAL_HEADS):
            at = h * HD
            qn[h, here, :] = (natural[:, at : at + HD] * HD ** (-0.5)).astype(BF16)
            ka[h, here, :HD] = natural[:, WIDTH + at : WIDTH + at + HD].astype(BF16)
            ka[h, here, HD:] = key_tail
            va[h, here, :HD] = natural[:, 2 * WIDTH + at : 2 * WIDTH + at + HD].astype(BF16)
            va[h, here, HD:] = value_tail
    turned = dot_nt(wt[...], normed[...]) + bias_col[...]
    row = lax.broadcasted_iota(jnp.int32, (HD, padded), 0)
    query_tail = jnp.where(row == 0, 1.0, 0.0).astype(BF16)
    for h in range(LOCAL_HEADS):
        at = h * HD
        qn[h, total:, :] = jnp.zeros((padded - total, HD), BF16)
        qa[h, :HD, :total] = (turned[at : at + HD] * HD ** (-0.5)).astype(BF16)
        qa[h, :HD, total:] = jnp.zeros((HD, padded - total), BF16)
        qa[h, HD:, :] = query_tail
        kt[h] = turned[WIDTH + at : WIDTH + at + HD].astype(BF16)
        vt[h] = turned[2 * WIDTH + at : 2 * WIDTH + at + HD].astype(BF16)


def project(x_blocks, rows, gain, shift, w, wt, bias, bias_col):
    model = x_blocks[0].shape[1]
    total = MEMBERS * rows
    padded = -(-total // TILE) * TILE
    n = LOCAL_HEADS
    outs = [
        jax.ShapeDtypeStruct((total, model), BF16),
        jax.ShapeDtypeStruct((n, 2 * HD, padded), BF16),
        jax.ShapeDtypeStruct((n, total, 2 * HD), BF16),
        jax.ShapeDtypeStruct((n, total, 2 * HD), BF16),
        jax.ShapeDtypeStruct((n, padded, HD), BF16),
        jax.ShapeDtypeStruct((n, HD, total), BF16),
        jax.ShapeDtypeStruct((n, HD, total), BF16),
    ]
    flops = 4 * total * model * 3 * WIDTH
    return pl.pallas_call(
        project_kernel,
        out_shape=outs,
        in_specs=[pl.BlockSpec(memory_space=VMEM)] * 10,
        out_specs=[pl.BlockSpec(memory_space=VMEM)] * len(outs),
        compiler_params=params(),
        cost_estimate=QUICK,
        name="project",
    )(*x_blocks, gain, shift, w, wt, bias, bias_col)


def forward_kernel(qa, ka, vt, l0, l1, l2, l3, turned, logs, held, even, odd):
    head = pl.program_id(0)
    rows = l0.shape[0]
    tiles = qa.shape[2] // TILE

    def scored(i, out):
        here = pl.ds(pl.multiple_of(i * TILE, TILE), TILE)
        out[...] = dot(ka[0], qa[0, :, here])

    def mixed_of(i, scores):
        here = pl.ds(pl.multiple_of(i * TILE, TILE), TILE)
        peak = jnp.max(scores[...], axis=0, keepdims=True)
        weights = jnp.exp(scores[...] - peak)
        sums = jnp.sum(weights, axis=0, keepdims=True)
        mixed = dot(vt[0], weights.astype(BF16)) * (1.0 / sums)
        turned[0, :, here] = mixed
        logs[0, :, here] = peak + jnp.log(sums)
        held[here, :] = mixed.T.astype(BF16)

    scored(0, even)

    def pair(i, carry):
        scored(2 * i + 1, odd)
        mixed_of(2 * i, even)
        scored(jnp.minimum(2 * i + 2, tiles - 1), even)
        mixed_of(2 * i + 1, odd)
        return carry

    lax.fori_loop(0, tiles // 2, pair, 0)
    if tiles % 2:
        mixed_of(tiles - 1, even)
    for h in range(LOCAL_HEADS):

        @pl.when(head == h)
        def _(h=h):
            for d, low in enumerate((l0, l1, l2, l3)):
                low[:, h * HD : (h + 1) * HD] = held[d * rows : (d + 1) * rows, :]


def attend(qa, ka, vt):
    n, total, _ = ka.shape
    padded = qa.shape[2]
    rows = total // MEMBERS
    per_head = lambda *shape: pl.BlockSpec((1,) + shape, lambda h: (h, 0, 0))
    *low, turned, logs = pl.pallas_call(
        forward_kernel,
        grid=(n,),
        out_shape=[jax.ShapeDtypeStruct((rows, WIDTH), BF16)] * MEMBERS
        + [
            jax.ShapeDtypeStruct((n, HD, padded), F32),
            jax.ShapeDtypeStruct((n, 1, padded), F32),
        ],
        in_specs=[per_head(2 * HD, padded), per_head(total, 2 * HD), per_head(HD, total)],
        out_specs=[whole(rows, WIDTH)] * MEMBERS + [per_head(HD, padded), per_head(1, padded)],
        scratch_shapes=[VMEM((padded, HD), BF16), VMEM((total, TILE), F32), VMEM((total, TILE), F32)],
        compiler_params=params(),
        cost_estimate=QUICK,
        name="attend",
    )(qa, ka, vt)
    return low, turned, logs


def three_parts(row):
    high = row.astype(BF16).astype(F32)
    rest = row - high
    middle = rest.astype(BF16).astype(F32)
    return high, middle, rest - middle


def backward_kernel(head, qa, ka, va, qn, kt, turned, logs, g0, g1, g2, g3, out_q, out_k, out_v, held_g, sum_k, sum_v):
    rows = g0.shape[0]
    total = ka.shape[1]
    padded = qa.shape[2]
    tiles = padded // TILE
    for d, part in enumerate((g0, g1, g2, g3)):
        held_g[d * rows : (d + 1) * rows, :] = part[:, head * HD : (head + 1) * HD]
    held_g[total:, :] = jnp.zeros((padded - total, HD), BF16)
    sum_k[...] = jnp.zeros_like(sum_k)
    sum_v[...] = jnp.zeros_like(sum_v)
    row = lax.broadcasted_iota(jnp.int32, (HD, TILE), 0)

    def some(i, width):
        here = pl.ds(pl.multiple_of(i * TILE, TILE), TILE)
        grad = held_g[here, :]
        grad_turned = grad.astype(F32).T
        delta = jnp.sum(grad_turned * turned[0, :, here], axis=0, keepdims=True)
        high, middle, least = three_parts(-logs[0, :, here])
        tail = jnp.where(row == 0, 1.0, jnp.where(row == 1, high, jnp.where(row == 2, middle, jnp.where(row == 3, least, 0.0))))
        query = jnp.concatenate([qa[0, :HD, here], tail.astype(BF16)], axis=0)
        probs = jnp.exp(dot(ka[0], query))
        high, middle, least = three_parts(-delta)
        tail = jnp.where(row == 0, high, jnp.where(row == 1, middle, jnp.where(row == 2, least, 0.0)))
        grad_tail = jnp.concatenate([grad_turned, tail], axis=0).astype(BF16)
        grad_scores = (probs * dot(va[0], grad_tail)).astype(BF16)
        sum_v[...] += dot(probs.astype(BF16), grad)
        sum_k[...] += dot(grad_scores, qn[0, here, :])
        query_grad = dot(kt[0], grad_scores) * HD ** (-0.5)
        out_q[pl.ds(pl.multiple_of(i * TILE, TILE), width), :] = query_grad.T.astype(BF16)[:width]

    def full(i, carry):
        some(i, TILE)
        return carry

    lax.fori_loop(0, tiles - 1, full, 0)
    some(tiles - 1, total - (tiles - 1) * TILE)
    out_k[...] = sum_k[...].astype(BF16)
    out_v[...] = sum_v[...].astype(BF16)


def attend_back(head, qa, ka, va, qn, kt, turned, logs, grads):
    n, total, _ = ka.shape
    padded = qa.shape[2]
    rows = grads[0].shape[0]
    per_head = lambda *shape: pl.BlockSpec((1,) + shape, lambda i: (head, 0, 0))
    return pl.pallas_call(
        functools.partial(backward_kernel, head),
        grid=(1,),
        out_shape=[jax.ShapeDtypeStruct((total, HD), BF16)] * 3,
        in_specs=[
            per_head(2 * HD, padded),
            per_head(total, 2 * HD),
            per_head(total, 2 * HD),
            per_head(padded, HD),
            per_head(HD, total),
            per_head(HD, padded),
            per_head(1, padded),
        ]
        + [whole(rows, WIDTH)] * MEMBERS,
        out_specs=[whole(total, HD)] * 3,
        scratch_shapes=[
            VMEM((padded, HD), BF16),
            VMEM((total, HD), F32),
            VMEM((total, HD), F32),
        ],
        compiler_params=params(),
        cost_estimate=QUICK,
        name="attend_back",
    )(qa, ka, va, qn, kt, turned, logs, *grads)


def unproject_kernel(*refs):
    columns, normed, w = refs[:9], refs[9], refs[10]
    n0, n1, n2, n3, first, second, sums, joint = refs[11:]
    rows = n0.shape[0]
    for s in range(3):
        for h in range(LOCAL_HEADS):
            at = s * WIDTH + h * HD
            joint[:, at : at + HD] = columns[3 * h + s][...]
    for d, out in enumerate((n0, n1, n2, n3)):
        out[...] = dot_nt(joint[d * rows : (d + 1) * rows, :], w[...]).astype(BF16)
    grad = dot_tn(normed[...], joint[...]).astype(BF16)
    pieces, each, _ = first.shape
    for i in range(pieces):
        first[i] = grad[2 * i * each : (2 * i + 1) * each]
        second[i] = grad[(2 * i + 1) * each : (2 * i + 2) * each]
    sums[...] = jnp.sum(joint[...].astype(F32), axis=0, keepdims=True)


def unproject(columns, normed, w, pieces):
    total, model = normed.shape
    rows = total // MEMBERS
    width = 3 * WIDTH
    shaped = jax.ShapeDtypeStruct
    outs = [shaped((rows, model), BF16)] * MEMBERS
    outs += [shaped((pieces, model // pieces // 2, width), BF16)] * 2 + [shaped((1, width), F32)]
    return pl.pallas_call(
        unproject_kernel,
        out_shape=outs,
        in_specs=[pl.BlockSpec(memory_space=VMEM)] * 11,
        out_specs=[pl.BlockSpec(memory_space=VMEM)] * len(outs),
        scratch_shapes=[VMEM((total, width), BF16)],
        compiler_params=params(),
        cost_estimate=QUICK,
        name="unproject",
    )(*columns, normed, w)


def close_kernel(x, p0, p1, gain, hidden, grad, low, vectors):
    rows = hidden.shape[0]
    unit, inverse = normalized(x[:rows, :].astype(F32))
    given = p0[...].astype(F32) + p1[...].astype(F32)
    vectors[0:1, :] = jnp.sum(given * unit, axis=0, keepdims=True)
    vectors[1:2, :] = jnp.sum(given, axis=0, keepdims=True)
    scaled = given * gain[...][None]
    inner = scaled - jnp.mean(scaled, axis=-1, keepdims=True)
    inner = inner - unit * jnp.mean(scaled * unit, axis=-1, keepdims=True)
    total = hidden[...] + inverse * inner
    grad[...] = total
    low[...] = total.astype(BF16)


def close(x, parts, gain, hidden):
    rows, model = hidden.shape
    shaped = jax.ShapeDtypeStruct
    return pl.pallas_call(
        close_kernel,
        out_shape=[shaped((rows, model), F32), shaped((rows, model), BF16), shaped((2, model), F32)],
        in_specs=[pl.BlockSpec(memory_space=VMEM)] * 5,
        out_specs=[pl.BlockSpec(memory_space=VMEM)] * 3,
        compiler_params=params(),
        cost_estimate=QUICK,
        name="close",
    )(x, *parts, gain, hidden)


def middle_kernel(
    side, x, a0, a1, a2, a3, wo, out_bias, gain, shift, cot, down_bias, up, up_bias, down,
    layer, down_send, down_keep, rest_send, rest_keep, grad_up_bias, grad_hidden, g0, g1, g2, g3, vectors,
    hidden, normed, grad_down, total_out, total_grad, valid,
):
    step = pl.program_id(0)
    last = pl.num_programs(0) - 1
    half = pl.num_programs(0) // 2
    rows, model = cot.shape
    pieces = down_keep.shape[0]
    each = half * model // pieces
    share = model // each

    @pl.when(step == 0)
    def _():
        valid[...] = mask_column(x, rows)
        value = x[:rows, :].astype(F32) + out_bias[...][None]
        for e, part in enumerate((a0, a1, a2, a3)):
            value += dot(part[...], wo[e])
        hidden[...] = value
        unit, _ = normalized(value)
        normed[...] = (unit * gain[...][None] + shift[...][None]).astype(BF16)
        low = (valid[...] * cot[...].astype(F32)).astype(BF16)
        grad_down[...] = low
        vectors[3:4, :] = jnp.sum(low.astype(F32), axis=0, keepdims=True)
        total_out[...] = value + down_bias[...][None]
        total_grad[...] = jnp.zeros_like(total_grad)

    gate = dot(normed[...], up[...]) + up_bias[0]
    below = 0.5 * (1.0 + lax.erf(gate * (0.5**0.5)))
    active = (gate * below).astype(BF16)
    slope = below + gate * (jnp.exp(-0.5 * gate * gate) * (0.5 / jnp.pi) ** 0.5)
    low = grad_down[...]
    grad_gate = (dot_nt(low, down[...]) * slope).astype(BF16)
    total_out[...] += dot(active, down[...])
    total_grad[...] += dot_nt(grad_gate, up[...])
    grad_up_bias[0] = jnp.sum(grad_gate.astype(F32), axis=0, keepdims=True)
    of_down = dot_tn(active, low).astype(BF16)
    of_up = dot_tn(normed[...], grad_gate).astype(BF16)
    for i in range(2 * half):

        @pl.when(step == i)
        def _(i=i):
            down_held, rest_held = (down_send, rest_send) if i < half else (down_keep, rest_keep)
            for j in range(share):
                at = (i % half) * share + j
                down_held[at] = of_down[j * each : (j + 1) * each]
                rest_held[at, :each, :] = of_up[j * each : (j + 1) * each]

    @pl.when(step == last)
    def _():
        unit, inverse = normalized(hidden[...])
        layer[...] = (valid[...] * total_out[...]).astype(BF16)
        grad = total_grad[...]
        vectors[0:1, :] = jnp.sum(grad * unit, axis=0, keepdims=True)
        vectors[1:2, :] = jnp.sum(grad, axis=0, keepdims=True)
        scaled = grad * gain[...][None]
        inner = scaled - jnp.mean(scaled, axis=-1, keepdims=True)
        inner = inner - unit * jnp.mean(scaled * unit, axis=-1, keepdims=True)
        grad = grad_down[...].astype(F32) + inverse * inner
        grad_hidden[...] = grad
        branch = grad.astype(BF16)
        vectors[2:3, :] = jnp.sum(branch.astype(F32), axis=0, keepdims=True)
        parts = (a0, a1, a2, a3)
        count = pieces // 2
        few = WIDTH // count
        for e, given in enumerate((g0, g1, g2, g3)):
            given[...] = dot_nt(branch, wo[e]).astype(BF16)
            held = rest_keep if e < 2 else rest_send
            place = (side[1] ^ (e & 1)) * count
            of_out = dot_tn(parts[e][...], branch).astype(BF16)
            for j in range(count):
                held[place + j, each:, :] = of_out[j * few : (j + 1) * few]


def middle(core, near, pieces, x, attended, wo, out_bias, gain, shift, cot, down_bias, up, up_bias, down):
    rows, model = cot.shape
    blocks = up.shape[1] // model
    half = blocks // 2

    def block_of(i, side):
        return lax.rem(i, half) + half * jnp.where(i < half, 1 - side[0], side[0])

    whole_s = lambda *shape: pl.BlockSpec(shape, lambda i, side: (0,) * len(shape))
    each = half * model // pieces
    held = (pieces, each, model)
    rest = (pieces, each + 2 * WIDTH // pieces, model)
    shaped = jax.ShapeDtypeStruct
    outs = [
        (shaped((rows, model), BF16), whole_s(rows, model)),
        (shaped(held, BF16), whole_s(*held)),
        (shaped(held, BF16), whole_s(*held)),
        (shaped(rest, BF16), whole_s(*rest)),
        (shaped(rest, BF16), whole_s(*rest)),
        (shaped((blocks, 1, model), F32), pl.BlockSpec((1, 1, model), lambda i, side: (block_of(i, side), 0, 0))),
        (shaped((rows, model), F32), whole_s(rows, model)),
    ]
    outs += [(shaped((rows, WIDTH), BF16), whole_s(rows, WIDTH))] * MEMBERS
    outs += [(shaped((4, model), F32), whole_s(4, model))]
    return pl.pallas_call(
        middle_kernel,
        out_shape=[o[0] for o in outs],
        grid_spec=pltpu.PrefetchScalarGridSpec(
            num_scalar_prefetch=1,
            grid=(blocks,),
            in_specs=[whole_s(*x.shape)]
            + [whole_s(rows, WIDTH)] * MEMBERS
            + [whole_s(MEMBERS, WIDTH, model)]
            + [whole_s(model)] * 3
            + [whole_s(rows, model), whole_s(model)]
            + [
                pl.BlockSpec((model, model), lambda i, side: (0, block_of(i, side))),
                pl.BlockSpec((1, 1, model), lambda i, side: (block_of(i, side), 0, 0)),
                pl.BlockSpec((model, model), lambda i, side: (block_of(i, side), 0)),
            ],
            out_specs=[o[1] for o in outs],
            scratch_shapes=[
                VMEM((rows, model), F32),
                VMEM((rows, model), BF16),
                VMEM((rows, model), BF16),
                VMEM((rows, model), F32),
                VMEM((rows, model), F32),
                VMEM((rows, 1), F32),
            ],
        ),
        compiler_params=params(),
        cost_estimate=QUICK,
        name="middle",
    )(
        jnp.stack([core, near]).astype(jnp.int32),
        x, *attended, wo, out_bias, gain, shift, cot, down_bias,
        up, up_bias.reshape(blocks, 1, model), down,
    )


def place_down_kernel(side, a0, b0, a1, b1, out):
    lanes = a0.shape[2]

    @pl.when(pl.program_id(0) == 0)
    def _():
        out[:, :lanes] = a0[0].astype(F32)
        out[:, lanes:] = b0[0].astype(F32)

    @pl.when(pl.program_id(0) == 1)
    def _():
        out[:, :lanes] = a1[0].astype(F32)
        out[:, lanes:] = b1[0].astype(F32)


def place_rest_kernel(side, a0, b0, a1, b1, up, out):
    lanes = a0.shape[2]
    each = up.shape[0]

    @pl.when(pl.program_id(0) == 0)
    def _():
        for at, part in ((0, a0), (lanes, b0)):
            up[:, at : at + lanes] = part[0, :each, :].astype(F32)
            out[:, at : at + lanes] = part[0, each:, :].astype(F32)

    @pl.when(pl.program_id(0) == 1)
    def _():
        for at, part in ((0, a1), (lanes, b1)):
            up[:, at : at + lanes] = part[0, :each, :].astype(F32)
            out[:, at : at + lanes] = part[0, each:, :].astype(F32)


def placed(kernel, core, parts, outs):
    pieces, rows, lanes = parts[0].shape
    first = pl.BlockSpec((1, rows, lanes), lambda n, i, side: (jnp.where(n == 0, i, pieces - 1), 0, 0))
    second = pl.BlockSpec((1, rows, lanes), lambda n, i, side: (jnp.where(n == 0, 0, i), 0, 0))
    return pl.pallas_call(
        kernel,
        out_shape=[jax.ShapeDtypeStruct(shape, F32) for shape, _, _ in outs],
        grid_spec=pltpu.PrefetchScalarGridSpec(
            num_scalar_prefetch=1,
            grid=(2, pieces),
            in_specs=[first, first, second, second],
            out_specs=[
                pl.BlockSpec(block, lambda n, i, side, place=place: place(lax.rem(n + side[0], 2), i))
                for _, block, place in outs
            ],
        ),
        compiler_params=params(),
        cost_estimate=QUICK,
        name="placed",
    )(core, *parts)


def placed_down(core, parts, hidden_units):
    pieces, each, lanes = parts[0].shape
    (down,) = placed(
        place_down_kernel,
        core,
        parts,
        [((hidden_units, 2 * lanes), (each, 2 * lanes), lambda k, i: (k * pieces + i, 0))],
    )
    return down


def placed_rest(core, parts, hidden_units):
    pieces, rows, lanes = parts[0].shape
    model = 2 * lanes
    each = hidden_units // 2 // pieces
    few = rows - each
    share = model // each
    half = hidden_units // model // 2
    return placed(
        place_rest_kernel,
        core,
        parts,
        [
            ((model, hidden_units), (each, model), lambda k, i: (lax.rem(i, share), k * half + i // share)),
            ((2 * pieces * few, model), (few, model), lambda k, i: (k * pieces + i, 0)),
        ],
    )


def place_in_kernel(gathered, out):
    model = out.shape[1] // 3
    rows = gathered.shape[5]
    for n in range(2):
        for p in range(2):
            here = pl.ds((2 * n + p) * rows, rows)
            for s in range(3):
                parts = [
                    gathered[0, k, p, q, n, :, s * WIDTH : (s + 1) * WIDTH]
                    for k in range(2)
                    for q in range(2)
                ]
                out[here, s * model : (s + 1) * model] = jnp.concatenate(parts, axis=1).astype(F32)


def placed_in(gathered):
    pieces, *rest = gathered.shape
    rows, width = rest[-2:]
    model = width * MEMBERS // 3
    return pl.pallas_call(
        place_in_kernel,
        grid=(pieces,),
        out_shape=jax.ShapeDtypeStruct((pieces * 4 * rows, 3 * model), F32),
        in_specs=[pl.BlockSpec((1, *rest), lambda i: (i, 0, 0, 0, 0, 0, 0))],
        out_specs=pl.BlockSpec((4 * rows, 3 * model), lambda i: (i, 0)),
        compiler_params=params(),
        cost_estimate=QUICK,
        name="placed_in",
    )(gathered)


def over_cube(value, bit):
    count = lax.axis_size("cube")
    return lax.ppermute(value, "cube", [(i, i ^ (1 << bit)) for i in range(count)])


def over_blk(value, bit):
    return lax.ppermute(value, "blk", [(i, i ^ (1 << bit)) for i in range(MEMBERS)])


def chosen_pairs(is_home, cube_flip, blk_flip):
    pairs = []
    for c in range(lax.axis_size("cube")):
        for b in range(MEMBERS):
            if ((c & 1) == (b >> 1)) == is_home:
                pairs.append((c * MEMBERS + b, (c ^ cube_flip) * MEMBERS + (b ^ blk_flip)))
    return pairs


def sent_between(value, is_home, cube_flip, blk_flip):
    return lax.ppermute(value, ("cube", "blk"), chosen_pairs(is_home, cube_flip, blk_flip))


def exchanged(parts):
    far = over_blk(parts[3], 0)
    near = over_blk(parts[1], 0)
    core = over_cube(parts[2], 0)
    return [parts[0], near, core, over_cube(far, 0)]


def half_of(rows, which, axis=0):
    size = rows.shape[axis] // 2
    return lax.dynamic_slice_in_dim(rows, which * size, size, axis)


def added(first, second):
    return (first.astype(F32) + second.astype(F32)).astype(BF16)


def halved(rows, flag, send, axis=0):
    got = send(half_of(rows, 1 - flag, axis))
    return added(half_of(rows, flag, axis), got)


def joined(own, got, flag, axis=0):
    return jnp.where(
        flag == 0,
        jnp.concatenate([own, got], axis),
        jnp.concatenate([got, own], axis),
    )


def cube_bits():
    return list(range(1, lax.axis_size("cube").bit_length() - 1))


def flag_of(index, bit):
    return (index >> bit) & 1


def summing(keep, send, cube, blk):
    (got,) = yield [(send, lambda v: over_cube(v, 0))]
    bits = cube_bits()
    pieces, rows, lanes = keep.shape
    total = added(keep, got).reshape((2,) * len(bits) + (rows, lanes))
    parts = [total[..., : lanes // 2], total[..., lanes // 2 :]]
    parts = yield from scattered(parts, cube)
    total = jnp.concatenate([p.reshape(2, 2, rows // MEMBERS, lanes // 2) for p in parts], axis=3)
    for bit in range(2):
        flag = flag_of(blk, bit)
        (got,) = yield [(half_of(total, 1 - flag, 1 - bit), functools.partial(over_blk, bit=bit))]
        total = added(half_of(total, flag, 1 - bit), got)
    for bit in (1, 0):
        (got,) = yield [(total, functools.partial(over_blk, bit=bit))]
        total = joined(total, got, flag_of(blk, bit), 1 - bit)
    total = total.reshape((1,) * len(bits) + (rows, lanes))
    parts = [total[..., : lanes // 2], total[..., lanes // 2 :]]
    for steps in zip(bits[::-1], bits):
        got = yield [(part, functools.partial(over_cube, bit=bit)) for part, bit in zip(parts, steps)]
        parts = [
            joined(part, other, flag_of(cube, bit), len(bits) - bit)
            for part, other, bit in zip(parts, got, steps)
        ]
    parts = [part.reshape(pieces, rows, lanes // 2) for part in parts]
    got = yield [(part, lambda v: over_cube(v, 0)) for part in parts]
    return parts + list(got)


def scattered(parts, cube):
    bits = cube_bits()
    for steps in zip(bits, bits[::-1]):
        flags = [flag_of(cube, bit) for bit in steps]
        axes = [len(bits) - bit for bit in steps]
        got = yield [
            (half_of(part, 1 - flag, axis), functools.partial(over_cube, bit=bit))
            for part, flag, axis, bit in zip(parts, flags, axes, steps)
        ]
        parts = [
            added(half_of(part, flag, axis), other)
            for part, flag, axis, other in zip(parts, flags, axes, got)
        ]
    return parts


def summing_columns(parts, cube, blk):
    bits = cube_bits()
    _, rows, lanes = parts[0].shape
    parts = yield from scattered([p.reshape((2,) * len(bits) + (rows, lanes)) for p in parts], cube)
    total = jnp.concatenate([p.reshape(1, 2, rows // 2, lanes) for p in parts])
    flag = flag_of(blk, 1)
    (got,) = yield [(half_of(total, 1 - flag, 1), functools.partial(over_blk, bit=1))]
    return added(half_of(total, flag, 1), got).reshape(2, rows // 2, lanes)


class Order:
    def __init__(self, token):
        self.token = token

    def __call__(self, values):
        values, self.token = lax.optimization_barrier((values, self.token))
        return values


class Running:
    def __init__(self, steps, order):
        self.steps = steps
        self.order = order
        self.result = None
        self.sent(next(steps))

    def sent(self, ready):
        values = self.order([v for v, _ in ready])
        self.arrived = [move(v) for v, (_, move) in zip(values, ready)]

    def step(self):
        arrived = self.order(self.arrived)
        try:
            ready = self.steps.send(arrived)
        except StopIteration as stop:
            self.result = stop.value
        else:
            self.sent(ready)

    def finish(self):
        while self.result is None:
            self.step()
        return self.result


def summing_vectors(rows):
    for bit in range(2):
        (got,) = yield [(rows, functools.partial(over_blk, bit=bit))]
        rows = rows + got
    for bit in range(lax.axis_size("cube").bit_length() - 1):
        (got,) = yield [(rows, functools.partial(over_cube, bit=bit))]
        rows = rows + got
    return rows


def member_columns(matrix, member, axis):
    return lax.dynamic_slice_in_dim(matrix, member * WIDTH, WIDTH, axis)


def body(
    inputs,
    cotangent,
    absent_groups,
    token_group,
    pre_gain,
    pre_shift,
    input_weight,
    input_bias,
    output_weight,
    output_bias,
    mid_gain,
    mid_shift,
    up_weight,
    up_bias,
    down_weight,
    down_bias,
):
    _, rows, model = inputs.shape
    hidden_units = up_weight.shape[1]
    cube, blk = lax.axis_index("cube"), lax.axis_index("blk")
    core = cube & 1
    pieces = lax.axis_size("cube") // 2
    at_home = core == (blk >> 1)
    member = 2 * core + (blk & 1)

    def moved(value):
        return jnp.where(at_home, value, sent_between(value, False, 1, 2))

    group_match = token_group[0][None, :] == jnp.arange(GROUPS, dtype=jnp.int32)[:, None]
    lacking = jnp.sum(jnp.where(group_match, absent_groups.reshape(GROUPS, 1), 0), axis=0)
    valid_here = (1 - lacking).astype(BF16)
    carried = jnp.concatenate(
        [inputs[0], jnp.broadcast_to(jnp.pad(valid_here, (0, model - rows)), (16, model))]
    )
    arriving = sent_between(carried, False, 1, 2)
    near_home = sent_between(carried, True, 0, 1)

    in_columns = jnp.concatenate(
        [member_columns(input_weight[:, s * model : (s + 1) * model], member, 1) for s in range(3)],
        axis=1,
    )
    bias_columns = member_columns(input_bias, member, 1)
    bias_columns = jnp.concatenate([bias_columns[0], jnp.zeros((WIDTH,), F32), bias_columns[1]])
    out_rows = jnp.stack([member_columns(output_weight, member ^ e, 0) for e in range(MEMBERS)])
    prepared = (in_columns, in_columns.T, bias_columns, bias_columns[:, None], out_rows)
    prepared, arriving = lax.optimization_barrier((prepared, arriving))
    in_columns, in_columns_turned, bias_columns, bias_turned, out_rows = prepared

    own = jnp.where(at_home, carried, arriving)
    near = jnp.where(at_home, near_home, sent_between(arriving, False, 0, 1))
    x_blocks = [own, near, over_cube(own, 0), over_cube(near, 0)]

    normed_low, qa, ka, va, qn, kt, vt = project(
        x_blocks, rows, pre_gain, pre_shift, in_columns, in_columns_turned, bias_columns, bias_turned
    )
    qa, cot_here = lax.optimization_barrier((qa, cotangent[0]))
    cot_own = moved(cot_here)
    attended_own, turned, logs = attend(qa, ka, vt)
    attended = exchanged(attended_own)
    (
        layer_here,
        down_send,
        down_keep,
        rest_send,
        rest_keep,
        grad_up_bias,
        grad_hidden,
        *grad_attended,
        middle_vectors,
    ) = middle(
        core,
        blk & 1,
        pieces,
        own,
        attended,
        out_rows,
        output_bias,
        mid_gain,
        mid_shift,
        cot_own,
        down_bias,
        up_weight,
        up_bias,
        down_weight,
    )
    blocks = hidden_units // model
    order = Order(core.astype(jnp.int32)[None])
    down_run = Running(summing(down_keep, down_send, cube, blk), order)
    rest_run = Running(summing(rest_keep, rest_send, cube, blk), order)
    grads_here = exchanged(grad_attended)
    down_run.step()
    rest_run.step()
    columns = []

    def back(head):
        grads = order(grads_here)
        columns.extend(order(attend_back(head, qa, ka, va, qn, kt, turned, logs, grads)))

    back(0)
    down_run.step()
    layer_out = moved(order(layer_here))
    back(1)
    down_run.step()
    rest_run.step()
    back(2)
    down_run.step()
    rest_run.step()
    p0, p1, p2, p3, in_first, in_second, column_total = order(
        unproject(order(columns), normed_low, in_columns, pieces)
    )
    core_far, core_near = over_cube(p3, 0), over_cube(p2, 0)
    in_run = Running(summing_columns([in_first, in_second], cube, blk), order)
    down_run.step()
    core_far, core_near = order((core_far, core_near))
    near_sum, own_sum = order((added(p1, core_far), added(p0, core_near)))
    near_got = over_blk(near_sum, 0)
    in_run.step()
    rest_run.step()
    down_run.step()
    in_run.step()
    rest_run.step()
    down_run.step()
    grad_here, grad_low, grad_pre = order(
        close(own, order([own_sum, near_got]), pre_gain, grad_hidden)
    )
    grad_moved = sent_between(grad_low, False, 1, 2)
    column_total = column_total[0]
    here_bias = jnp.stack([column_total[:WIDTH], column_total[2 * WIDTH :]])
    spread_bias = lax.dynamic_update_slice_in_dim(
        jnp.zeros((2, model), F32), here_bias, member * WIDTH, 1
    )
    vectors = jnp.concatenate(
        [grad_pre, middle_vectors, spread_bias, grad_up_bias.reshape(blocks, model)]
    )
    vector_run = Running(summing_vectors(vectors), order)
    gathered = lax.all_gather(in_run.finish(), ("cube", "blk"))
    rest_run.step()
    vector_run.step()
    down_run.step()
    rest_run.step()
    vector_run.step()
    down_run.step()
    rest_run.step()
    vector_run.step()
    down_run.step()
    (grad_down_weight,) = order([placed_down(order.token, down_run.finish(), hidden_units)])
    rest_run.step()
    vectors = vector_run.finish()
    grad_moved = order(grad_moved)
    input_grad = order(jnp.where(at_home, grad_here, grad_moved.astype(F32)))
    gathered = order(gathered)
    gathered = gathered.reshape((pieces, 2, 2, 2) + in_run.result.shape)
    grad_input_weight = order(placed_in(gathered))
    rest_sum = rest_run.finish()
    grad_up_weight, grad_output_weight = placed_rest(order.token, rest_sum, hidden_units)
    return (
        layer_out[None],
        input_grad[None],
        vectors[0],
        vectors[1],
        grad_input_weight,
        vectors[6:8],
        grad_output_weight,
        vectors[4],
        vectors[2],
        vectors[3],
        grad_up_weight,
        vectors[8:].reshape(-1),
        grad_down_weight,
        vectors[5],
    )


def solution(mesh):
    rows_spec = P("cube", "blk", None)
    return jax.shard_map(
        body,
        mesh=mesh,
        in_specs=(rows_spec, rows_spec, P("cube", None), P("cube", "blk")) + (P(),) * 12,
        out_specs=(rows_spec, rows_spec) + (P(),) * 12,
        check_vma=False,
    )
```

time: 490 us -> 413 us (0.84)
  blocking collectives: 38.9 us -> 0 us
  Pallas kernels: 100 us -> 133 us
  starting transfers between devices: 101 us -> 72.9 us
  local copies, waits for them, and re-layouts: 49 us -> 28.1 us
  other arithmetic: 58.6 us -> 38.6 us
  between operations: 1.92 us -> 15.1 us
  waiting for transfers between devices: 126 us -> 117 us
  matrix products: 5.38 us -> 0 us
    pallas_call x1 -> x8, Pallas kernels: 33.7 us -> 73.9 us  [the longest x3 37.7 us: attend_back(): pl.pallas_call(functools.partial(backward_kernel, head), grid=(1,), out_s...]
    psum x1 -> x0, blocking collectives: 38.9 us -> none  [body(): vectors = lax.psum(vectors, ('cube', 'blk'))]
    ppermute x41 -> x37, waiting for transfers between devices: 47 us -> 22.1 us  [over_cube(): lax.ppermute(value, 'cube', [(i, i ^ 1 << bit) for i in range(count)])]
    ppermute x41 -> x37, starting transfers between devices: 62.2 us -> 39 us  [over_cube(): lax.ppermute(value, 'cube', [(i, i ^ 1 << bit) for i in range(count)])]
    ppermute x9 -> x6, waiting for transfers between devices: 21.3 us -> 37.1 us  [sent_between(): lax.ppermute(value, ('cube', 'blk'), chosen_pairs(is_home, cube_flip, blk...]
    unnamed x84 -> x83, local copies, waits for them, and re-layouts: 21.8 us -> 6.17 us
    convert_element_type x5 -> x1, other arithmetic: 11.5 us -> 0.01 us  [body(): valid_here = (1 - lacking).astype(BF16)]
    ppermute x9 -> x6, starting transfers between devices: 30 us -> 20.4 us  [sent_between(): lax.ppermute(value, ('cube', 'blk'), chosen_pairs(is_home, cube_flip, blk...]
  transfers between devices with their start and end apart: 66 -> 60, of which waited for: 29 -> 26; matrix products, arithmetic and copies ran while one was open for 21% -> 13% of each run, Pallas kernels for 15% -> 21%
where the time goes in v3:
time: 413 us; the launch traced here: 405 us
  Pallas kernels  133 us (32%)
  waiting for transfers between devices  117 us (28%)
  starting transfers between devices  72.9 us (18%)
  other arithmetic  38.6 us (9%)
  local copies, waits for them, and re-layouts  28.1 us (7%)
  between operations  15.1 us (4%)
    ppermute x16, waiting for transfers between devices, over_blk(): lax.ppermute(value, 'blk', [(i, i ^ 1 << bit) for i in range(MEMBERS)])  58.2 us
    ppermute x37, starting transfers between devices, over_cube(): lax.ppermute(value, 'cube', [(i, i ^ 1 << bit) for i in range(count)])  39 us
    pallas_call x3, Pallas kernels, attend_back(): pl.pallas_call(functools.partial(backward_kernel, head), grid=(1,), out_s...  37.7 us
    ppermute x6, waiting for transfers between devices, sent_between(): lax.ppermute(value, ('cube', 'blk'), chosen_pairs(is_home, cube_flip, blk...  37.1 us
    pallas_call x1, Pallas kernels, middle(): pl.pallas_call(middle_kernel, out_shape=[o[0] for o in outs], grid_spec=p...  27.8 us
    ppermute x37, waiting for transfers between devices, over_cube(): lax.ppermute(value, 'cube', [(i, i ^ 1 << bit) for i in range(count)])  22.1 us
    ppermute x6, starting transfers between devices, sent_between(): lax.ppermute(value, ('cube', 'blk'), chosen_pairs(is_home, cube_flip, blk...  20.4 us
    pallas_call x1, Pallas kernels, attend(): pl.pallas_call(forward_kernel, grid=(n,), out_shape=[jax.ShapeDtypeStruct...  20.2 us
  transfers between devices with their start and end apart: 60, of which 26 were waited for; matrix products, arithmetic and copies ran while one was open for 13% of the time, Pallas kernels for 21%

profile of v3, /device:TPU:1, one launch (start us, length us, event | category | flops | bytes accessed | tf_op | source)
XLA Modules:
  0.0 405.2 jit_solution(4188113854384902321)
XLA Ops:
  8.0 2.0 pad_maximum_fusion.2
  10.7 5.6 %collective-permute-start = (bf16[448,768]{1,0:T(8,128)(2,1)}, bf16[448,768]{1,0:T(8,128)(2,1)}, u32[]{:S(2)}, u32[]{:S(2)}) collective-permute-start(bf16[448,768]{1,0:T(8,128)(2,1)} %pad_maximum_fusion.2), channel_id=1, source_target_pairs={{2,4},{3,5},{4,2},{5,3},{10,12},{11,13},{12,10},{13,11},{18,20},{1... | collective-permute-start | bytes 2064392 | tf_op jit(solution)/shard_map/ppermute | solution.py:594
  17.3 3.2 fusion.7
  20.8 1.4 constant_dynamic-slice_fusion.14
  22.5 1.3 pad_maximum_fusion.1.w.refs_10_
  25.1 7.6 %collective-permute-done = bf16[448,768]{1,0:T(8,128)(2,1)} collective-permute-done((bf16[448,768]{1,0:T(8,128)(2,1)}, bf16[448,768]{1,0:T(8,128)(2,1)}, u32[]{:S(2)}, u32[]{:S(2)}) %collective-permute-start) | collective-permute-done | bytes 688160 | tf_op jit(solution)/shard_map/ppermute | solution.py:594
  32.7 2.4 collective-permute-start.2
  35.1 1.3 broadcast_select_fusion.1.x0.x
  37.4 7.3 %collective-permute-done.2 = bf16[448,768]{1,0:T(8,128)(2,1)} collective-permute-done((bf16[448,768]{1,0:T(8,128)(2,1)}, bf16[448,768]{1,0:T(8,128)(2,1)}, u32[]{:S(2)}, u32[]{:S(2)}) %collective-permute-start.2) | collective-permute-done | bytes 688160 | tf_op jit(solution)/shard_map/ppermute | solution.py:594
  45.9 1.3 copy.39.wt
  48.2 11.2 %project.1 = (bf16[1728,768]{1,0:T(8,128)(2,1)}, bf16[3,128,1792]{2,1,0:T(8,128)(2,1)}, bf16[3,1728,128]{2,1,0:T(8,128)(2,1)}, bf16[3,1728,128]{2,1,0:T(8,128)(2...) custom-call(bf16[448,768]{1,0:T(8,128)(2,1)} %copy-done, ...), custom_call_target="tpu_custom_call" | custom-call | flops 1 | bytes 1 | tf_op jit(solution)/shard_map/project/pallas_call | solution.py:111
  59.4 5.3 %collective-permute-start.9 = (bf16[432,768]{1,0:T(8,128)(2,1)S(1)}, bf16[432,768]{1,0:T(8,128)(2,1)S(1)}, u32[]{:S(2)}, u32[]{:S(2)}) collective-permute-start(bf16[432,768]{1,0:T(8,128)(2,1)S(1)} %bitcast.71), channel_id=1, source_target_pairs={{2,4},{3,5},{4,2},{5,3},{10,12},{11,13},{12,10},{13,11},{18,20},{1... | collective-permute-start | bytes 1990664 | tf_op jit(solution)/shard_map/ppermute | solution.py:594
  64.7 20.2 %attend.1 = (bf16[432,192]{1,0:T(8,128)(2,1)}, bf16[432,192]{1,0:T(8,128)(2,1)}, bf16[432,192]{1,0:T(8,128)(2,1)}, bf16[432,192]{1,0:T(8,128)(2,1)}, f32[3,64,1792]{2,1,0:T(8,128)}, /*index=5*/f32[3,1,1792]{2,1,0:T(1,128)}) custom-call(bf16[3,128,1792]{2,1,0:T(8,128)(2,1)} %get-tuple-element.280.qa, bf16[3,1728,128]{2,1,0:T(8,128)(2,1)} %get-tuple-element.281.ka, ...), custom_call_target="tpu_custom_call" | custom-call | flops 1 | bytes 1 | tf_op jit(solution)/shard_map/attend/pallas_call | solution.py:166
  85.0 1.7 collective-permute-start.7
  87.3 3.8 collective-permute-done.7
  92.1 1.4 collective-permute-done.5.a1
  94.4 27.8 %middle.1 = (bf16[432,768]{1,0:T(8,128)(2,1)}, bf16[4,384,768]{2,1,0:T(8,128)(2,1)}, bf16[4,384,768]{2,1,0:T(8,128)(2,1)}, bf16[4,480,768]{2,1,0:T(8,128)(2,1)},...) custom-call(s32[2]{0:T(128)} %pad_add_fusion.side, ...), custom_call_target="tpu_custom_call" | custom-call | flops 1 | bytes 1 | tf_op jit(solution)/shard_map/middle/pallas_call | solution.py:426
  124.8 5.2 %collective-permute-done.15 = bf16[432,192]{1,0:T(8,128)(2,1)} collective-permute-done((bf16[432,192]{1,0:T(8,128)(2,1)}, bf16[432,192]{1,0:T(8,128)(2,1)}, u32[]{:S(2)}, u32[]{:S(2)}) %collective-permute-start.15) | collective-permute-done | bytes 165920 | tf_op jit(solution)/shard_map/ppermute | solution.py:581
  130.0 1.3 collective-permute-start.16
  131.3 2.9 add_convert_fusion.1
  142.6 12.5 %attend_back.3 = (bf16[1728,64]{1,0:T(8,128)(2,1)}, bf16[1728,64]{1,0:T(8,128)(2,1)}, bf16[1728,64]{1,0:T(8,128)(2,1)}) custom-call(bf16[3,128,1792]{2,1,0:T(8,128)(2,1)} %get-tuple-element.280.qa, bf16[3,1728,128]{2,1,0:T(8,128)(2,1)} %get-tuple-element.281.ka, bf16[3,1728,128]{2,1,0:T(8,128)(2,1)} %get-tuple-element.300.va, ...), custom_call_target="tpu_custom_call" | custom-call | flops 1 | bytes 1 | tf_op jit(solution)/shard_map/attend_back/pallas_call | solution.py:236
  155.1 1.5 add_convert_fusion.7
  162.4 12.6 %attend_back.4 = (bf16[1728,64]{1,0:T(8,128)(2,1)}, bf16[1728,64]{1,0:T(8,128)(2,1)}, bf16[1728,64]{1,0:T(8,128)(2,1)}) custom-call(bf16[3,128,1792]{2,1,0:T(8,128)(2,1)} %get-tuple-element.280.qa, bf16[3,1728,128]{2,1,0:T(8,128)(2,1)} %get-tuple-element.281.ka, bf16[3,1728,128]{2,1,0:T(8,128)(2,1)} %get-tuple-element.300.va, ...), custom_call_target="tpu_custom_call" | custom-call | flops 1 | bytes 1 | tf_op jit(solution)/shard_map/attend_back/pallas_call | solution.py:236
  179.2 4.3 %collective-permute-done.19 = bf16[2,1,480,384]{3,2,1,0:T(8,128)(2,1)} collective-permute-done((bf16[2,1,480,384]{3,2,1,0:T(8,128)(2,1)}, bf16[2,1,480,384]{3,2,1,0:T(8,128)(2,1)}, u32[]{:S(2)}, u32[]{:S(2)}) %collective-permute-start.19) | collective-permute-done | bytes 737312 | tf_op jit(solution)/shard_map/ppermute | solution.py:577
  183.6 1.3 add_convert_fusion.2
  184.9 1.6 add_convert_fusion.3
  188.4 12.6 %attend_back.5 = (bf16[1728,64]{1,0:T(8,128)(2,1)}, bf16[1728,64]{1,0:T(8,128)(2,1)}, bf16[1728,64]{1,0:T(8,128)(2,1)}) custom-call(bf16[3,128,1792]{2,1,0:T(8,128)(2,1)} %get-tuple-element.280.qa, bf16[3,1728,128]{2,1,0:T(8,128)(2,1)} %get-tuple-element.281.ka, bf16[3,1728,128]{2,1,0:T(8,128)(2,1)} %get-tuple-element.300.va, ...), custom_call_target="tpu_custom_call" | custom-call | flops 1 | bytes 1 | tf_op jit(solution)/shard_map/attend_back/pallas_call | solution.py:236
  202.2 3.4 collective-permute-start.28
  206.5 8.7 %unproject.1 = (bf16[432,768]{1,0:T(8,128)(2,1)}, bf16[432,768]{1,0:T(8,128)(2,1)}, bf16[432,768]{1,0:T(8,128)(2,1)}, bf16[432,768]{1,0:T(8,128)(2,1)}, bf16[4,9...) custom-call(bf16[1728,64]{1,0:T(8,128)(2,1)} %get-tuple-element.379.refs_0_, ...), custom_call_target="tpu_custom_call" | custom-call | flops 1 | bytes 1 | tf_op jit(solution)/shard_map/unproject/pallas_call | solution.py:287
  215.2 1.7 constant_dynamic-slice_fusion.4
  216.9 2.4 collective-permute-start.26
  219.3 1.7 constant_dynamic-slice_fusion.3
  224.8 1.3 dynamic_update_slice.3
  226.1 1.5 collective-permute-start.31
  232.4 5.4 %collective-permute-done.31 = bf16[2,1,120,768]{3,2,1,0:T(8,128)(2,1)S(1)} collective-permute-done((bf16[2,1,120,768]{3,2,1,0:T(8,128)(2,1)}, bf16[2,1,120,768]{3,2,1,0:T(8,128)(2,1)S(1)}, u32[]{:S(2)}, u32[]{:S(2)}) %collective-permute-start.31) | collective-permute-done | bytes 368672 | tf_op jit(solution)/shard_map/ppermute | solution.py:581
  237.9 1.7 collective-permute-start.36
  240.8 1.5 collective-permute-start.34
  242.3 1.3 collective-permute-done.37
  244.8 5.6 %collective-permute-done.35 = bf16[1,1,120,768]{3,2,1,0:T(8,128)(2,1)S(1)} collective-permute-done((bf16[1,1,120,768]{3,2,1,0:T(8,128)(2,1)S(1)}, bf16[1,1,120,768]{3,2,1,0:T(8,128)(2,1)S(1)}, u32[]{:S(2)}, u32[]{:S(2)}) %collective-permute-start.35) | collective-permute-done | bytes 184352 | tf_op jit(solution)/shard_map/ppermute | solution.py:581
  250.4 3.8 collective-permute-done.34
  254.3 14.1 %collective-permute-done.29.p1 = bf16[432,768]{1,0:T(8,128)(2,1)S(1)} collective-permute-done((bf16[432,768]{1,0:T(8,128)(2,1)S(1)}, bf16[432,768]{1,0:T(8,128)(2,1)S(1)}, u32[]{:S(2)}, u32[]{:S(2)}) %collective-permute-start.29) | collective-permute-done | bytes 663584 | tf_op jit(solution)/shard_map/ppermute | solution.py:581
  269.3 4.3 %close.1 = (f32[432,768]{1,0:T(8,128)}, bf16[432,768]{1,0:T(8,128)(2,1)}, f32[2,768]{1,0:T(2,128)}) custom-call(bf16[448,768]{1,0:T(8,128)(2,1)} %copy-done, bf16[432,768]{1,0:T(8,128)(2,1)} %add_convert_fusion.4.p0, bf16[432,768]{1,0:T(8,128)(2,1)} %copy-done.25, f32[768]{0:T(1024)} %gain.5, f32[432,768]{1,0:T(8,128)} %get-tuple-element.445.hidden), custom_call_target="tpu_custom_call" | custom-call | flops 1 | bytes 1 | tf_op jit(solution)/shard_map/close/pallas_call | solution.py:316
  277.1 9.0 %collective-permute-done.40 = bf16[1,1,120,768]{3,2,1,0:T(8,128)(2,1)S(1)} collective-permute-done((bf16[1,1,120,768]{3,2,1,0:T(8,128)(2,1)S(1)}, bf16[1,1,120,768]{3,2,1,0:T(8,128)(2,1)S(1)}, u32[]{:S(2)}, u32[]{:S(2)}) %collective-permute-start.40) | collective-permute-done | bytes 184352 | tf_op jit(solution)/shard_map/ppermute | solution.py:581
  286.1 1.5 collective-permute-start.43
  287.6 2.2 collective-permute-done.39
  290.9 1.4 collective-permute-start.50
  292.3 7.7 %collective-permute-done.43 = bf16[2,1,120,768]{3,2,1,0:T(8,128)(2,1)S(1)} collective-permute-done((bf16[2,1,120,768]{3,2,1,0:T(8,128)(2,1)S(1)}, bf16[2,1,120,768]{3,2,1,0:T(8,128)(2,1)S(1)}, u32[]{:S(2)}, u32[]{:S(2)}) %collective-permute-start.43) | collective-permute-done | bytes 368672 | tf_op jit(solution)/shard_map/ppermute | solution.py:581
  300.3 2.0 collective-permute-start.48
  302.3 1.5 collective-permute-done.49
  304.3 8.7 %collective-permute-start.54 = (bf16[4,384,384]{2,1,0:T(8,128)(2,1)S(1)}, bf16[4,384,384]{2,1,0:T(8,128)(2,1)S(1)}, u32[]{:S(2)}, u32[]{:S(2)}) collective-permute-start(bf16[4,384,384]{2,1,0:T(8,128)(2,1)S(1)} %bitcast.49), channel_id=1, source_target_pairs={{0,4},{4,0},{8,12},{12,8},{16,20},{20,16},{24,28},{28,24},{1,5},{5... | collective-permute-start | bytes 3538952 | tf_op jit(solution)/shard_map/ppermute | solution.py:577
  313.1 2.2 collective-permute-done.48
  317.0 3.5 collective-permute-start.46
  322.3 8.3 %placed.2 = f32[3072,768]{1,0:T(8,128)} custom-call(s32[1]{0:T(128)} %bitcast.side, bf16[4,384,384]{2,1,0:T(8,128)(2,1)} %bitcast.50, bf16[4,384,384]{2,1,0:T(8,128)(2,1)} %bitcast.52, bf16[4,384,384]{2,1,0:T(8,128)(2,1)} %copy-done.22, bf16[4,384,384]{2,1,0:T(8,128)(2,1)} %collective-permute-done.55.b1), custom_call_target="tpu_custom_call" | custom-call | flops 1 | bytes 1 | tf_op jit(solution)/shard_map/placed/pallas_call | solution.py:497
  330.6 6.6 %collective-permute-done.52 = bf16[2,1,480,384]{3,2,1,0:T(8,128)(2,1)S(1)} collective-permute-done((bf16[2,1,480,384]{3,2,1,0:T(8,128)(2,1)S(1)}, bf16[2,1,480,384]{3,2,1,0:T(8,128)(2,1)S(1)}, u32[]{:S(2)}, u32[]{:S(2)}) %collective-permute-start.52) | collective-permute-done | bytes 737312 | tf_op jit(solution)/shard_map/ppermute | solution.py:577
  339.3 1.6 maximum_select_fusion
  341.0 2.2 maximum_select_fusion.1
  343.2 3.3 collective-permute-start.57
  346.6 2.9 collective-permute-start.18
  349.5 3.5 collective-permute-start.38
  353.9 2.5 collective-permute-done.51
  357.0 16.7 %collective-permute-done.18 = bf16[432,768]{1,0:T(8,128)(2,1)S(1)} collective-permute-done((bf16[432,768]{1,0:T(8,128)(2,1)S(1)}, bf16[432,768]{1,0:T(8,128)(2,1)S(1)}, u32[]{:S(2)}, u32[]{:S(2)}) %collective-permute-start.18) | collective-permute-done | bytes 663584 | tf_op jit(solution)/shard_map/ppermute | solution.py:594
  375.2 5.6 %collective-permute-done.38 = bf16[432,768]{1,0:T(8,128)(2,1)S(1)} collective-permute-done((bf16[432,768]{1,0:T(8,128)(2,1)S(1)}, bf16[432,768]{1,0:T(8,128)(2,1)S(1)}, u32[]{:S(2)}, u32[]{:S(2)}) %collective-permute-start.38) | collective-permute-done | bytes 663584 | tf_op jit(solution)/shard_map/ppermute | solution.py:594
  383.3 5.7 %placed_in.1 = f32[768,2304]{1,0:T(8,128)} custom-call(bf16[4,2,2,2,2,48,576]{6,5,4,3,2,1,0:T(8,128)(2,1)} %bitcast.53), custom_call_target="tpu_custom_call" | custom-call | flops 1 | bytes 1 | tf_op jit(solution)/shard_map/placed_in/pallas_call | solution.py:563
  389.0 9.2 %placed.3 = (f32[768,3072]{1,0:T(8,128)}, f32[768,768]{1,0:T(8,128)}) custom-call(s32[1]{0:T(128)} %bitcast.side, bf16[4,480,384]{2,1,0:T(8,128)(2,1)} %bitcast.46, bf16[4,480,384]{2,1,0:T(8,128)(2,1)} %bitcast.48, bf16[4,480,384]{2,1,0:T(8,128)(2,1)} %collective-permute-done.57.a1, bf16[4,480,384]{2,1,0:T(8,128)(2,1)} %collective-permute-done.58.b1), custom_call_target="tpu_custom_call" | custom-call | flops 1 | bytes 1 | tf_op jit(solution)/shard_map/placed/pallas_call | solution.py:497
  (243 shorter events, 63.3 us)
Async XLA Ops:
  7.2 376.1 %all-gather.3.cloned.1.call-start = ((), (), s32[]{:S(2)}) async-start(), calls=%async_computation | async-start | bytes 4055040 | tf_op jit(solution)/shard_map/all_gather | solution.py:873
  10.0 26.4 %collective-permute-start.1 = (bf16[448,768]{1,0:T(8,128)(2,1)}, bf16[448,768]{1,0:T(8,128)(2,1)S(1)}, u32[]{:S(2)}, u32[]{:S(2)}) collective-permute-start(bf16[448,768]{1,0:T(8,128)(2,1)} %pad_maximum_fusion.2), channel_id=1, source_target_pairs={{0,1},{1,0},{6,7},{7,6},{8,9},{9,8},{14,15},{15,14},{16,17},{17,16... | collective-permute-start | bytes 2064392 | tf_op jit(solution)/shard_map/ppermute | solution.py:594
  10.7 22.0 %collective-permute-start = (bf16[448,768]{1,0:T(8,128)(2,1)}, bf16[448,768]{1,0:T(8,128)(2,1)}, u32[]{:S(2)}, u32[]{:S(2)}) collective-permute-start(bf16[448,768]{1,0:T(8,128)(2,1)} %pad_maximum_fusion.2), channel_id=1, source_target_pairs={{2,4},{3,5},{4,2},{5,3},{10,12},{11,13},{12,10},{13,11},{18,20},{1... | collective-permute-start | bytes 2064392 | tf_op jit(solution)/shard_map/ppermute | solution.py:594
  32.7 12.0 %collective-permute-start.2 = (bf16[448,768]{1,0:T(8,128)(2,1)}, bf16[448,768]{1,0:T(8,128)(2,1)}, u32[]{:S(2)}, u32[]{:S(2)}) collective-permute-start(bf16[448,768]{1,0:T(8,128)(2,1)} %collective-permute-done), channel_id=1, source_target_pairs={{2,3},{3,2},{4,5},{5,4},{10,11},{11,10},{12,13},{13,12},{18,19},{1... | collective-permute-start | bytes 2064392 | tf_op jit(solution)/shard_map/ppermute | solution.py:594
  36.4 11.7 %collective-permute-start.3 = (bf16[448,768]{1,0:T(8,128)(2,1)S(1)}, bf16[448,768]{1,0:T(8,128)(2,1)}, u32[]{:S(2)}, u32[]{:S(2)}) collective-permute-start(bf16[448,768]{1,0:T(8,128)(2,1)S(1)} %broadcast_select_fusion.1.x0.x), channel_id=1, source_target_pairs={{0,4},{4,0},{8,12},{12,8},{16,20},{20,16},{24,28},{28,24},{1,5},{5... | collective-permute-start | bytes 2064392 | tf_op jit(solution)/shard_map/ppermute | solution.py:577
  45.9 2.3 collective-permute-start.4
  59.4 31.7 %collective-permute-start.9 = (bf16[432,768]{1,0:T(8,128)(2,1)S(1)}, bf16[432,768]{1,0:T(8,128)(2,1)S(1)}, u32[]{:S(2)}, u32[]{:S(2)}) collective-permute-start(bf16[432,768]{1,0:T(8,128)(2,1)S(1)} %bitcast.71), channel_id=1, source_target_pairs={{2,4},{3,5},{4,2},{5,3},{10,12},{11,13},{12,10},{13,11},{18,20},{1... | collective-permute-start | bytes 1990664 | tf_op jit(solution)/shard_map/ppermute | solution.py:594
  85.0 6.1 %collective-permute-start.7 = (bf16[432,192]{1,0:T(8,128)(2,1)}, bf16[432,192]{1,0:T(8,128)(2,1)S(1)}, u32[]{:S(2)}, u32[]{:S(2)}) collective-permute-start(bf16[432,192]{1,0:T(8,128)(2,1)} %get-tuple-element.286), channel_id=1, source_target_pairs={{0,1},{1,0},{2,3},{3,2},{4,5},{5,4},{6,7},{7,6},{8,9},{9,8},{10,11... | collective-permute-start | bytes 497672 | tf_op jit(solution)/shard_map/ppermute | solution.py:581
  87.3 6.2 %collective-permute-start.5 = (bf16[432,192]{1,0:T(8,128)(2,1)}, bf16[432,192]{1,0:T(8,128)(2,1)S(1)}, u32[]{:S(2)}, u32[]{:S(2)}) collective-permute-start(bf16[432,192]{1,0:T(8,128)(2,1)} %get-tuple-element.284), channel_id=1, source_target_pairs={{0,1},{1,0},{2,3},{3,2},{4,5},{5,4},{6,7},{7,6},{8,9},{9,8},{10,11... | collective-permute-start | bytes 497672 | tf_op jit(solution)/shard_map/ppermute | solution.py:581
  87.3 6.2 %collective-permute-start.6 = (bf16[432,192]{1,0:T(8,128)(2,1)}, bf16[432,192]{1,0:T(8,128)(2,1)S(1)}, u32[]{:S(2)}, u32[]{:S(2)}) collective-permute-start(bf16[432,192]{1,0:T(8,128)(2,1)} %get-tuple-element.285), channel_id=1, source_target_pairs={{0,4},{4,0},{8,12},{12,8},{16,20},{20,16},{24,28},{28,24},{1,5},{5... | collective-permute-start | bytes 497672 | tf_op jit(solution)/shard_map/ppermute | solution.py:577
  91.1 2.4 collective-permute-start.8
  122.1 9.2 %collective-permute-start.10 = (bf16[4,384,768]{2,1,0:T(8,128)(2,1)}, bf16[4,384,768]{2,1,0:T(8,128)(2,1)}, u32[]{:S(2)}, u32[]{:S(2)}) collective-permute-start(bf16[4,384,768]{2,1,0:T(8,128)(2,1)} %get-tuple-element.292), channel_id=1, source_target_pairs={{0,4},{4,0},{8,12},{12,8},{16,20},{20,16},{24,28},{28,24},{1,5},{5... | collective-permute-start | bytes 7077896 | tf_op jit(solution)/shard_map/ppermute | solution.py:577
  122.2 15.3 %collective-permute-start.17 = (bf16[4,480,768]{2,1,0:T(8,128)(2,1)}, bf16[4,480,768]{2,1,0:T(8,128)(2,1)S(1)}, u32[]{:S(2)}, u32[]{:S(2)}) collective-permute-start(bf16[4,480,768]{2,1,0:T(8,128)(2,1)} %get-tuple-element.310), channel_id=1, source_target_pairs={{0,4},{4,0},{8,12},{12,8},{16,20},{20,16},{24,28},{28,24},{1,5},{5... | collective-permute-start | bytes 8847368 | tf_op jit(solution)/shard_map/ppermute | solution.py:577
  122.7 7.3 %collective-permute-start.15 = (bf16[432,192]{1,0:T(8,128)(2,1)}, bf16[432,192]{1,0:T(8,128)(2,1)}, u32[]{:S(2)}, u32[]{:S(2)}) collective-permute-start(bf16[432,192]{1,0:T(8,128)(2,1)} %get-tuple-element.308), channel_id=1, source_target_pairs={{0,1},{1,0},{2,3},{3,2},{4,5},{5,4},{6,7},{7,6},{8,9},{9,8},{10,11... | collective-permute-start | bytes 497672 | tf_op jit(solution)/shard_map/ppermute | solution.py:581
  123.3 18.5 %collective-permute-start.13 = (bf16[432,192]{1,0:T(8,128)(2,1)}, bf16[432,192]{1,0:T(8,128)(2,1)S(1)}, u32[]{:S(2)}, u32[]{:S(2)}) collective-permute-start(bf16[432,192]{1,0:T(8,128)(2,1)} %get-tuple-element.306), channel_id=1, source_target_pairs={{0,1},{1,0},{2,3},{3,2},{4,5},{5,4},{6,7},{7,6},{8,9},{9,8},{10,11... | collective-permute-start | bytes 497672 | tf_op jit(solution)/shard_map/ppermute | solution.py:581
  124.2 17.6 %collective-permute-start.14 = (bf16[432,192]{1,0:T(8,128)(2,1)}, bf16[432,192]{1,0:T(8,128)(2,1)S(1)}, u32[]{:S(2)}, u32[]{:S(2)}) collective-permute-start(bf16[432,192]{1,0:T(8,128)(2,1)} %get-tuple-element.307), channel_id=1, source_target_pairs={{0,4},{4,0},{8,12},{12,8},{16,20},{20,16},{24,28},{28,24},{1,5},{5... | collective-permute-start | bytes 497672 | tf_op jit(solution)/shard_map/ppermute | solution.py:577
  130.0 11.8 %collective-permute-start.16 = (bf16[432,192]{1,0:T(8,128)(2,1)}, bf16[432,192]{1,0:T(8,128)(2,1)S(1)}, u32[]{:S(2)}, u32[]{:S(2)}) collective-permute-start(bf16[432,192]{1,0:T(8,128)(2,1)} %collective-permute-done.15), channel_id=1, source_target_pairs={{0,4},{4,0},{8,12},{12,8},{16,20},{20,16},{24,28},{28,24},{1,5},{5... | collective-permute-start | bytes 497672 | tf_op jit(solution)/shard_map/ppermute | solution.py:577
  136.3 18.8 %collective-permute-start.11 = (bf16[2,1,384,384]{3,2,1,0:T(8,128)(2,1)}, bf16[2,1,384,384]{3,2,1,0:T(8,128)(2,1)}, u32[]{:S(2)}, u32[]{:S(2)}) collective-permute-start(bf16[2,1,384,384]{3,2,1,0:T(8,128)(2,1)} %constant_dynamic-slice_fusion.13), channel_id=1, source_target_pairs={{0,8},{4,12},{8,0},{12,4},{16,24},{20,28},{24,16},{28,20},{1,9},{5... | collective-permute-start | bytes 1769480 | tf_op jit(solution)/shard_map/ppermute | solution.py:577
  137.5 17.6 %collective-permute-start.12 = (bf16[1,2,384,384]{3,2,1,0:T(8,128)(2,1)}, bf16[1,2,384,384]{3,2,1,0:T(8,128)(2,1)}, u32[]{:S(2)}, u32[]{:S(2)}) collective-permute-start(bf16[1,2,384,384]{3,2,1,0:T(8,128)(2,1)} %constant_dynamic-slice_fusion.12), channel_id=1, source_target_pairs={{0,16},{4,20},{8,24},{12,28},{16,0},{20,4},{24,8},{28,12},{1,17},{... | collective-permute-start | bytes 1769480 | tf_op jit(solution)/shard_map/ppermute | solution.py:577
  159.5 15.5 %collective-permute-start.21 = (bf16[1,1,384,384]{3,2,1,0:T(8,128)(2,1)}, bf16[1,1,384,384]{3,2,1,0:T(8,128)(2,1)S(1)}, u32[]{:S(2)}, u32[]{:S(2)}) collective-permute-start(bf16[1,1,384,384]{3,2,1,0:T(8,128)(2,1)} %constant_dynamic-slice_fusion.9), channel_id=1, source_target_pairs={{0,16},{4,20},{8,24},{12,28},{16,0},{20,4},{24,8},{28,12},{1,17},{... | collective-permute-start | bytes 884744 | tf_op jit(solution)/shard_map/ppermute | solution.py:577
  159.7 16.0 %collective-permute-start.22 = (bf16[1,1,384,384]{3,2,1,0:T(8,128)(2,1)}, bf16[1,1,384,384]{3,2,1,0:T(8,128)(2,1)S(1)}, u32[]{:S(2)}, u32[]{:S(2)}) collective-permute-start(bf16[1,1,384,384]{3,2,1,0:T(8,128)(2,1)} %constant_dynamic-slice_fusion.8), channel_id=1, source_target_pairs={{0,8},{4,12},{8,0},{12,4},{16,24},{20,28},{24,16},{28,20},{1,9},{5... | collective-permute-start | bytes 884744 | tf_op jit(solution)/shard_map/ppermute | solution.py:577
  160.5 23.0 %collective-permute-start.19 = (bf16[2,1,480,384]{3,2,1,0:T(8,128)(2,1)}, bf16[2,1,480,384]{3,2,1,0:T(8,128)(2,1)}, u32[]{:S(2)}, u32[]{:S(2)}) collective-permute-start(bf16[2,1,480,384]{3,2,1,0:T(8,128)(2,1)} %constant_dynamic-slice_fusion.11), channel_id=1, source_target_pairs={{0,8},{4,12},{8,0},{12,4},{16,24},{20,28},{24,16},{28,20},{1,9},{5... | collective-permute-start | bytes 2211848 | tf_op jit(solution)/shard_map/ppermute | solution.py:577
  161.2 22.4 %collective-permute-start.20 = (bf16[1,2,480,384]{3,2,1,0:T(8,128)(2,1)}, bf16[1,2,480,384]{3,2,1,0:T(8,128)(2,1)}, u32[]{:S(2)}, u32[]{:S(2)}) collective-permute-start(bf16[1,2,480,384]{3,2,1,0:T(8,128)(2,1)} %constant_dynamic-slice_fusion.10), channel_id=1, source_target_pairs={{0,16},{4,20},{8,24},{12,28},{16,0},{20,4},{24,8},{28,12},{1,17},{... | collective-permute-start | bytes 2211848 | tf_op jit(solution)/shard_map/ppermute | solution.py:577
  178.6 22.4 %collective-permute-start.25 = (bf16[2,1,96,768]{3,2,1,0:T(8,128)(2,1)}, bf16[2,1,96,768]{3,2,1,0:T(8,128)(2,1)}, u32[]{:S(2)}, u32[]{:S(2)}) collective-permute-start(bf16[2,1,96,768]{3,2,1,0:T(8,128)(2,1)} %fusion.3), channel_id=1, source_target_pairs={{0,1},{1,0},{2,3},{3,2},{4,5},{5,4},{6,7},{7,6},{8,9},{9,8},{10,11... | collective-permute-start | bytes 884744 | tf_op jit(solution)/shard_map/ppermute | solution.py:581
  186.6 18.9 %collective-permute-start.23 = (bf16[1,1,480,384]{3,2,1,0:T(8,128)(2,1)S(1)}, bf16[1,1,480,384]{3,2,1,0:T(8,128)(2,1)S(1)}, u32[]{:S(2)}, u32[]{:S(2)}) collective-permute-start(bf16[1,1,480,384]{3,2,1,0:T(8,128)(2,1)S(1)} %constant_dynamic-slice_fusion.7), channel_id=1, source_target_pairs={{0,16},{4,20},{8,24},{12,28},{16,0},{20,4},{24,8},{28,12},{1,17},{... | collective-permute-start | bytes 1105928 | tf_op jit(solution)/shard_map/ppermute | solution.py:577
  187.8 17.7 %collective-permute-start.24 = (bf16[1,1,480,384]{3,2,1,0:T(8,128)(2,1)S(1)}, bf16[1,1,480,384]{3,2,1,0:T(8,128)(2,1)S(1)}, u32[]{:S(2)}, u32[]{:S(2)}) collective-permute-start(bf16[1,1,480,384]{3,2,1,0:T(8,128)(2,1)S(1)} %constant_dynamic-slice_fusion.6), channel_id=1, source_target_pairs={{0,8},{4,12},{8,0},{12,4},{16,24},{20,28},{24,16},{28,20},{1,9},{5... | collective-permute-start | bytes 1105928 | tf_op jit(solution)/shard_map/ppermute | solution.py:577
  202.2 18.9 %collective-permute-start.28 = (bf16[1,1,96,768]{3,2,1,0:T(8,128)(2,1)S(1)}, bf16[1,1,96,768]{3,2,1,0:T(8,128)(2,1)}, u32[]{:S(2)}, u32[]{:S(2)}) collective-permute-start(bf16[1,1,96,768]{3,2,1,0:T(8,128)(2,1)S(1)} %constant_dynamic-slice_fusion.5), channel_id=1, source_target_pairs={{0,2},{1,3},{2,0},{3,1},{4,6},{5,7},{6,4},{7,5},{8,10},{9,11},{10,... | collective-permute-start | bytes 442376 | tf_op jit(solution)/shard_map/ppermute | solution.py:581
  215.2 12.5 %copy-start.29 = (bf16[432,768]{1,0:T(8,128)(2,1)S(1)}, bf16[432,768]{1,0:T(8,128)(2,1)}, u32[]{:S(2)}) copy-start(bf16[432,768]{1,0:T(8,128)(2,1)} %get-tuple-element.397) | copy-start | bytes 1990660
  216.9 9.2 %collective-permute-start.26 = (bf16[432,768]{1,0:T(8,128)(2,1)}, bf16[432,768]{1,0:T(8,128)(2,1)S(1)}, u32[]{:S(2)}, u32[]{:S(2)}) collective-permute-start(bf16[432,768]{1,0:T(8,128)(2,1)} %get-tuple-element.398), channel_id=1, source_target_pairs={{0,4},{4,0},{8,12},{12,8},{16,20},{20,16},{24,28},{28,24},{1,5},{5... | collective-permute-start | bytes 1990664 | tf_op jit(solution)/shard_map/ppermute | solution.py:577
  219.3 8.4 %collective-permute-start.27 = (bf16[432,768]{1,0:T(8,128)(2,1)}, bf16[432,768]{1,0:T(8,128)(2,1)S(1)}, u32[]{:S(2)}, u32[]{:S(2)}) collective-permute-start(bf16[432,768]{1,0:T(8,128)(2,1)} %get-tuple-element.399), channel_id=1, source_target_pairs={{0,4},{4,0},{8,12},{12,8},{16,20},{20,16},{24,28},{28,24},{1,5},{5... | collective-permute-start | bytes 1990664 | tf_op jit(solution)/shard_map/ppermute | solution.py:577
  222.0 17.7 %collective-permute-start.30 = (bf16[1,1,96,768]{3,2,1,0:T(8,128)(2,1)S(1)}, bf16[1,1,96,768]{3,2,1,0:T(8,128)(2,1)}, u32[]{:S(2)}, u32[]{:S(2)}) collective-permute-start(bf16[1,1,96,768]{3,2,1,0:T(8,128)(2,1)S(1)} %add_convert_fusion.17), channel_id=1, source_target_pairs={{0,2},{1,3},{2,0},{3,1},{4,6},{5,7},{6,4},{7,5},{8,10},{9,11},{10,... | collective-permute-start | bytes 442376 | tf_op jit(solution)/shard_map/ppermute | solution.py:581
  222.0 7.4 %collective-permute-start.32 = (bf16[2,1,96,576]{3,2,1,0:T(8,128)(2,1)}, bf16[2,1,96,576]{3,2,1,0:T(8,128)(2,1)}, u32[]{:S(2)}, u32[]{:S(2)}) collective-permute-start(bf16[2,1,96,576]{3,2,1,0:T(8,128)(2,1)} %constant_dynamic-slice_fusion.4), channel_id=1, source_target_pairs={{0,8},{4,12},{8,0},{12,4},{16,24},{20,28},{24,16},{28,20},{1,9},{5... | collective-permute-start | bytes 663560 | tf_op jit(solution)/shard_map/ppermute | solution.py:577
  223.3 7.0 %collective-permute-start.33 = (bf16[1,2,96,576]{3,2,1,0:T(8,128)(2,1)}, bf16[1,2,96,576]{3,2,1,0:T(8,128)(2,1)}, u32[]{:S(2)}, u32[]{:S(2)}) collective-permute-start(bf16[1,2,96,576]{3,2,1,0:T(8,128)(2,1)} %constant_dynamic-slice_fusion.3), channel_id=1, source_target_pairs={{0,16},{4,20},{8,24},{12,28},{16,0},{20,4},{24,8},{28,12},{1,17},{... | collective-permute-start | bytes 663560 | tf_op jit(solution)/shard_map/ppermute | solution.py:577
  226.1 11.7 %collective-permute-start.31 = (bf16[2,1,120,768]{3,2,1,0:T(8,128)(2,1)}, bf16[2,1,120,768]{3,2,1,0:T(8,128)(2,1)S(1)}, u32[]{:S(2)}, u32[]{:S(2)}) collective-permute-start(bf16[2,1,120,768]{3,2,1,0:T(8,128)(2,1)} %fusion.1), channel_id=1, source_target_pairs={{0,1},{1,0},{2,3},{3,2},{4,5},{5,4},{6,7},{7,6},{8,9},{9,8},{10,11... | collective-permute-start | bytes 1105928 | tf_op jit(solution)/shard_map/ppermute | solution.py:581
  237.9 4.4 %collective-permute-start.36 = (bf16[1,1,96,576]{3,2,1,0:T(8,128)(2,1)S(1)}, bf16[1,1,96,576]{3,2,1,0:T(8,128)(2,1)S(1)}, u32[]{:S(2)}, u32[]{:S(2)}) collective-permute-start(bf16[1,1,96,576]{3,2,1,0:T(8,128)(2,1)S(1)} %constant_dynamic-slice_fusion.2), channel_id=1, source_target_pairs={{0,16},{4,20},{8,24},{12,28},{16,0},{20,4},{24,8},{28,12},{1,17},{... | collective-permute-start | bytes 331784 | tf_op jit(solution)/shard_map/ppermute | solution.py:577
  239.6 4.0 collective-permute-start.37
  240.7 9.7 %collective-permute-start.35 = (bf16[1,1,120,768]{3,2,1,0:T(8,128)(2,1)S(1)}, bf16[1,1,120,768]{3,2,1,0:T(8,128)(2,1)S(1)}, u32[]{:S(2)}, u32[]{:S(2)}) collective-permute-start(bf16[1,1,120,768]{3,2,1,0:T(8,128)(2,1)S(1)} %constant_dynamic-slice_fusion), channel_id=1, source_target_pairs={{0,2},{1,3},{2,0},{3,1},{4,6},{5,7},{6,4},{7,5},{8,10},{9,11},{10,... | collective-permute-start | bytes 552968 | tf_op jit(solution)/shard_map/ppermute | solution.py:581
  240.8 13.4 %collective-permute-start.34 = (bf16[2,1,96,768]{3,2,1,0:T(8,128)(2,1)S(1)}, bf16[2,1,96,768]{3,2,1,0:T(8,128)(2,1)S(1)}, u32[]{:S(2)}, u32[]{:S(2)}) collective-permute-start(bf16[2,1,96,768]{3,2,1,0:T(8,128)(2,1)S(1)} %maximum_select_fusion.11), channel_id=1, source_target_pairs={{0,1},{1,0},{2,3},{3,2},{4,5},{5,4},{6,7},{7,6},{8,9},{9,8},{10,11... | collective-permute-start | bytes 884744 | tf_op jit(solution)/shard_map/ppermute | solution.py:581
  242.3 26.2 %collective-permute-start.29 = (bf16[432,768]{1,0:T(8,128)(2,1)S(1)}, bf16[432,768]{1,0:T(8,128)(2,1)S(1)}, u32[]{:S(2)}, u32[]{:S(2)}) collective-permute-start(bf16[432,768]{1,0:T(8,128)(2,1)S(1)} %add_convert_fusion.5), channel_id=1, source_target_pairs={{0,1},{1,0},{2,3},{3,2},{4,5},{5,4},{6,7},{7,6},{8,9},{9,8},{10,11... | collective-permute-start | bytes 1990664 | tf_op jit(solution)/shard_map/ppermute | solution.py:581
  243.8 30.6 %collective-permute-start.41 = (bf16[2,1,48,576]{3,2,1,0:T(8,128)(2,1)S(1)}, bf16[2,1,48,576]{3,2,1,0:T(8,128)(2,1)S(1)}, u32[]{:S(2)}, u32[]{:S(2)}) collective-permute-start(bf16[2,1,48,576]{3,2,1,0:T(8,128)(2,1)S(1)} %fusion.5), channel_id=1, source_target_pairs={{0,2},{1,3},{2,0},{3,1},{4,6},{5,7},{6,4},{7,5},{8,10},{9,11},{10,... | collective-permute-start | bytes 331784 | tf_op jit(solution)/shard_map/ppermute | solution.py:581
  275.0 11.0 %collective-permute-start.40 = (bf16[1,1,120,768]{3,2,1,0:T(8,128)(2,1)S(1)}, bf16[1,1,120,768]{3,2,1,0:T(8,128)(2,1)S(1)}, u32[]{:S(2)}, u32[]{:S(2)}) collective-permute-start(bf16[1,1,120,768]{3,2,1,0:T(8,128)(2,1)S(1)} %add_convert_fusion.16), channel_id=1, source_target_pairs={{0,2},{1,3},{2,0},{3,1},{4,6},{5,7},{6,4},{7,5},{8,10},{9,11},{10,... | collective-permute-start | bytes 552968 | tf_op jit(solution)/shard_map/ppermute | solution.py:581
  275.6 15.0 %collective-permute-start.44 = (bf16[1,1,384,384]{3,2,1,0:T(8,128)(2,1)S(1)}, bf16[1,1,384,384]{3,2,1,0:T(8,128)(2,1)S(1)}, u32[]{:S(2)}, u32[]{:S(2)}) collective-permute-start(bf16[1,1,384,384]{3,2,1,0:T(8,128)(2,1)S(1)} %get-tuple-element.469), channel_id=1, source_target_pairs={{0,16},{4,20},{8,24},{12,28},{16,0},{20,4},{24,8},{28,12},{1,17},{... | collective-permute-start | bytes 884744 | tf_op jit(solution)/shard_map/ppermute | solution.py:577
  276.5 14.0 %collective-permute-start.45 = (bf16[1,1,384,384]{3,2,1,0:T(8,128)(2,1)S(1)}, bf16[1,1,384,384]{3,2,1,0:T(8,128)(2,1)S(1)}, u32[]{:S(2)}, u32[]{:S(2)}) collective-permute-start(bf16[1,1,384,384]{3,2,1,0:T(8,128)(2,1)S(1)} %get-tuple-element.470), channel_id=1, source_target_pairs={{0,8},{4,12},{8,0},{12,4},{16,24},{20,28},{24,16},{28,20},{1,9},{5... | collective-permute-start | bytes 884744 | tf_op jit(solution)/shard_map/ppermute | solution.py:577
  286.1 3.8 collective-permute-start.39
  286.1 13.9 %collective-permute-start.43 = (bf16[2,1,120,768]{3,2,1,0:T(8,128)(2,1)S(1)}, bf16[2,1,120,768]{3,2,1,0:T(8,128)(2,1)S(1)}, u32[]{:S(2)}, u32[]{:S(2)}) collective-permute-start(bf16[2,1,120,768]{3,2,1,0:T(8,128)(2,1)S(1)} %maximum_select_fusion.10), channel_id=1, source_target_pairs={{0,1},{1,0},{2,3},{3,2},{4,5},{5,4},{6,7},{7,6},{8,9},{9,8},{10,11... | collective-permute-start | bytes 1105928 | tf_op jit(solution)/shard_map/ppermute | solution.py:581
  290.8 13.0 %collective-permute-start.49 = (bf16[2,1,384,384]{3,2,1,0:T(8,128)(2,1)S(1)}, bf16[2,1,384,384]{3,2,1,0:T(8,128)(2,1)S(1)}, u32[]{:S(2)}, u32[]{:S(2)}) collective-permute-start(bf16[2,1,384,384]{3,2,1,0:T(8,128)(2,1)S(1)} %maximum_select_fusion.8), channel_id=1, source_target_pairs={{0,8},{4,12},{8,0},{12,4},{16,24},{20,28},{24,16},{28,20},{1,9},{5... | collective-permute-start | bytes 1769480 | tf_op jit(solution)/shard_map/ppermute | solution.py:577
  290.9 12.9 %collective-permute-start.50 = (bf16[1,2,384,384]{3,2,1,0:T(8,128)(2,1)S(1)}, bf16[1,2,384,384]{3,2,1,0:T(8,128)(2,1)S(1)}, u32[]{:S(2)}, u32[]{:S(2)}) collective-permute-start(bf16[1,2,384,384]{3,2,1,0:T(8,128)(2,1)S(1)} %maximum_select_fusion.9), channel_id=1, source_target_pairs={{0,16},{4,20},{8,24},{12,28},{16,0},{20,4},{24,8},{28,12},{1,17},{... | collective-permute-start | bytes 1769480 | tf_op jit(solution)/shard_map/ppermute | solution.py:577
  292.3 7.9 %collective-permute-start.42 = (f32[12,768]{1,0:T(8,128)S(1)}, f32[12,768]{1,0:T(8,128)S(1)}, u32[]{:S(2)}, u32[]{:S(2)}) collective-permute-start(f32[12,768]{1,0:T(8,128)S(1)} %fusion.6), channel_id=1, source_target_pairs={{0,2},{1,3},{2,0},{3,1},{4,6},{5,7},{6,4},{7,5},{8,10},{9,11},{10,... | collective-permute-start | bytes 110600 | tf_op jit(solution)/shard_map/ppermute | solution.py:581
  300.2 12.9 %collective-permute-start.47 = (bf16[1,1,480,384]{3,2,1,0:T(8,128)(2,1)S(1)}, bf16[1,1,480,384]{3,2,1,0:T(8,128)(2,1)S(1)}, u32[]{:S(2)}, u32[]{:S(2)}) collective-permute-start(bf16[1,1,480,384]{3,2,1,0:T(8,128)(2,1)S(1)} %get-tuple-element.482), channel_id=1, source_target_pairs={{0,16},{4,20},{8,24},{12,28},{16,0},{20,4},{24,8},{28,12},{1,17},{... | collective-permute-start | bytes 1105928 | tf_op jit(solution)/shard_map/ppermute | solution.py:577
  300.3 15.0 %collective-permute-start.48 = (bf16[1,1,480,384]{3,2,1,0:T(8,128)(2,1)S(1)}, bf16[1,1,480,384]{3,2,1,0:T(8,128)(2,1)S(1)}, u32[]{:S(2)}, u32[]{:S(2)}) collective-permute-start(bf16[1,1,480,384]{3,2,1,0:T(8,128)(2,1)S(1)} %get-tuple-element.483), channel_id=1, source_target_pairs={{0,8},{4,12},{8,0},{12,4},{16,24},{20,28},{24,16},{28,20},{1,9},{5... | collective-permute-start | bytes 1105928 | tf_op jit(solution)/shard_map/ppermute | solution.py:577
  304.3 17.0 %collective-permute-start.54 = (bf16[4,384,384]{2,1,0:T(8,128)(2,1)S(1)}, bf16[4,384,384]{2,1,0:T(8,128)(2,1)S(1)}, u32[]{:S(2)}, u32[]{:S(2)}) collective-permute-start(bf16[4,384,384]{2,1,0:T(8,128)(2,1)S(1)} %bitcast.49), channel_id=1, source_target_pairs={{0,4},{4,0},{8,12},{12,8},{16,20},{20,16},{24,28},{28,24},{1,5},{5... | collective-permute-start | bytes 3538952 | tf_op jit(solution)/shard_map/ppermute | solution.py:577
  313.0 8.3 %collective-permute-start.55 = (bf16[4,384,384]{2,1,0:T(8,128)(2,1)S(1)}, bf16[4,384,384]{2,1,0:T(8,128)(2,1)}, u32[]{:S(2)}, u32[]{:S(2)}) collective-permute-start(bf16[4,384,384]{2,1,0:T(8,128)(2,1)S(1)} %bitcast.51), channel_id=1, source_target_pairs={{0,4},{4,0},{8,12},{12,8},{16,20},{20,16},{24,28},{28,24},{1,5},{5... | collective-permute-start | bytes 3538952 | tf_op jit(solution)/shard_map/ppermute | solution.py:577
  315.6 15.0 %copy-start.11 = (bf16[1,2,480,384]{3,2,1,0:T(8,128)(2,1)}, bf16[1,2,480,384]{3,2,1,0:T(8,128)(2,1)S(1)}, u32[]{:S(2)}) copy-start(bf16[1,2,480,384]{3,2,1,0:T(8,128)(2,1)S(1)} %maximum_select_fusion.6) | copy-start | bytes 2211844
  315.7 21.6 %collective-permute-start.52 = (bf16[2,1,480,384]{3,2,1,0:T(8,128)(2,1)S(1)}, bf16[2,1,480,384]{3,2,1,0:T(8,128)(2,1)S(1)}, u32[]{:S(2)}, u32[]{:S(2)}) collective-permute-start(bf16[2,1,480,384]{3,2,1,0:T(8,128)(2,1)S(1)} %maximum_select_fusion.5), channel_id=1, source_target_pairs={{0,8},{4,12},{8,0},{12,4},{16,24},{20,28},{24,16},{28,20},{1,9},{5... | collective-permute-start | bytes 2211848 | tf_op jit(solution)/shard_map/ppermute | solution.py:577
  316.5 22.8 %collective-permute-start.53 = (bf16[1,2,480,384]{3,2,1,0:T(8,128)(2,1)S(1)}, bf16[1,2,480,384]{3,2,1,0:T(8,128)(2,1)}, u32[]{:S(2)}, u32[]{:S(2)}) collective-permute-start(bf16[1,2,480,384]{3,2,1,0:T(8,128)(2,1)S(1)} %maximum_select_fusion.6), channel_id=1, source_target_pairs={{0,16},{4,20},{8,24},{12,28},{16,0},{20,4},{24,8},{28,12},{1,17},{... | collective-permute-start | bytes 2211848 | tf_op jit(solution)/shard_map/ppermute | solution.py:577
  317.0 4.3 %collective-permute-start.46 = (f32[12,768]{1,0:T(8,128)S(1)}, f32[12,768]{1,0:T(8,128)S(1)}, u32[]{:S(2)}, u32[]{:S(2)}) collective-permute-start(f32[12,768]{1,0:T(8,128)S(1)} %add.188), channel_id=1, source_target_pairs={{0,4},{4,0},{8,12},{12,8},{16,20},{20,16},{24,28},{28,24},{1,5},{5... | collective-permute-start | bytes 110600 | tf_op jit(solution)/shard_map/ppermute | solution.py:577
  343.1 38.9 %copy-start.2 = (bf16[2,2,480,384]{3,2,1,0:T(8,128)(2,1)}, bf16[2,2,480,384]{3,2,1,0:T(8,128)(2,1)S(1)}, u32[]{:S(2)}) copy-start(bf16[2,2,480,384]{3,2,1,0:T(8,128)(2,1)S(1)} %maximum_select_fusion.1) | copy-start | bytes 4423684
  343.2 37.7 %copy-start.20 = (f32[432,768]{1,0:T(8,128)S(1)}, f32[432,768]{1,0:T(8,128)}, u32[]{:S(2)}) copy-start(f32[432,768]{1,0:T(8,128)} %get-tuple-element.450) | copy-start | bytes 3981316
  343.2 45.8 %collective-permute-start.57 = (bf16[4,480,384]{2,1,0:T(8,128)(2,1)S(1)}, bf16[4,480,384]{2,1,0:T(8,128)(2,1)}, u32[]{:S(2)}, u32[]{:S(2)}) collective-permute-start(bf16[4,480,384]{2,1,0:T(8,128)(2,1)S(1)} %bitcast.45), channel_id=1, source_target_pairs={{0,4},{4,0},{8,12},{12,8},{16,20},{20,16},{24,28},{28,24},{1,5},{5... | collective-permute-start | bytes 4423688 | tf_op jit(solution)/shard_map/ppermute | solution.py:577
  346.5 42.4 %collective-permute-start.58 = (bf16[4,480,384]{2,1,0:T(8,128)(2,1)S(1)}, bf16[4,480,384]{2,1,0:T(8,128)(2,1)}, u32[]{:S(2)}, u32[]{:S(2)}) collective-permute-start(bf16[4,480,384]{2,1,0:T(8,128)(2,1)S(1)} %bitcast.47), channel_id=1, source_target_pairs={{0,4},{4,0},{8,12},{12,8},{16,20},{20,16},{24,28},{28,24},{1,5},{5... | collective-permute-start | bytes 4423688 | tf_op jit(solution)/shard_map/ppermute | solution.py:577
  346.6 27.1 %collective-permute-start.18 = (bf16[432,768]{1,0:T(8,128)(2,1)S(1)}, bf16[432,768]{1,0:T(8,128)(2,1)S(1)}, u32[]{:S(2)}, u32[]{:S(2)}) collective-permute-start(bf16[432,768]{1,0:T(8,128)(2,1)S(1)} %copy-done.27), channel_id=1, source_target_pairs={{2,4},{3,5},{4,2},{5,3},{10,12},{11,13},{12,10},{13,11},{18,20},{1... | collective-permute-start | bytes 1990664 | tf_op jit(solution)/shard_map/ppermute | solution.py:594
  349.5 31.3 %collective-permute-start.38 = (bf16[432,768]{1,0:T(8,128)(2,1)S(1)}, bf16[432,768]{1,0:T(8,128)(2,1)S(1)}, u32[]{:S(2)}, u32[]{:S(2)}) collective-permute-start(bf16[432,768]{1,0:T(8,128)(2,1)S(1)} %copy-done.40), channel_id=1, source_target_pairs={{2,4},{3,5},{4,2},{5,3},{10,12},{11,13},{12,10},{13,11},{18,20},{1... | collective-permute-start | bytes 1990664 | tf_op jit(solution)/shard_map/ppermute | solution.py:594
  353.1 3.3 collective-permute-start.51
  356.4 18.2 %collective-permute-start.56 = (f32[12,768]{1,0:T(8,128)S(1)}, f32[12,768]{1,0:T(8,128)S(1)}, u32[]{:S(2)}, u32[]{:S(2)}) collective-permute-start(f32[12,768]{1,0:T(8,128)S(1)} %add.190), channel_id=1, source_target_pairs={{0,16},{4,20},{8,24},{12,28},{16,0},{20,4},{24,8},{28,12},{1,17},{... | collective-permute-start | bytes 110600 | tf_op jit(solution)/shard_map/ppermute | solution.py:577
  (37 other events, 143.2 us)
Sparse Core Ops, SparseCore 0:
  275.2 74.9 all-gather.2

commit v4 on v3

--- a/solution.py
+++ b/solution.py
@@ -20,6 +20,7 @@
 LANES = 128
 VMEM = pltpu.VMEM
 QUICK = pl.CostEstimate(flops=1, bytes_accessed=1, transcendentals=0)
+LONG = pl.CostEstimate(flops=20_000_000_000, bytes_accessed=60_000_000, transcendentals=0)
 
 
 def dot(left, right):
@@ -114,7 +115,7 @@
         in_specs=[pl.BlockSpec(memory_space=VMEM)] * 10,
         out_specs=[pl.BlockSpec(memory_space=VMEM)] * len(outs),
         compiler_params=params(),
-        cost_estimate=QUICK,
+        cost_estimate=LONG,
         name="project",
     )(*x_blocks, gain, shift, w, wt, bias, bias_col)
 
@@ -175,7 +176,7 @@
         out_specs=[whole(rows, WIDTH)] * MEMBERS + [per_head(HD, padded), per_head(1, padded)],
         scratch_shapes=[VMEM((padded, HD), BF16), VMEM((total, TILE), F32), VMEM((total, TILE), F32)],
         compiler_params=params(),
-        cost_estimate=QUICK,
+        cost_estimate=LONG,
         name="attend",
     )(qa, ka, vt)
     return low, turned, logs
@@ -254,14 +255,14 @@
             VMEM((total, HD), F32),
         ],
         compiler_params=params(),
-        cost_estimate=QUICK,
+        cost_estimate=LONG,
         name="attend_back",
     )(qa, ka, va, qn, kt, turned, logs, *grads)
 
 
-def unproject_kernel(*refs):
+def unproject_kernel(where, *refs):
     columns, normed, w = refs[:9], refs[9], refs[10]
-    n0, n1, n2, n3, first, second, sums, joint = refs[11:]
+    n0, n1, n2, n3, a_send, a_keep, b_send, b_keep, sums, joint, grad = refs[11:]
     rows = n0.shape[0]
     for s in range(3):
         for h in range(LOCAL_HEADS):
@@ -269,31 +270,46 @@
             joint[:, at : at + HD] = columns[3 * h + s][...]
     for d, out in enumerate((n0, n1, n2, n3)):
         out[...] = dot_nt(joint[d * rows : (d + 1) * rows, :], w[...]).astype(BF16)
-    grad = dot_tn(normed[...], joint[...]).astype(BF16)
-    pieces, each, _ = first.shape
-    for i in range(pieces):
-        first[i] = grad[2 * i * each : (2 * i + 1) * each]
-        second[i] = grad[(2 * i + 1) * each : (2 * i + 2) * each]
-    sums[...] = jnp.sum(joint[...].astype(F32), axis=0, keepdims=True)
-
-
-def unproject(columns, normed, w, pieces):
+    whole_grad = dot_tn(joint[...], normed[...])
+    count, each, model = grad.shape
+    for i in range(count):
+        grad[i] = whole_grad[i * each : (i + 1) * each]
+    pieces = count // 2
+    for r in range(pieces):
+        for p in range(2):
+            part = grad[(r ^ where[1]) * 2 + (p ^ (where[2] // 2))].astype(BF16)
+            out = (a_keep, a_send)[r % 2]
+            out[r // 2, p] = part[:, : model // 2]
+            out = (b_keep, b_send)[2 * r // pieces]
+            out[r % (pieces // 2), p] = part[:, model // 2 :]
+    total = jnp.sum(joint[...].astype(F32), axis=0, keepdims=True)
+    sums[...] = jnp.zeros_like(sums)
+    for m in range(MEMBERS):
+
+        @pl.when(2 * where[0] + where[2] % 2 == m)
+        def _(m=m):
+            sums[0:1, m * WIDTH : (m + 1) * WIDTH] = total[:, :WIDTH]
+            sums[1:2, m * WIDTH : (m + 1) * WIDTH] = total[:, 2 * WIDTH :]
+
+
+def unproject(where, columns, normed, w, pieces):
     total, model = normed.shape
     rows = total // MEMBERS
     width = 3 * WIDTH
+    each = width // pieces // 2
     shaped = jax.ShapeDtypeStruct
     outs = [shaped((rows, model), BF16)] * MEMBERS
-    outs += [shaped((pieces, model // pieces // 2, width), BF16)] * 2 + [shaped((1, width), F32)]
+    outs += [shaped((pieces // 2, 2, each, model // 2), BF16)] * 4 + [shaped((2, model), F32)]
     return pl.pallas_call(
         unproject_kernel,
         out_shape=outs,
-        in_specs=[pl.BlockSpec(memory_space=VMEM)] * 11,
+        in_specs=[pl.BlockSpec(memory_space=pltpu.SMEM)] + [pl.BlockSpec(memory_space=VMEM)] * 11,
         out_specs=[pl.BlockSpec(memory_space=VMEM)] * len(outs),
-        scratch_shapes=[VMEM((total, width), BF16)],
+        scratch_shapes=[VMEM((total, width), BF16), VMEM((2 * pieces, each, model), F32)],
         compiler_params=params(),
-        cost_estimate=QUICK,
+        cost_estimate=LONG,
         name="unproject",
-    )(*columns, normed, w)
+    )(where, *columns, normed, w)
 
 
 def close_kernel(x, p0, p1, gain, hidden, grad, low, vectors):
@@ -319,7 +335,7 @@
         in_specs=[pl.BlockSpec(memory_space=VMEM)] * 5,
         out_specs=[pl.BlockSpec(memory_space=VMEM)] * 3,
         compiler_params=params(),
-        cost_estimate=QUICK,
+        cost_estimate=LONG,
         name="close",
     )(x, *parts, gain, hidden)
 
@@ -363,15 +379,18 @@
     grad_up_bias[0] = jnp.sum(grad_gate.astype(F32), axis=0, keepdims=True)
     of_down = dot_tn(active, low).astype(BF16)
     of_up = dot_tn(normed[...], grad_gate).astype(BF16)
+    few = each // MEMBERS
     for i in range(2 * half):
 
         @pl.when(step == i)
         def _(i=i):
             down_held, rest_held = (down_send, rest_send) if i < half else (down_keep, rest_keep)
             for j in range(share):
-                at = (i % half) * share + j
-                down_held[at] = of_down[j * each : (j + 1) * each]
-                rest_held[at, :each, :] = of_up[j * each : (j + 1) * each]
+                piece = ((i % half) * share + j) ^ side[1]
+                for z in range(MEMBERS):
+                    at = j * each + z * few
+                    down_held[piece, z ^ side[2]] = of_down[at : at + few]
+                    rest_held[piece, z ^ side[2], :few, :] = of_up[at : at + few]
 
     @pl.when(step == last)
     def _():
@@ -389,17 +408,19 @@
         vectors[2:3, :] = jnp.sum(branch.astype(F32), axis=0, keepdims=True)
         parts = (a0, a1, a2, a3)
         count = pieces // 2
-        few = WIDTH // count
+        some = WIDTH // count // MEMBERS
         for e, given in enumerate((g0, g1, g2, g3)):
             given[...] = dot_nt(branch, wo[e]).astype(BF16)
             held = rest_keep if e < 2 else rest_send
-            place = (side[1] ^ (e & 1)) * count
+            place = ((side[2] % 2) ^ (e & 1)) * count
             of_out = dot_tn(parts[e][...], branch).astype(BF16)
             for j in range(count):
-                held[place + j, each:, :] = of_out[j * few : (j + 1) * few]
-
-
-def middle(core, near, pieces, x, attended, wo, out_bias, gain, shift, cot, down_bias, up, up_bias, down):
+                for z in range(MEMBERS):
+                    at = (j * MEMBERS + z) * some
+                    held[(place + j) ^ side[1], z ^ side[2], few:, :] = of_out[at : at + some]
+
+
+def middle(where, pieces, x, attended, wo, out_bias, gain, shift, cot, down_bias, up, up_bias, down):
     rows, model = cot.shape
     blocks = up.shape[1] // model
     half = blocks // 2
@@ -408,9 +429,9 @@
         return lax.rem(i, half) + half * jnp.where(i < half, 1 - side[0], side[0])
 
     whole_s = lambda *shape: pl.BlockSpec(shape, lambda i, side: (0,) * len(shape))
-    each = half * model // pieces
-    held = (pieces, each, model)
-    rest = (pieces, each + 2 * WIDTH // pieces, model)
+    each = half * model // pieces // MEMBERS
+    held = (pieces, MEMBERS, each, model)
+    rest = (pieces, MEMBERS, each + 2 * WIDTH // pieces // MEMBERS, model)
     shaped = jax.ShapeDtypeStruct
     outs = [
         (shaped((rows, model), BF16), whole_s(rows, model)),
@@ -450,126 +471,249 @@
             ],
         ),
         compiler_params=params(),
-        cost_estimate=QUICK,
+        cost_estimate=LONG,
         name="middle",
     )(
-        jnp.stack([core, near]).astype(jnp.int32),
+        where,
         x, *attended, wo, out_bias, gain, shift, cot, down_bias,
         up, up_bias.reshape(blocks, 1, model), down,
     )
 
 
-def place_down_kernel(side, a0, b0, a1, b1, out):
-    lanes = a0.shape[2]
-
-    @pl.when(pl.program_id(0) == 0)
-    def _():
-        out[:, :lanes] = a0[0].astype(F32)
-        out[:, lanes:] = b0[0].astype(F32)
-
-    @pl.when(pl.program_id(0) == 1)
-    def _():
-        out[:, :lanes] = a1[0].astype(F32)
-        out[:, lanes:] = b1[0].astype(F32)
-
-
-def place_rest_kernel(side, a0, b0, a1, b1, up, out):
-    lanes = a0.shape[2]
-    each = up.shape[0]
-
-    @pl.when(pl.program_id(0) == 0)
-    def _():
-        for at, part in ((0, a0), (lanes, b0)):
-            up[:, at : at + lanes] = part[0, :each, :].astype(F32)
-            out[:, at : at + lanes] = part[0, each:, :].astype(F32)
-
-    @pl.when(pl.program_id(0) == 1)
-    def _():
-        for at, part in ((0, a1), (lanes, b1)):
-            up[:, at : at + lanes] = part[0, :each, :].astype(F32)
-            out[:, at : at + lanes] = part[0, each:, :].astype(F32)
-
-
-def placed(kernel, core, parts, outs):
-    pieces, rows, lanes = parts[0].shape
-    first = pl.BlockSpec((1, rows, lanes), lambda n, i, side: (jnp.where(n == 0, i, pieces - 1), 0, 0))
-    second = pl.BlockSpec((1, rows, lanes), lambda n, i, side: (jnp.where(n == 0, 0, i), 0, 0))
+def reversed_bits(index, count):
+    bits = count.bit_length() - 1
+    total = 0
+    for bit in range(bits):
+        total = total | (((index >> bit) & 1) << (bits - 1 - bit))
+    return total
+
+
+def streamed(steps):
+    for ins, _, _ in steps:
+        for copy in ins:
+            copy.start()
+    for ins, compute, outs in steps:
+        for copy in ins:
+            copy.wait()
+        compute()
+        for copy in outs:
+            copy.start()
+    for _, _, outs in steps:
+        for copy in outs:
+            copy.wait()
+
+
+def place_kernel(where, a0, b0, a1, b1, *refs):
+    pieces, _, few, lanes = a0.shape
+    count = (len(refs) - 2) // 2
+    outs, held_in, held, (sem_in, sem_out) = refs[:count], refs[count], refs[count + 1 : -2], refs[-2:]
+    model = 2 * lanes
+    if count == 1:
+        each = few * MEMBERS
+        cuts = [(0, few)]
+    else:
+        each = outs[1].shape[0] // 2 // pieces
+        cuts = [(0, few - each // MEMBERS), (few - each // MEMBERS, each // MEMBERS)]
+    steps = []
+    for n, parts in enumerate(((a0, b0), (a1, b1))):
+        half = n ^ where[0]
+        for r in range(pieces):
+            slot = n * pieces + r
+            piece = r ^ where[1]
+            ins = [
+                pltpu.make_async_copy(part.at[at], held_in.at[slot, i], sem_in.at[slot, i])
+                for i, (part, at) in enumerate(zip(parts, (reversed_bits(r, pieces), r)))
+            ]
+
+            def compute(slot=slot):
+                for z in range(MEMBERS):
+                    given = reversed_bits(z ^ where[2], MEMBERS)
+                    for i in range(2):
+                        for out, (start, size) in zip(held, cuts):
+                            value = held_in[slot, i, given, start : start + size, :]
+                            out[slot, z * size : (z + 1) * size, i * lanes : (i + 1) * lanes] = value.astype(F32)
+
+            places = []
+            for out, (_, size) in zip(outs, cuts):
+                rows = size * MEMBERS
+                if out.shape[1] == model:
+                    places.append(out.at[pl.ds((half * pieces + piece) * rows, rows)])
+                else:
+                    share = model // rows
+                    column = half * (out.shape[1] // model // 2) + piece // share
+                    places.append(
+                        out.at[
+                            pl.ds(lax.rem(piece, share) * rows, rows),
+                            pl.ds(pl.multiple_of(column * model, model), model),
+                        ]
+                    )
+            sends = [
+                pltpu.make_async_copy(given.at[slot], place, sem_out.at[slot, i])
+                for i, (given, place) in enumerate(zip(held, places))
+            ]
+            steps.append((ins, compute, sends))
+    streamed(steps)
+
+
+def placed(where, parts, shapes):
+    pieces, _, few, lanes = parts[0].shape
+    count = len(shapes)
+    sizes = [shape[0] * shape[1] // (2 * lanes) // 2 // pieces for shape in shapes]
+    return pl.pallas_call(
+        place_kernel,
+        out_shape=[jax.ShapeDtypeStruct(shape, F32) for shape in shapes],
+        in_specs=[pl.BlockSpec(memory_space=pltpu.SMEM)] + [pl.BlockSpec(memory_space=pl.ANY)] * 4,
+        out_specs=[pl.BlockSpec(memory_space=pl.ANY)] * count,
+        scratch_shapes=[VMEM((2 * pieces, 2, MEMBERS, few, lanes), BF16)]
+        + [VMEM((2 * pieces, size, 2 * lanes), F32) for size in sizes]
+        + [pltpu.SemaphoreType.DMA((2 * pieces, 2)), pltpu.SemaphoreType.DMA((2 * pieces, count))],
+        compiler_params=params(),
+        cost_estimate=LONG,
+        name="placed",
+    )(where, *parts)
+
+
+def placed_down(where, parts, hidden_units):
+    return placed(where, parts, [(hidden_units, 2 * parts[0].shape[3])])
+
+
+def placed_rest(where, parts, hidden_units):
+    model = 2 * parts[0].shape[3]
+    return placed(where, parts, [(model, hidden_units), (model, model)])
+
+
+def place_in_kernel(where, a0, b0, a1, b1, out, held):
+    pieces, _, each, lanes = a0.shape
+    model = 2 * lanes
+    for half, (first, second) in enumerate(((a0, b0), (a1, b1))):
+        for r in range(pieces):
+            for z in range(MEMBERS):
+                at = reversed_bits(z, MEMBERS)
+                piece, side = r ^ where[1], z ^ where[2]
+                member = 2 * (half ^ where[0]) + side % 2
+                place = piece * 2 + side // 2
+                held[member, place, :, :lanes] = first[reversed_bits(r, pieces), at].astype(F32)
+                held[member, place, :, lanes:] = second[r, at].astype(F32)
+    for m in range(MEMBERS):
+        columns = held[m].reshape(3 * WIDTH, model)
+        for s in range(3):
+            at = s * model + m * WIDTH
+            out[:, at : at + WIDTH] = columns[s * WIDTH : (s + 1) * WIDTH].T
+
+
+def placed_in(where, parts):
+    pieces, _, rows, lanes = parts[0].shape
+    model = 2 * lanes
+    return pl.pallas_call(
+        place_in_kernel,
+        out_shape=jax.ShapeDtypeStruct((model, 3 * model), F32),
+        in_specs=[pl.BlockSpec(memory_space=pltpu.SMEM)] + [pl.BlockSpec(memory_space=VMEM)] * 4,
+        out_specs=pl.BlockSpec(memory_space=VMEM),
+        scratch_shapes=[VMEM((MEMBERS, 2 * pieces, rows, model), F32)],
+        compiler_params=params(),
+        cost_estimate=LONG,
+        name="placed_in",
+    )(where, *parts)
+
+
+def plus(first, second):
+    return (first.astype(F32) + second.astype(F32)).astype(BF16)
+
+
+def fold_core_kernel(keep, got, a_send, a_keep, b_send, b_keep, held, held_got, held_out, sem_in, sem_out):
+    pieces, _, _, lanes = keep.shape
+    steps = []
+    for p in range(pieces):
+        ins = [
+            pltpu.make_async_copy(keep.at[p], held.at[p], sem_in.at[p, 0]),
+            pltpu.make_async_copy(got.at[p], held_got.at[p], sem_in.at[p, 1]),
+        ]
+
+        def compute(p=p):
+            total = plus(held[p], held_got[p])
+            held_out[p, 0] = total[:, :, : lanes // 2]
+            held_out[p, 1] = total[:, :, lanes // 2 :]
+
+        first = (a_keep, a_send)[p % 2].at[p // 2]
+        second = (b_keep, b_send)[2 * p // pieces].at[p % (pieces // 2)]
+        outs = [
+            pltpu.make_async_copy(held_out.at[p, i], place, sem_out.at[p, i])
+            for i, place in enumerate((first, second))
+        ]
+        steps.append((ins, compute, outs))
+    streamed(steps)
+
+
+def fold_core(keep, got):
+    pieces, quarters, rows, lanes = keep.shape
+    half = (quarters, rows, lanes // 2)
+    return pl.pallas_call(
+        fold_core_kernel,
+        out_shape=[jax.ShapeDtypeStruct((pieces // 2, *half), BF16)] * 4,
+        in_specs=[pl.BlockSpec(memory_space=pl.ANY)] * 2,
+        out_specs=[pl.BlockSpec(memory_space=pl.ANY)] * 4,
+        scratch_shapes=[
+            VMEM(keep.shape, BF16),
+            VMEM(keep.shape, BF16),
+            VMEM((pieces, 2, *half), BF16),
+            pltpu.SemaphoreType.DMA((pieces, 2)),
+            pltpu.SemaphoreType.DMA((pieces, 2)),
+        ],
+        compiler_params=params(),
+        cost_estimate=QUICK,
+        name="fold_core",
+    )(keep, got)
+
+
+def in_vmem(kernel, outs, *values, name):
     return pl.pallas_call(
         kernel,
-        out_shape=[jax.ShapeDtypeStruct(shape, F32) for shape, _, _ in outs],
-        grid_spec=pltpu.PrefetchScalarGridSpec(
-            num_scalar_prefetch=1,
-            grid=(2, pieces),
-            in_specs=[first, first, second, second],
-            out_specs=[
-                pl.BlockSpec(block, lambda n, i, side, place=place: place(lax.rem(n + side[0], 2), i))
-                for _, block, place in outs
-            ],
-        ),
+        out_shape=outs,
+        in_specs=[pl.BlockSpec(memory_space=VMEM)] * len(values),
+        out_specs=[pl.BlockSpec(memory_space=VMEM)] * len(outs),
         compiler_params=params(),
         cost_estimate=QUICK,
-        name="placed",
-    )(core, *parts)
-
-
-def placed_down(core, parts, hidden_units):
-    pieces, each, lanes = parts[0].shape
-    (down,) = placed(
-        place_down_kernel,
-        core,
-        parts,
-        [((hidden_units, 2 * lanes), (each, 2 * lanes), lambda k, i: (k * pieces + i, 0))],
-    )
-    return down
-
-
-def placed_rest(core, parts, hidden_units):
-    pieces, rows, lanes = parts[0].shape
-    model = 2 * lanes
-    each = hidden_units // 2 // pieces
-    few = rows - each
-    share = model // each
-    half = hidden_units // model // 2
-    return placed(
-        place_rest_kernel,
-        core,
-        parts,
-        [
-            ((model, hidden_units), (each, model), lambda k, i: (lax.rem(i, share), k * half + i // share)),
-            ((2 * pieces * few, model), (few, model), lambda k, i: (k * pieces + i, 0)),
-        ],
-    )
-
-
-def place_in_kernel(gathered, out):
-    model = out.shape[1] // 3
-    rows = gathered.shape[5]
-    for n in range(2):
-        for p in range(2):
-            here = pl.ds((2 * n + p) * rows, rows)
-            for s in range(3):
-                parts = [
-                    gathered[0, k, p, q, n, :, s * WIDTH : (s + 1) * WIDTH]
-                    for k in range(2)
-                    for q in range(2)
-                ]
-                out[here, s * model : (s + 1) * model] = jnp.concatenate(parts, axis=1).astype(F32)
-
-
-def placed_in(gathered):
-    pieces, *rest = gathered.shape
-    rows, width = rest[-2:]
-    model = width * MEMBERS // 3
-    return pl.pallas_call(
-        place_in_kernel,
-        grid=(pieces,),
-        out_shape=jax.ShapeDtypeStruct((pieces * 4 * rows, 3 * model), F32),
-        in_specs=[pl.BlockSpec((1, *rest), lambda i: (i, 0, 0, 0, 0, 0, 0))],
-        out_specs=pl.BlockSpec((4 * rows, 3 * model), lambda i: (i, 0)),
-        compiler_params=params(),
-        cost_estimate=QUICK,
-        name="placed_in",
-    )(gathered)
+        name=name,
+    )(*values)
+
+
+def fold_planes_kernel(ak, ag, bk, bg, a_send, a_keep, b_send, b_keep):
+    count = ak.shape[0]
+    for r in range(count):
+        out = (a_keep, a_send)[r % 2]
+        out[r // 2] = plus(ak[r], ag[r])
+        out = (b_keep, b_send)[2 * r // count]
+        out[r % (count // 2)] = plus(bk[r], bg[r])
+
+
+def fold_last_kernel(ak, ag, bk, bg, send, keep):
+    quarters = ak.shape[1]
+    lanes = ak.shape[3]
+    for z in range(quarters):
+        out = (keep, send)[z % 2]
+        out[z // 2, :, :lanes] = plus(ak[0, z], ag[0, z])
+        out[z // 2, :, lanes:] = plus(bk[0, z], bg[0, z])
+
+
+def fold_planes(ak, ag, bk, bg):
+    count, quarters, rows, lanes = ak.shape
+    if count > 1:
+        outs = [jax.ShapeDtypeStruct((count // 2, quarters, rows, lanes), BF16)] * 4
+        return in_vmem(fold_planes_kernel, outs, ak, ag, bk, bg, name="fold_planes")
+    outs = [jax.ShapeDtypeStruct((quarters // 2, rows, 2 * lanes), BF16)] * 2
+    return in_vmem(fold_last_kernel, outs, ak, ag, bk, bg, name="fold_last")
+
+
+def fold_quarters_kernel(keep, got, *outs):
+    for z in range(keep.shape[0]):
+        out = outs[len(outs) - 1 - z]
+        out[...] = plus(keep[z], got[z])
+
+
+def fold_quarters(keep, got):
+    count, rows, lanes = keep.shape
+    outs = [jax.ShapeDtypeStruct((rows, lanes), BF16)] * count
+    return in_vmem(fold_quarters_kernel, outs, keep, got, name="fold_quarters")
 
 
 def over_cube(value, bit):
@@ -601,88 +745,64 @@
     return [parts[0], near, core, over_cube(far, 0)]
 
 
-def half_of(rows, which, axis=0):
-    size = rows.shape[axis] // 2
-    return lax.dynamic_slice_in_dim(rows, which * size, size, axis)
-
-
-def added(first, second):
-    return (first.astype(F32) + second.astype(F32)).astype(BF16)
-
-
-def halved(rows, flag, send, axis=0):
-    got = send(half_of(rows, 1 - flag, axis))
-    return added(half_of(rows, flag, axis), got)
-
-
-def joined(own, got, flag, axis=0):
-    return jnp.where(
-        flag == 0,
-        jnp.concatenate([own, got], axis),
-        jnp.concatenate([got, own], axis),
-    )
-
-
 def cube_bits():
     return list(range(1, lax.axis_size("cube").bit_length() - 1))
 
 
-def flag_of(index, bit):
-    return (index >> bit) & 1
-
-
-def summing(keep, send, cube, blk):
-    (got,) = yield [(send, lambda v: over_cube(v, 0))]
-    bits = cube_bits()
-    pieces, rows, lanes = keep.shape
-    total = added(keep, got).reshape((2,) * len(bits) + (rows, lanes))
-    parts = [total[..., : lanes // 2], total[..., lanes // 2 :]]
-    parts = yield from scattered(parts, cube)
-    total = jnp.concatenate([p.reshape(2, 2, rows // MEMBERS, lanes // 2) for p in parts], axis=3)
+def by_cube(bit):
+    return functools.partial(over_cube, bit=bit)
+
+
+def by_blk(bit):
+    return functools.partial(over_blk, bit=bit)
+
+
+def scattering(a_send, a_keep, b_send, b_keep):
+    for low, high in zip(cube_bits(), cube_bits()[::-1]):
+        a_got, b_got = yield [(a_send, by_cube(low)), (b_send, by_cube(high))]
+        *folded, = fold_planes(a_keep, a_got, b_keep, b_got)
+        if len(folded) == 2:
+            return folded
+        a_send, a_keep, b_send, b_keep = folded
+
+
+def spreading(shard):
+    (got,) = yield [(shard, by_blk(1))]
+    both = jnp.stack([shard, got])
+    (got,) = yield [(both, by_blk(0))]
+    both = jnp.concatenate([both, got])[None]
+    lanes = both.shape[3] // 2
+    a_part, b_part = both[..., :lanes], both[..., lanes:]
+    for low, high in zip(cube_bits(), cube_bits()[::-1]):
+        a_got, b_got = yield [(a_part, by_cube(high)), (b_part, by_cube(low))]
+        a_part, b_part = jnp.concatenate([a_part, a_got]), jnp.concatenate([b_part, b_got])
+    got = yield [(a_part, by_cube(0)), (b_part, by_cube(0))]
+    return [a_part, b_part, *got]
+
+
+def summing(keep, send):
+    (got,) = yield [(send, by_cube(0))]
+    send, keep = yield from scattering(*fold_core(keep, got))
+    (got,) = yield [(send, by_blk(0))]
+    send, keep = fold_quarters(keep, got)
+    (got,) = yield [(send, by_blk(1))]
+    return (yield from spreading(plus(keep, got)))
+
+
+def summing_columns(parts):
+    send, keep = yield from scattering(*parts)
+    (got,) = yield [(send, by_blk(1))]
+    return (yield from spreading(plus(keep[0], got[0])))
+
+
+def summing_vectors(rows):
     for bit in range(2):
-        flag = flag_of(blk, bit)
-        (got,) = yield [(half_of(total, 1 - flag, 1 - bit), functools.partial(over_blk, bit=bit))]
-        total = added(half_of(total, flag, 1 - bit), got)
-    for bit in (1, 0):
-        (got,) = yield [(total, functools.partial(over_blk, bit=bit))]
-        total = joined(total, got, flag_of(blk, bit), 1 - bit)
-    total = total.reshape((1,) * len(bits) + (rows, lanes))
-    parts = [total[..., : lanes // 2], total[..., lanes // 2 :]]
-    for steps in zip(bits[::-1], bits):
-        got = yield [(part, functools.partial(over_cube, bit=bit)) for part, bit in zip(parts, steps)]
-        parts = [
-            joined(part, other, flag_of(cube, bit), len(bits) - bit)
-            for part, other, bit in zip(parts, got, steps)
-        ]
-    parts = [part.reshape(pieces, rows, lanes // 2) for part in parts]
-    got = yield [(part, lambda v: over_cube(v, 0)) for part in parts]
-    return parts + list(got)
-
-
-def scattered(parts, cube):
-    bits = cube_bits()
-    for steps in zip(bits, bits[::-1]):
-        flags = [flag_of(cube, bit) for bit in steps]
-        axes = [len(bits) - bit for bit in steps]
-        got = yield [
-            (half_of(part, 1 - flag, axis), functools.partial(over_cube, bit=bit))
-            for part, flag, axis, bit in zip(parts, flags, axes, steps)
-        ]
-        parts = [
-            added(half_of(part, flag, axis), other)
-            for part, flag, axis, other in zip(parts, flags, axes, got)
-        ]
-    return parts
-
-
-def summing_columns(parts, cube, blk):
-    bits = cube_bits()
-    _, rows, lanes = parts[0].shape
-    parts = yield from scattered([p.reshape((2,) * len(bits) + (rows, lanes)) for p in parts], cube)
-    total = jnp.concatenate([p.reshape(1, 2, rows // 2, lanes) for p in parts])
-    flag = flag_of(blk, 1)
-    (got,) = yield [(half_of(total, 1 - flag, 1), functools.partial(over_blk, bit=1))]
-    return added(half_of(total, flag, 1), got).reshape(2, rows // 2, lanes)
+        (got,) = yield [(rows, by_blk(bit))]
+        rows = rows + got
+    for bit in range(lax.axis_size("cube").bit_length() - 1):
+        (got,) = yield [(rows, by_cube(bit))]
+        rows = rows + got
+    return rows
 
 
 class Order:
@@ -718,16 +838,6 @@
         while self.result is None:
             self.step()
         return self.result
-
-
-def summing_vectors(rows):
-    for bit in range(2):
-        (got,) = yield [(rows, functools.partial(over_blk, bit=bit))]
-        rows = rows + got
-    for bit in range(lax.axis_size("cube").bit_length() - 1):
-        (got,) = yield [(rows, functools.partial(over_cube, bit=bit))]
-        rows = rows + got
-    return rows
 
 
 def member_columns(matrix, member, axis):
@@ -757,6 +867,7 @@
     cube, blk = lax.axis_index("cube"), lax.axis_index("blk")
     core = cube & 1
     pieces = lax.axis_size("cube") // 2
+    where = jnp.stack([core, cube >> 1, blk]).astype(jnp.int32)
     at_home = core == (blk >> 1)
     member = 2 * core + (blk & 1)
 
@@ -805,8 +916,7 @@
         *grad_attended,
         middle_vectors,
     ) = middle(
-        core,
-        blk & 1,
+        where,
         pieces,
         own,
         attended,
@@ -821,12 +931,14 @@
         down_weight,
     )
     blocks = hidden_units // model
-    order = Order(core.astype(jnp.int32)[None])
-    down_run = Running(summing(down_keep, down_send, cube, blk), order)
-    rest_run = Running(summing(rest_keep, rest_send, cube, blk), order)
-    grads_here = exchanged(grad_attended)
+    order = Order(where)
+    down_run = Running(summing(down_keep, down_send), order)
+    rest_run = Running(summing(rest_keep, rest_send), order)
+    far, near = order((over_blk(grad_attended[3], 0), over_blk(grad_attended[1], 0)))
+    core_parts = (over_cube(grad_attended[2], 0), over_cube(far, 0))
     down_run.step()
     rest_run.step()
+    grads_here = [grad_attended[0], near, *order(core_parts)]
     columns = []
 
     def back(head):
@@ -835,22 +947,28 @@
 
     back(0)
     down_run.step()
-    layer_out = moved(order(layer_here))
+    layer_moved = sent_between(order(layer_here), False, 1, 2)
     back(1)
     down_run.step()
     rest_run.step()
     back(2)
+    layer_out = jnp.where(at_home, layer_here, order(layer_moved))
     down_run.step()
     rest_run.step()
-    p0, p1, p2, p3, in_first, in_second, column_total = order(
-        unproject(order(columns), normed_low, in_columns, pieces)
+    p0, p1, p2, p3, *in_parts, biases = order(
+        unproject(where, order(columns), normed_low, in_columns, pieces)
     )
+    in_run = Running(summing_columns(in_parts), order)
     core_far, core_near = over_cube(p3, 0), over_cube(p2, 0)
-    in_run = Running(summing_columns([in_first, in_second], cube, blk), order)
     down_run.step()
-    core_far, core_near = order((core_far, core_near))
-    near_sum, own_sum = order((added(p1, core_far), added(p0, core_near)))
+    rest_run.step()
+    in_run.step()
+    near_sum, own_sum = order((plus(p1, order(core_far)), plus(p0, core_near)))
+    down_run.step()
+    in_run.step()
+    rest_run.step()
     near_got = over_blk(near_sum, 0)
+    down_run.step()
     in_run.step()
     rest_run.step()
     down_run.step()
@@ -861,35 +979,27 @@
         close(own, order([own_sum, near_got]), pre_gain, grad_hidden)
     )
     grad_moved = sent_between(grad_low, False, 1, 2)
-    column_total = column_total[0]
-    here_bias = jnp.stack([column_total[:WIDTH], column_total[2 * WIDTH :]])
-    spread_bias = lax.dynamic_update_slice_in_dim(
-        jnp.zeros((2, model), F32), here_bias, member * WIDTH, 1
+    vector_run = Running(
+        summing_vectors(
+            jnp.concatenate([grad_pre, middle_vectors, biases, grad_up_bias.reshape(blocks, model)])
+        ),
+        order,
     )
-    vectors = jnp.concatenate(
-        [grad_pre, middle_vectors, spread_bias, grad_up_bias.reshape(blocks, model)]
-    )
-    vector_run = Running(summing_vectors(vectors), order)
-    gathered = lax.all_gather(in_run.finish(), ("cube", "blk"))
+    in_run.step()
     rest_run.step()
     vector_run.step()
-    down_run.step()
+    (grad_down_weight,) = order(placed_down(order.token, down_run.finish(), hidden_units))
+    vector_run.step()
     rest_run.step()
+    in_run.step()
     vector_run.step()
-    down_run.step()
-    rest_run.step()
+    input_grad = order(jnp.where(at_home, grad_here, order(grad_moved).astype(F32)))
+    rest_sum = rest_run.finish()
     vector_run.step()
-    down_run.step()
-    (grad_down_weight,) = order([placed_down(order.token, down_run.finish(), hidden_units)])
-    rest_run.step()
+    in_run.step()
     vectors = vector_run.finish()
-    grad_moved = order(grad_moved)
-    input_grad = order(jnp.where(at_home, grad_here, grad_moved.astype(F32)))
-    gathered = order(gathered)
-    gathered = gathered.reshape((pieces, 2, 2, 2) + in_run.result.shape)
-    grad_input_weight = order(placed_in(gathered))
-    rest_sum = rest_run.finish()
-    grad_up_weight, grad_output_weight = placed_rest(order.token, rest_sum, hidden_units)
+    grad_up_weight, grad_output_weight = order(placed_rest(order.token, rest_sum, hidden_units))
+    grad_input_weight = placed_in(order.token, in_run.finish())
     return (
         layer_out[None],
         input_grad[None],

time: 413 us -> 375 us (0.908)
  Pallas kernels: 133 us -> 157 us
  other arithmetic: 38.6 us -> 18.9 us
  between operations: 15.1 us -> 1.75 us
  waiting for transfers between devices: 117 us -> 106 us
  local copies, waits for them, and re-layouts: 28.1 us -> 18.8 us
  starting transfers between devices: 72.9 us -> 65.9 us
    pallas_call x3 -> x13, Pallas kernels: 23.2 us -> 46.7 us  [the longest x8 17.7 us: in_vmem(): pl.pallas_call(kernel, out_shape=outs, in_specs=[pl.BlockSpec(memory_spac...]
    convert_element_type x21 -> x5, other arithmetic: 17.9 us -> 1.26 us  [plus(): return (first.astype(F32) + second.astype(F32)).astype(BF16)]
    ppermute x6, waiting for transfers between devices: 37.1 us -> 26.7 us  [sent_between(): lax.ppermute(value, ('cube', 'blk'), chosen_pairs(is_home, cube_flip, blk...]
    ppermute x37 -> x43, starting transfers between devices: 39 us -> 29 us  [over_cube(): lax.ppermute(value, 'cube', [(i, i ^ 1 << bit) for i in range(count)])]
    dynamic_slice x14 -> x0, local copies, waits for them, and re-layouts: 8.87 us -> none  [half_of(): return lax.dynamic_slice_in_dim(rows, which * size, size, axis)]
    select_n x13 -> x1, other arithmetic: 7.17 us -> 1.19 us  [body(): jnp.where(at_home, grad_here, order(grad_moved).astype(F32))]
    ppermute x6, starting transfers between devices: 20.4 us -> 24.9 us  [sent_between(): lax.ppermute(value, ('cube', 'blk'), chosen_pairs(is_home, cube_flip, blk...]
    concatenate x4 -> x13, other arithmetic: 2.27 us -> 6.56 us  [the longest x6 3.33 us: spreading(): jnp.concatenate([b_part, b_got])]
  transfers between devices with their start and end apart: 60 -> 67, of which waited for: 26 -> 27; matrix products, arithmetic and copies ran while one was open for 13% -> 6% of each run, Pallas kernels for 21% -> 26%
where the time goes in v4:
time: 375 us; the launch traced here: 368 us
  Pallas kernels  157 us (42%)
  waiting for transfers between devices  106 us (28%)
  starting transfers between devices  65.9 us (18%)
  other arithmetic  18.9 us (5%)
  local copies, waits for them, and re-layouts  18.8 us (5%)
    ppermute x18, waiting for transfers between devices, over_blk(): lax.ppermute(value, 'blk', [(i, i ^ 1 << bit) for i in range(MEMBERS)])  58.5 us
    pallas_call x3, Pallas kernels, attend_back(): pl.pallas_call(functools.partial(backward_kernel, head), grid=(1,), out_s...  37.5 us
    ppermute x43, starting transfers between devices, over_cube(): lax.ppermute(value, 'cube', [(i, i ^ 1 << bit) for i in range(count)])  29 us
    pallas_call x1, Pallas kernels, middle(): pl.pallas_call(middle_kernel, out_shape=[o[0] for o in outs], grid_spec=p...  27.8 us
    ppermute x6, waiting for transfers between devices, sent_between(): lax.ppermute(value, ('cube', 'blk'), chosen_pairs(is_home, cube_flip, blk...  26.7 us
    ppermute x6, starting transfers between devices, sent_between(): lax.ppermute(value, ('cube', 'blk'), chosen_pairs(is_home, cube_flip, blk...  24.9 us
    ppermute x43, waiting for transfers between devices, over_cube(): lax.ppermute(value, 'cube', [(i, i ^ 1 << bit) for i in range(count)])  20.4 us
    pallas_call x1, Pallas kernels, attend(): pl.pallas_call(forward_kernel, grid=(n,), out_shape=[jax.ShapeDtypeStruct...  20.3 us
  transfers between devices with their start and end apart: 67, of which 27 were waited for; matrix products, arithmetic and copies ran while one was open for 6% of the time, Pallas kernels for 26%

profile of v4, /device:TPU:1, one launch (start us, length us, event | category | flops | bytes accessed | tf_op | source)
XLA Modules:
  0.0 368.1 jit_solution(13144189272493079552)
XLA Ops:
  1.5 2.0 pad_maximum_fusion.10
  3.5 1.5 collective-permute-start.1
  5.0 5.6 %collective-permute-start = (bf16[448,768]{1,0:T(8,128)(2,1)}, bf16[448,768]{1,0:T(8,128)(2,1)}, u32[]{:S(2)}, u32[]{:S(2)}) collective-permute-start(bf16[448,768]{1,0:T(8,128)(2,1)} %pad_maximum_fusion.10), channel_id=1, source_target_pairs={{2,4},{3,5},{4,2},{5,3},{10,12},{11,13},{12,10},{13,11},{18,20},{1... | collective-permute-start | bytes 2064392 | tf_op jit(solution)/shard_map/ppermute | solution.py:738
  11.5 3.2 fusion.1
  15.0 1.4 constant_dynamic-slice_fusion
  16.7 1.3 pad_maximum_fusion.5.w.refs_10_
  19.3 7.6 %collective-permute-done = bf16[448,768]{1,0:T(8,128)(2,1)} collective-permute-done((bf16[448,768]{1,0:T(8,128)(2,1)}, bf16[448,768]{1,0:T(8,128)(2,1)}, u32[]{:S(2)}, u32[]{:S(2)}) %collective-permute-start) | collective-permute-done | bytes 688160 | tf_op jit(solution)/shard_map/ppermute | solution.py:738
  26.9 2.4 collective-permute-start.2
  29.3 1.3 broadcast_select_fusion.1.x0.x
  30.7 8.1 %collective-permute-done.2 = bf16[448,768]{1,0:T(8,128)(2,1)S(1)} collective-permute-done((bf16[448,768]{1,0:T(8,128)(2,1)}, bf16[448,768]{1,0:T(8,128)(2,1)S(1)}, u32[]{:S(2)}, u32[]{:S(2)}) %collective-permute-start.2) | collective-permute-done | bytes 688160 | tf_op jit(solution)/shard_map/ppermute | solution.py:738
  39.0 1.3 copy.33.wt
  41.2 11.2 %project.1 = (bf16[1728,768]{1,0:T(8,128)(2,1)}, bf16[3,128,1792]{2,1,0:T(8,128)(2,1)}, bf16[3,1728,128]{2,1,0:T(8,128)(2,1)}, bf16[3,1728,128]{2,1,0:T(8,128)(2...) custom-call(bf16[448,768]{1,0:T(8,128)(2,1)} %copy-done.12, ...), custom_call_target="tpu_custom_call" | custom-call | flops 20000000000 | bytes 60000000 | tf_op jit(solution)/shard_map/project/pallas_call | solution.py:112
  52.4 5.4 %collective-permute-start.9 = (bf16[432,768]{1,0:T(8,128)(2,1)S(1)}, bf16[432,768]{1,0:T(8,128)(2,1)S(1)}, u32[]{:S(2)}, u32[]{:S(2)}) collective-permute-start(bf16[432,768]{1,0:T(8,128)(2,1)S(1)} %bitcast.48), channel_id=1, source_target_pairs={{2,4},{3,5},{4,2},{5,3},{10,12},{11,13},{12,10},{13,11},{18,20},{1... | collective-permute-start | bytes 1990664 | tf_op jit(solution)/shard_map/ppermute | solution.py:738
  57.8 20.3 %attend.1 = (bf16[432,192]{1,0:T(8,128)(2,1)}, bf16[432,192]{1,0:T(8,128)(2,1)}, bf16[432,192]{1,0:T(8,128)(2,1)}, bf16[432,192]{1,0:T(8,128)(2,1)}, f32[3,64,1792]{2,1,0:T(8,128)}, /*index=5*/f32[3,1,1792]{2,1,0:T(1,128)}) custom-call(bf16[3,128,1792]{2,1,0:T(8,128)(2,1)} %get-tuple-element.345.qa, bf16[3,1728,128]{2,1,0:T(8,128)(2,1)} %get-tuple-element.346.ka, ...), custom_call_target="tpu_custom_call" | custom-call | flops 20000000000 | bytes 60000000 | tf_op jit(solution)/shard_map/attend/pallas_call | solution.py:167
  78.1 1.7 collective-permute-start.7
  80.5 3.7 %collective-permute-done.7 = bf16[432,192]{1,0:T(8,128)(2,1)S(1)} collective-permute-done((bf16[432,192]{1,0:T(8,128)(2,1)}, bf16[432,192]{1,0:T(8,128)(2,1)S(1)}, u32[]{:S(2)}, u32[]{:S(2)}) %collective-permute-start.7) | collective-permute-done | bytes 165920 | tf_op jit(solution)/shard_map/ppermute | solution.py:725
  85.1 1.5 collective-permute-done.5.a1
  87.4 27.8 %middle.1 = (bf16[432,768]{1,0:T(8,128)(2,1)}, bf16[4,4,96,768]{3,2,1,0:T(8,128)(2,1)}, bf16[4,4,96,768]{3,2,1,0:T(8,128)(2,1)}, bf16[4,4,120,768]{3,2,1,0:T(8,1...) custom-call(s32[3]{0:T(128)} %pad_add_fusion.side.where, ...), custom_call_target="tpu_custom_call" | custom-call | flops 20000000000 | bytes 60000000 | tf_op jit(solution)/shard_map/middle/pallas_call | solution.py:447
  117.9 5.2 %collective-permute-done.11 = bf16[432,192]{1,0:T(8,128)(2,1)} collective-permute-done((bf16[432,192]{1,0:T(8,128)(2,1)}, bf16[432,192]{1,0:T(8,128)(2,1)}, u32[]{:S(2)}, u32[]{:S(2)}) %collective-permute-start.11) | collective-permute-done | bytes 165920 | tf_op jit(solution)/shard_map/ppermute | solution.py:725
  123.1 4.7 %collective-permute-done.12.g1 = bf16[432,192]{1,0:T(8,128)(2,1)} collective-permute-done((bf16[432,192]{1,0:T(8,128)(2,1)}, bf16[432,192]{1,0:T(8,128)(2,1)}, u32[]{:S(2)}, u32[]{:S(2)}) %collective-permute-start.12) | collective-permute-done | bytes 165920 | tf_op jit(solution)/shard_map/ppermute | solution.py:725
  128.7 3.5 fold_core.2
  132.2 1.3 collective-permute-start.13
  134.7 1.6 copy-done
  136.3 4.3 %fold_core.3 = (bf16[2,4,120,384]{3,2,1,0:T(8,128)(2,1)}, bf16[2,4,120,384]{3,2,1,0:T(8,128)(2,1)}, bf16[2,4,120,384]{3,2,1,0:T(8,128)(2,1)}, bf16[2,4,120,384]{3,2,1,0:T(8,128)(2,1)}) custom-call(bf16[4,4,120,768]{3,2,1,0:T(8,128)(2,1)} %get-tuple-element.380.keep, bf16[4,4,120,768]{3,2,1,0:T(8,128)(2,1)} %copy-done), custom_call_target="tpu_custom_call" | custom-call | flops 1 | bytes 1 | tf_op jit(solution)/shard_map/fold_core/pallas_call | solution.py:650
  141.1 12.4 %attend_back.3 = (bf16[1728,64]{1,0:T(8,128)(2,1)}, bf16[1728,64]{1,0:T(8,128)(2,1)}, bf16[1728,64]{1,0:T(8,128)(2,1)}) custom-call(bf16[3,128,1792]{2,1,0:T(8,128)(2,1)} %get-tuple-element.345.qa, bf16[3,1728,128]{2,1,0:T(8,128)(2,1)} %get-tuple-element.346.ka, bf16[3,1728,128]{2,1,0:T(8,128)(2,1)} %get-tuple-element.371.va, ...), custom_call_target="tpu_custom_call" | custom-call | flops 20000000000 | bytes 60000000 | tf_op jit(solution)/shard_map/attend_back/pallas_call | solution.py:237
  154.6 2.7 fold_planes.3
  159.7 6.4 %collective-permute-start.18 = (bf16[432,768]{1,0:T(8,128)(2,1)S(1)}, bf16[432,768]{1,0:T(8,128)(2,1)S(1)}, u32[]{:S(2)}, u32[]{:S(2)}) collective-permute-start(bf16[432,768]{1,0:T(8,128)(2,1)S(1)} %copy-done.15), channel_id=1, source_target_pairs={{2,4},{3,5},{4,2},{5,3},{10,12},{11,13},{12,10},{13,11},{18,20},{1... | collective-permute-start | bytes 1990664 | tf_op jit(solution)/shard_map/ppermute | solution.py:738
  166.1 12.6 %attend_back.4 = (bf16[1728,64]{1,0:T(8,128)(2,1)}, bf16[1728,64]{1,0:T(8,128)(2,1)}, bf16[1728,64]{1,0:T(8,128)(2,1)}) custom-call(bf16[3,128,1792]{2,1,0:T(8,128)(2,1)} %get-tuple-element.345.qa, bf16[3,1728,128]{2,1,0:T(8,128)(2,1)} %get-tuple-element.346.ka, bf16[3,1728,128]{2,1,0:T(8,128)(2,1)} %get-tuple-element.371.va, ...), custom_call_target="tpu_custom_call" | custom-call | flops 20000000000 | bytes 60000000 | tf_op jit(solution)/shard_map/attend_back/pallas_call | solution.py:237
  179.6 2.1 fold_last.3
  181.7 1.5 collective-permute-start.25
  184.3 3.0 fold_planes.4
  187.7 12.4 %attend_back.5 = (bf16[1728,64]{1,0:T(8,128)(2,1)}, bf16[1728,64]{1,0:T(8,128)(2,1)}, bf16[1728,64]{1,0:T(8,128)(2,1)}) custom-call(bf16[3,128,1792]{2,1,0:T(8,128)(2,1)} %get-tuple-element.345.qa, bf16[3,1728,128]{2,1,0:T(8,128)(2,1)} %get-tuple-element.346.ka, bf16[3,1728,128]{2,1,0:T(8,128)(2,1)} %get-tuple-element.371.va, ...), custom_call_target="tpu_custom_call" | custom-call | flops 20000000000 | bytes 60000000 | tf_op jit(solution)/shard_map/attend_back/pallas_call | solution.py:237
  201.0 1.8 fold_quarters.2
  203.7 2.3 fold_last.4
  206.0 9.4 %unproject.1 = (bf16[432,768]{1,0:T(8,128)(2,1)}, bf16[432,768]{1,0:T(8,128)(2,1)}, bf16[432,768]{1,0:T(8,128)(2,1)}, bf16[432,768]{1,0:T(8,128)(2,1)}, bf16[2,2...) custom-call(s32[3]{0:T(128)} %pad_add_fusion.side.where, ...), custom_call_target="tpu_custom_call" | custom-call | flops 20000000000 | bytes 60000000 | tf_op jit(solution)/shard_map/unproject/pallas_call | solution.py:303
  216.6 9.1 %collective-permute-done.30 = bf16[96,768]{1,0:T(8,128)(2,1)S(1)} collective-permute-done((bf16[96,768]{1,0:T(8,128)(2,1)S(1)}, bf16[96,768]{1,0:T(8,128)(2,1)S(1)}, u32[]{:S(2)}, u32[]{:S(2)}) %collective-permute-start.30) | collective-permute-done | bytes 147488 | tf_op jit(solution)/shard_map/ppermute | solution.py:725
  230.4 1.9 fold_quarters.3
  234.1 2.1 fold_planes.5
  238.4 1.3 collective-permute-start.35
  241.6 1.8 fold_last.5
  243.4 5.9 %collective-permute-done.35 = bf16[120,768]{1,0:T(8,128)(2,1)S(1)} collective-permute-done((bf16[120,768]{1,0:T(8,128)(2,1)}, bf16[120,768]{1,0:T(8,128)(2,1)S(1)}, u32[]{:S(2)}, u32[]{:S(2)}) %collective-permute-start.35) | collective-permute-done | bytes 184352 | tf_op jit(solution)/shard_map/ppermute | solution.py:725
  249.4 2.4 collective-permute-start.40
  252.2 7.7 %collective-permute-done.41 = bf16[1,72,768]{2,1,0:T(8,128)(2,1)S(1)} collective-permute-done((bf16[1,72,768]{2,1,0:T(8,128)(2,1)}, bf16[1,72,768]{2,1,0:T(8,128)(2,1)S(1)}, u32[]{:S(2)}, u32[]{:S(2)}) %collective-permute-start.41) | collective-permute-done | bytes 110624 | tf_op jit(solution)/shard_map/ppermute | solution.py:725
  260.4 3.5 collective-permute-done.40
  264.0 2.5 collective-permute-done.38
  269.7 5.5 %collective-permute-done.44 = bf16[2,120,768]{2,1,0:T(8,128)(2,1)S(1)} collective-permute-done((bf16[2,120,768]{2,1,0:T(8,128)(2,1)S(1)}, bf16[2,120,768]{2,1,0:T(8,128)(2,1)S(1)}, u32[]{:S(2)}, u32[]{:S(2)}) %collective-permute-start.44) | collective-permute-done | bytes 368672 | tf_op jit(solution)/shard_map/ppermute | solution.py:725
  275.6 2.8 collective-permute-done.42
  281.1 8.3 %collective-permute-done.32.p1 = bf16[432,768]{1,0:T(8,128)(2,1)S(1)} collective-permute-done((bf16[432,768]{1,0:T(8,128)(2,1)S(1)}, bf16[432,768]{1,0:T(8,128)(2,1)S(1)}, u32[]{:S(2)}, u32[]{:S(2)}) %collective-permute-start.32) | collective-permute-done | bytes 663584 | tf_op jit(solution)/shard_map/ppermute | solution.py:725
  289.5 3.8 %collective-permute-start.52 = (bf16[4,4,96,384]{3,2,1,0:T(8,128)(2,1)}, bf16[4,4,96,384]{3,2,1,0:T(8,128)(2,1)}, u32[]{:S(2)}, u32[]{:S(2)}) collective-permute-start(bf16[4,4,96,384]{3,2,1,0:T(8,128)(2,1)} %pad_maximum_fusion.3.a0), channel_id=1, source_target_pairs={{0,4},{4,0},{8,12},{12,8},{16,20},{20,16},{24,28},{28,24},{1,5},{5... | collective-permute-start | bytes 3538952 | tf_op jit(solution)/shard_map/ppermute | solution.py:721
  293.3 4.4 %close.1 = (f32[432,768]{1,0:T(8,128)}, bf16[432,768]{1,0:T(8,128)(2,1)}, f32[2,768]{1,0:T(2,128)}) custom-call(bf16[448,768]{1,0:T(8,128)(2,1)} %copy-done.12, bf16[432,768]{1,0:T(8,128)(2,1)} %add_convert_fusion.p0, bf16[432,768]{1,0:T(8,128)(2,1)} %copy-done.44, f32[768]{0:T(1024)} %gain.5, f32[432,768]{1,0:T(8,128)} %get-tuple-element.579.hidden), custom_call_target="tpu_custom_call" | custom-call | flops 20000000000 | bytes 60000000 | tf_op jit(solution)/shard_map/close/pallas_call | solution.py:332
  302.3 5.6 %placed.2 = f32[3072,768]{1,0:T(8,128)} custom-call(s32[3]{0:T(128)} %pad_add_fusion.side.where, bf16[4,4,96,384]{3,2,1,0:T(8,128)(2,1)} %pad_maximum_fusion.3.a0, bf16[4,4,96,384]{3,2,1,0:T(8,128)(2,1)} %pad_maximum_fusion.4.b0, bf16[4,4,96,384]{3,2,1,0:T(8,128)(2,1)} %collective-permute-done.52.a1, bf16[4,4,96,384]{3,2,1,0:T(8,128)(2,1)} %collective-permute-done.53.b1), custom_call_target="tpu_custom_call" | custom-call | flops 20000000000 | bytes 60000000 | tf_op jit(solution)/shard_map/placed/pallas_call | solution.py:562
  308.0 9.5 %collective-permute-done.57 = bf16[2,4,120,384]{3,2,1,0:T(8,128)(2,1)S(1)} collective-permute-done((bf16[2,4,120,384]{3,2,1,0:T(8,128)(2,1)}, bf16[2,4,120,384]{3,2,1,0:T(8,128)(2,1)S(1)}, u32[]{:S(2)}, u32[]{:S(2)}) %collective-permute-start.57) | collective-permute-done | bytes 737312 | tf_op jit(solution)/shard_map/ppermute | solution.py:721
  317.7 1.8 pad_maximum_fusion.1.b0
  319.6 2.2 collective-permute-start.60
  322.0 1.3 collective-permute-start.56
  323.2 3.6 collective-permute-start.46
  326.8 1.5 collective-permute-done.55
  328.4 1.3 collective-permute-start.54
  329.8 1.2 collective-permute-start.63
  332.2 11.0 %collective-permute-done.46 = bf16[432,768]{1,0:T(8,128)(2,1)S(1)} collective-permute-done((bf16[432,768]{1,0:T(8,128)(2,1)S(1)}, bf16[432,768]{1,0:T(8,128)(2,1)S(1)}, u32[]{:S(2)}, u32[]{:S(2)}) %collective-permute-start.46) | collective-permute-done | bytes 663584 | tf_op jit(solution)/shard_map/ppermute | solution.py:738
  344.6 1.5 collective-permute-done.59
  346.3 1.6 collective-permute-start.62
  349.4 6.5 %placed.3 = (f32[768,3072]{1,0:T(8,128)}, f32[768,768]{1,0:T(8,128)}) custom-call(s32[3]{0:T(128)} %pad_add_fusion.side.where, bf16[4,4,120,384]{3,2,1,0:T(8,128)(2,1)} %copy-done.2, bf16[4,4,120,384]{3,2,1,0:T(8,128)(2,1)} %copy-done.3, bf16[4,4,120,384]{3,2,1,0:T(8,128)(2,1)} %copy-done.40, bf16[4,4,120,384]{3,2,1,0:T(8,128)(2,1)} %copy-done.41), custom_call_target="tpu_custom_call" | custom-call | flops 20000000000 | bytes 60000000 | tf_op jit(solution)/shard_map/placed/pallas_call | solution.py:562
  358.8 9.1 %placed_in.1 = f32[768,2304]{1,0:T(8,128)} custom-call(s32[3]{0:T(128)} %pad_add_fusion.side.where, bf16[4,4,72,384]{3,2,1,0:T(8,128)(2,1)} %copy-done.8, bf16[4,4,72,384]{3,2,1,0:T(8,128)(2,1)} %copy-done.9, bf16[4,4,72,384]{3,2,1,0:T(8,128)(2,1)} %copy-done.42, bf16[4,4,72,384]{3,2,1,0:T(8,128)(2,1)} %collective-permute-done.66.b1), custom_call_target="tpu_custom_call" | custom-call | flops 20000000000 | bytes 60000000 | tf_op jit(solution)/shard_map/placed_in/pallas_call | solution.py:607
  (250 shorter events, 51.2 us)
Async XLA Ops:
  3.5 27.2 %collective-permute-start.1 = (bf16[448,768]{1,0:T(8,128)(2,1)}, bf16[448,768]{1,0:T(8,128)(2,1)}, u32[]{:S(2)}, u32[]{:S(2)}) collective-permute-start(bf16[448,768]{1,0:T(8,128)(2,1)} %pad_maximum_fusion.10), channel_id=1, source_target_pairs={{0,1},{1,0},{6,7},{7,6},{8,9},{9,8},{14,15},{15,14},{16,17},{17,16... | collective-permute-start | bytes 2064392 | tf_op jit(solution)/shard_map/ppermute | solution.py:738
  5.0 21.9 %collective-permute-start = (bf16[448,768]{1,0:T(8,128)(2,1)}, bf16[448,768]{1,0:T(8,128)(2,1)}, u32[]{:S(2)}, u32[]{:S(2)}) collective-permute-start(bf16[448,768]{1,0:T(8,128)(2,1)} %pad_maximum_fusion.10), channel_id=1, source_target_pairs={{2,4},{3,5},{4,2},{5,3},{10,12},{11,13},{12,10},{13,11},{18,20},{1... | collective-permute-start | bytes 2064392 | tf_op jit(solution)/shard_map/ppermute | solution.py:738
  26.9 11.9 %collective-permute-start.2 = (bf16[448,768]{1,0:T(8,128)(2,1)}, bf16[448,768]{1,0:T(8,128)(2,1)S(1)}, u32[]{:S(2)}, u32[]{:S(2)}) collective-permute-start(bf16[448,768]{1,0:T(8,128)(2,1)} %collective-permute-done), channel_id=1, source_target_pairs={{2,3},{3,2},{4,5},{5,4},{10,11},{11,10},{12,13},{13,12},{18,19},{1... | collective-permute-start | bytes 2064392 | tf_op jit(solution)/shard_map/ppermute | solution.py:738
  30.6 10.5 %collective-permute-start.3 = (bf16[448,768]{1,0:T(8,128)(2,1)S(1)}, bf16[448,768]{1,0:T(8,128)(2,1)}, u32[]{:S(2)}, u32[]{:S(2)}) collective-permute-start(bf16[448,768]{1,0:T(8,128)(2,1)S(1)} %broadcast_select_fusion.1.x0.x), channel_id=1, source_target_pairs={{0,4},{4,0},{8,12},{12,8},{16,20},{20,16},{24,28},{28,24},{1,5},{5... | collective-permute-start | bytes 2064392 | tf_op jit(solution)/shard_map/ppermute | solution.py:721
  52.4 31.8 %collective-permute-start.9 = (bf16[432,768]{1,0:T(8,128)(2,1)S(1)}, bf16[432,768]{1,0:T(8,128)(2,1)S(1)}, u32[]{:S(2)}, u32[]{:S(2)}) collective-permute-start(bf16[432,768]{1,0:T(8,128)(2,1)S(1)} %bitcast.48), channel_id=1, source_target_pairs={{2,4},{3,5},{4,2},{5,3},{10,12},{11,13},{12,10},{13,11},{18,20},{1... | collective-permute-start | bytes 1990664 | tf_op jit(solution)/shard_map/ppermute | solution.py:738
  78.1 6.1 %collective-permute-start.7 = (bf16[432,192]{1,0:T(8,128)(2,1)}, bf16[432,192]{1,0:T(8,128)(2,1)S(1)}, u32[]{:S(2)}, u32[]{:S(2)}) collective-permute-start(bf16[432,192]{1,0:T(8,128)(2,1)} %get-tuple-element.351), channel_id=1, source_target_pairs={{0,1},{1,0},{2,3},{3,2},{4,5},{5,4},{6,7},{7,6},{8,9},{9,8},{10,11... | collective-permute-start | bytes 497672 | tf_op jit(solution)/shard_map/ppermute | solution.py:725
  80.5 6.1 %collective-permute-start.5 = (bf16[432,192]{1,0:T(8,128)(2,1)}, bf16[432,192]{1,0:T(8,128)(2,1)S(1)}, u32[]{:S(2)}, u32[]{:S(2)}) collective-permute-start(bf16[432,192]{1,0:T(8,128)(2,1)} %get-tuple-element.349), channel_id=1, source_target_pairs={{0,1},{1,0},{2,3},{3,2},{4,5},{5,4},{6,7},{7,6},{8,9},{9,8},{10,11... | collective-permute-start | bytes 497672 | tf_op jit(solution)/shard_map/ppermute | solution.py:725
  80.5 6.1 %collective-permute-start.6 = (bf16[432,192]{1,0:T(8,128)(2,1)}, bf16[432,192]{1,0:T(8,128)(2,1)S(1)}, u32[]{:S(2)}, u32[]{:S(2)}) collective-permute-start(bf16[432,192]{1,0:T(8,128)(2,1)} %get-tuple-element.350), channel_id=1, source_target_pairs={{0,4},{4,0},{8,12},{12,8},{16,20},{20,16},{24,28},{28,24},{1,5},{5... | collective-permute-start | bytes 497672 | tf_op jit(solution)/shard_map/ppermute | solution.py:721
  115.2 19.5 %collective-permute-start.17 = (bf16[4,4,120,768]{3,2,1,0:T(8,128)(2,1)}, bf16[4,4,120,768]{3,2,1,0:T(8,128)(2,1)S(1)}, u32[]{:S(2)}, u32[]{:S(2)}) collective-permute-start(bf16[4,4,120,768]{3,2,1,0:T(8,128)(2,1)} %get-tuple-element.381), channel_id=1, source_target_pairs={{0,4},{4,0},{8,12},{12,8},{16,20},{20,16},{24,28},{28,24},{1,5},{5... | collective-permute-start | bytes 8847368 | tf_op jit(solution)/shard_map/ppermute | solution.py:721
  115.3 13.4 %collective-permute-start.10 = (bf16[4,4,96,768]{3,2,1,0:T(8,128)(2,1)}, bf16[4,4,96,768]{3,2,1,0:T(8,128)(2,1)}, u32[]{:S(2)}, u32[]{:S(2)}) collective-permute-start(bf16[4,4,96,768]{3,2,1,0:T(8,128)(2,1)} %get-tuple-element.357), channel_id=1, source_target_pairs={{0,4},{4,0},{8,12},{12,8},{16,20},{20,16},{24,28},{28,24},{1,5},{5... | collective-permute-start | bytes 7077896 | tf_op jit(solution)/shard_map/ppermute | solution.py:721
  115.8 7.3 %collective-permute-start.11 = (bf16[432,192]{1,0:T(8,128)(2,1)}, bf16[432,192]{1,0:T(8,128)(2,1)}, u32[]{:S(2)}, u32[]{:S(2)}) collective-permute-start(bf16[432,192]{1,0:T(8,128)(2,1)} %get-tuple-element.358), channel_id=1, source_target_pairs={{0,1},{1,0},{2,3},{3,2},{4,5},{5,4},{6,7},{7,6},{8,9},{9,8},{10,11... | collective-permute-start | bytes 497672 | tf_op jit(solution)/shard_map/ppermute | solution.py:725
  116.4 11.4 %collective-permute-start.12 = (bf16[432,192]{1,0:T(8,128)(2,1)}, bf16[432,192]{1,0:T(8,128)(2,1)}, u32[]{:S(2)}, u32[]{:S(2)}) collective-permute-start(bf16[432,192]{1,0:T(8,128)(2,1)} %get-tuple-element.359), channel_id=1, source_target_pairs={{0,1},{1,0},{2,3},{3,2},{4,5},{5,4},{6,7},{7,6},{8,9},{9,8},{10,11... | collective-permute-start | bytes 497672 | tf_op jit(solution)/shard_map/ppermute | solution.py:725
  117.3 23.3 %collective-permute-start.15 = (bf16[432,192]{1,0:T(8,128)(2,1)}, bf16[432,192]{1,0:T(8,128)(2,1)}, u32[]{:S(2)}, u32[]{:S(2)}) collective-permute-start(bf16[432,192]{1,0:T(8,128)(2,1)} %get-tuple-element.378), channel_id=1, source_target_pairs={{0,4},{4,0},{8,12},{12,8},{16,20},{20,16},{24,28},{28,24},{1,5},{5... | collective-permute-start | bytes 497672 | tf_op jit(solution)/shard_map/ppermute | solution.py:721
  127.8 12.7 %collective-permute-start.16 = (bf16[432,192]{1,0:T(8,128)(2,1)}, bf16[432,192]{1,0:T(8,128)(2,1)}, u32[]{:S(2)}, u32[]{:S(2)}) collective-permute-start(bf16[432,192]{1,0:T(8,128)(2,1)} %collective-permute-done.11), channel_id=1, source_target_pairs={{0,4},{4,0},{8,12},{12,8},{16,20},{20,16},{24,28},{28,24},{1,5},{5... | collective-permute-start | bytes 497672 | tf_op jit(solution)/shard_map/ppermute | solution.py:721
  132.2 21.4 %collective-permute-start.13 = (bf16[2,4,96,384]{3,2,1,0:T(8,128)(2,1)}, bf16[2,4,96,384]{3,2,1,0:T(8,128)(2,1)S(1)}, u32[]{:S(2)}, u32[]{:S(2)}) collective-permute-start(bf16[2,4,96,384]{3,2,1,0:T(8,128)(2,1)} %get-tuple-element.369), channel_id=1, source_target_pairs={{0,8},{4,12},{8,0},{12,4},{16,24},{20,28},{24,16},{28,20},{1,9},{5... | collective-permute-start | bytes 1769480 | tf_op jit(solution)/shard_map/ppermute | solution.py:721
  133.5 20.1 %collective-permute-start.14 = (bf16[2,4,96,384]{3,2,1,0:T(8,128)(2,1)}, bf16[2,4,96,384]{3,2,1,0:T(8,128)(2,1)S(1)}, u32[]{:S(2)}, u32[]{:S(2)}) collective-permute-start(bf16[2,4,96,384]{3,2,1,0:T(8,128)(2,1)} %get-tuple-element.370), channel_id=1, source_target_pairs={{0,16},{4,20},{8,24},{12,28},{16,0},{20,4},{24,8},{28,12},{1,17},{... | collective-permute-start | bytes 1769480 | tf_op jit(solution)/shard_map/ppermute | solution.py:721
  140.6 42.6 %collective-permute-start.19 = (bf16[2,4,120,384]{3,2,1,0:T(8,128)(2,1)}, bf16[2,4,120,384]{3,2,1,0:T(8,128)(2,1)S(1)}, u32[]{:S(2)}, u32[]{:S(2)}) collective-permute-start(bf16[2,4,120,384]{3,2,1,0:T(8,128)(2,1)} %get-tuple-element.409), channel_id=1, source_target_pairs={{0,8},{4,12},{8,0},{12,4},{16,24},{20,28},{24,16},{28,20},{1,9},{5... | collective-permute-start | bytes 2211848 | tf_op jit(solution)/shard_map/ppermute | solution.py:721
  140.9 42.3 %collective-permute-start.20 = (bf16[2,4,120,384]{3,2,1,0:T(8,128)(2,1)}, bf16[2,4,120,384]{3,2,1,0:T(8,128)(2,1)S(1)}, u32[]{:S(2)}, u32[]{:S(2)}) collective-permute-start(bf16[2,4,120,384]{3,2,1,0:T(8,128)(2,1)} %get-tuple-element.410), channel_id=1, source_target_pairs={{0,16},{4,20},{8,24},{12,28},{16,0},{20,4},{24,8},{28,12},{1,17},{... | collective-permute-start | bytes 2211848 | tf_op jit(solution)/shard_map/ppermute | solution.py:721
  157.3 21.5 %collective-permute-start.21 = (bf16[1,4,96,384]{3,2,1,0:T(8,128)(2,1)}, bf16[1,4,96,384]{3,2,1,0:T(8,128)(2,1)S(1)}, u32[]{:S(2)}, u32[]{:S(2)}) collective-permute-start(bf16[1,4,96,384]{3,2,1,0:T(8,128)(2,1)} %get-tuple-element.412), channel_id=1, source_target_pairs={{0,16},{4,20},{8,24},{12,28},{16,0},{20,4},{24,8},{28,12},{1,17},{... | collective-permute-start | bytes 884744 | tf_op jit(solution)/shard_map/ppermute | solution.py:721
  158.5 20.3 %collective-permute-start.22 = (bf16[1,4,96,384]{3,2,1,0:T(8,128)(2,1)}, bf16[1,4,96,384]{3,2,1,0:T(8,128)(2,1)S(1)}, u32[]{:S(2)}, u32[]{:S(2)}) collective-permute-start(bf16[1,4,96,384]{3,2,1,0:T(8,128)(2,1)} %get-tuple-element.413), channel_id=1, source_target_pairs={{0,8},{4,12},{8,0},{12,4},{16,24},{20,28},{24,16},{28,20},{1,9},{5... | collective-permute-start | bytes 884744 | tf_op jit(solution)/shard_map/ppermute | solution.py:721
  159.7 40.5 %collective-permute-start.18 = (bf16[432,768]{1,0:T(8,128)(2,1)S(1)}, bf16[432,768]{1,0:T(8,128)(2,1)S(1)}, u32[]{:S(2)}, u32[]{:S(2)}) collective-permute-start(bf16[432,768]{1,0:T(8,128)(2,1)S(1)} %copy-done.15), channel_id=1, source_target_pairs={{2,4},{3,5},{4,2},{5,3},{10,12},{11,13},{12,10},{13,11},{18,20},{1... | collective-permute-start | bytes 1990664 | tf_op jit(solution)/shard_map/ppermute | solution.py:738
  181.7 18.5 %collective-permute-start.25 = (bf16[2,96,768]{2,1,0:T(8,128)(2,1)}, bf16[2,96,768]{2,1,0:T(8,128)(2,1)S(1)}, u32[]{:S(2)}, u32[]{:S(2)}) collective-permute-start(bf16[2,96,768]{2,1,0:T(8,128)(2,1)} %get-tuple-element.460), channel_id=1, source_target_pairs={{0,1},{1,0},{2,3},{3,2},{4,5},{5,4},{6,7},{7,6},{8,9},{9,8},{10,11... | collective-permute-start | bytes 884744 | tf_op jit(solution)/shard_map/ppermute | solution.py:725
  187.3 15.6 %collective-permute-start.23 = (bf16[1,4,120,384]{3,2,1,0:T(8,128)(2,1)}, bf16[1,4,120,384]{3,2,1,0:T(8,128)(2,1)S(1)}, u32[]{:S(2)}, u32[]{:S(2)}) collective-permute-start(bf16[1,4,120,384]{3,2,1,0:T(8,128)(2,1)} %get-tuple-element.457), channel_id=1, source_target_pairs={{0,16},{4,20},{8,24},{12,28},{16,0},{20,4},{24,8},{28,12},{1,17},{... | collective-permute-start | bytes 1105928 | tf_op jit(solution)/shard_map/ppermute | solution.py:721
  187.5 15.3 %collective-permute-start.24 = (bf16[1,4,120,384]{3,2,1,0:T(8,128)(2,1)}, bf16[1,4,120,384]{3,2,1,0:T(8,128)(2,1)S(1)}, u32[]{:S(2)}, u32[]{:S(2)}) collective-permute-start(bf16[1,4,120,384]{3,2,1,0:T(8,128)(2,1)} %get-tuple-element.458), channel_id=1, source_target_pairs={{0,8},{4,12},{8,0},{12,4},{16,24},{20,28},{24,16},{28,20},{1,9},{5... | collective-permute-start | bytes 1105928 | tf_op jit(solution)/shard_map/ppermute | solution.py:721
  215.5 22.9 %collective-permute-start.26 = (bf16[432,768]{1,0:T(8,128)(2,1)}, bf16[432,768]{1,0:T(8,128)(2,1)S(1)}, u32[]{:S(2)}, u32[]{:S(2)}) collective-permute-start(bf16[432,768]{1,0:T(8,128)(2,1)} %get-tuple-element.493), channel_id=1, source_target_pairs={{0,4},{4,0},{8,12},{12,8},{16,20},{20,16},{24,28},{28,24},{1,5},{5... | collective-permute-start | bytes 1990664 | tf_op jit(solution)/shard_map/ppermute | solution.py:721
  215.6 24.2 %collective-permute-start.31 = (bf16[432,768]{1,0:T(8,128)(2,1)}, bf16[432,768]{1,0:T(8,128)(2,1)S(1)}, u32[]{:S(2)}, u32[]{:S(2)}) collective-permute-start(bf16[432,768]{1,0:T(8,128)(2,1)} %get-tuple-element.521), channel_id=1, source_target_pairs={{0,4},{4,0},{8,12},{12,8},{16,20},{20,16},{24,28},{28,24},{1,5},{5... | collective-permute-start | bytes 1990664 | tf_op jit(solution)/shard_map/ppermute | solution.py:721
  216.1 9.7 %collective-permute-start.30 = (bf16[96,768]{1,0:T(8,128)(2,1)S(1)}, bf16[96,768]{1,0:T(8,128)(2,1)S(1)}, u32[]{:S(2)}, u32[]{:S(2)}) collective-permute-start(bf16[96,768]{1,0:T(8,128)(2,1)S(1)} %copy-done.48), channel_id=1, source_target_pairs={{0,2},{1,3},{2,0},{3,1},{4,6},{5,7},{6,4},{7,5},{8,10},{9,11},{10,... | collective-permute-start | bytes 442376 | tf_op jit(solution)/shard_map/ppermute | solution.py:725
  216.6 12.9 %collective-permute-start.29 = (bf16[2,120,768]{2,1,0:T(8,128)(2,1)}, bf16[2,120,768]{2,1,0:T(8,128)(2,1)S(1)}, u32[]{:S(2)}, u32[]{:S(2)}) collective-permute-start(bf16[2,120,768]{2,1,0:T(8,128)(2,1)} %get-tuple-element.501), channel_id=1, source_target_pairs={{0,1},{1,0},{2,3},{3,2},{4,5},{5,4},{6,7},{7,6},{8,9},{9,8},{10,11... | collective-permute-start | bytes 1105928 | tf_op jit(solution)/shard_map/ppermute | solution.py:725
  225.8 6.7 %collective-permute-start.27 = (bf16[2,2,72,384]{3,2,1,0:T(8,128)(2,1)}, bf16[2,2,72,384]{3,2,1,0:T(8,128)(2,1)S(1)}, u32[]{:S(2)}, u32[]{:S(2)}) collective-permute-start(bf16[2,2,72,384]{3,2,1,0:T(8,128)(2,1)} %get-tuple-element.498), channel_id=1, source_target_pairs={{0,8},{4,12},{8,0},{12,4},{16,24},{20,28},{24,16},{28,20},{1,9},{5... | collective-permute-start | bytes 663560 | tf_op jit(solution)/shard_map/ppermute | solution.py:721
  227.0 6.4 %collective-permute-start.28 = (bf16[2,2,72,384]{3,2,1,0:T(8,128)(2,1)}, bf16[2,2,72,384]{3,2,1,0:T(8,128)(2,1)S(1)}, u32[]{:S(2)}, u32[]{:S(2)}) collective-permute-start(bf16[2,2,72,384]{3,2,1,0:T(8,128)(2,1)} %get-tuple-element.499), channel_id=1, source_target_pairs={{0,16},{4,20},{8,24},{12,28},{16,0},{20,4},{24,8},{28,12},{1,17},{... | collective-permute-start | bytes 663560 | tf_op jit(solution)/shard_map/ppermute | solution.py:721
  229.5 11.3 %collective-permute-start.33 = (bf16[96,768]{1,0:T(8,128)(2,1)S(1)}, bf16[96,768]{1,0:T(8,128)(2,1)S(1)}, u32[]{:S(2)}, u32[]{:S(2)}) collective-permute-start(bf16[96,768]{1,0:T(8,128)(2,1)S(1)} %add_convert_fusion.3), channel_id=1, source_target_pairs={{0,2},{1,3},{2,0},{3,1},{4,6},{5,7},{6,4},{7,5},{8,10},{9,11},{10,... | collective-permute-start | bytes 442376 | tf_op jit(solution)/shard_map/ppermute | solution.py:725
  236.1 4.8 %collective-permute-start.36 = (bf16[1,2,72,384]{3,2,1,0:T(8,128)(2,1)}, bf16[1,2,72,384]{3,2,1,0:T(8,128)(2,1)S(1)}, u32[]{:S(2)}, u32[]{:S(2)}) collective-permute-start(bf16[1,2,72,384]{3,2,1,0:T(8,128)(2,1)} %get-tuple-element.533), channel_id=1, source_target_pairs={{0,16},{4,20},{8,24},{12,28},{16,0},{20,4},{24,8},{28,12},{1,17},{... | collective-permute-start | bytes 331784 | tf_op jit(solution)/shard_map/ppermute | solution.py:721
  237.4 4.1 %collective-permute-start.37 = (bf16[1,2,72,384]{3,2,1,0:T(8,128)(2,1)}, bf16[1,2,72,384]{3,2,1,0:T(8,128)(2,1)}, u32[]{:S(2)}, u32[]{:S(2)}) collective-permute-start(bf16[1,2,72,384]{3,2,1,0:T(8,128)(2,1)} %get-tuple-element.534), channel_id=1, source_target_pairs={{0,8},{4,12},{8,0},{12,4},{16,24},{20,28},{24,16},{28,20},{1,9},{5... | collective-permute-start | bytes 331784 | tf_op jit(solution)/shard_map/ppermute | solution.py:721
  238.4 10.9 %collective-permute-start.35 = (bf16[120,768]{1,0:T(8,128)(2,1)}, bf16[120,768]{1,0:T(8,128)(2,1)S(1)}, u32[]{:S(2)}, u32[]{:S(2)}) collective-permute-start(bf16[120,768]{1,0:T(8,128)(2,1)} %get-tuple-element.531), channel_id=1, source_target_pairs={{0,2},{1,3},{2,0},{3,1},{4,6},{5,7},{6,4},{7,5},{8,10},{9,11},{10,... | collective-permute-start | bytes 552968 | tf_op jit(solution)/shard_map/ppermute | solution.py:725
  240.9 11.2 %collective-permute-start.34 = (bf16[2,96,768]{2,1,0:T(8,128)(2,1)S(1)}, bf16[2,96,768]{2,1,0:T(8,128)(2,1)S(1)}, u32[]{:S(2)}, u32[]{:S(2)}) collective-permute-start(bf16[2,96,768]{2,1,0:T(8,128)(2,1)S(1)} %pad_maximum_fusion.16), channel_id=1, source_target_pairs={{0,1},{1,0},{2,3},{3,2},{4,5},{5,4},{6,7},{7,6},{8,9},{9,8},{10,11... | collective-permute-start | bytes 884744 | tf_op jit(solution)/shard_map/ppermute | solution.py:725
  249.3 10.6 %collective-permute-start.41 = (bf16[1,72,768]{2,1,0:T(8,128)(2,1)}, bf16[1,72,768]{2,1,0:T(8,128)(2,1)S(1)}, u32[]{:S(2)}, u32[]{:S(2)}) collective-permute-start(bf16[1,72,768]{2,1,0:T(8,128)(2,1)} %get-tuple-element.551), channel_id=1, source_target_pairs={{0,2},{1,3},{2,0},{3,1},{4,6},{5,7},{6,4},{7,5},{8,10},{9,11},{10,... | collective-permute-start | bytes 331784 | tf_op jit(solution)/shard_map/ppermute | solution.py:725
  249.4 14.4 %collective-permute-start.40 = (bf16[120,768]{1,0:T(8,128)(2,1)S(1)}, bf16[120,768]{1,0:T(8,128)(2,1)S(1)}, u32[]{:S(2)}, u32[]{:S(2)}) collective-permute-start(bf16[120,768]{1,0:T(8,128)(2,1)S(1)} %add_convert_fusion.2), channel_id=1, source_target_pairs={{0,2},{1,3},{2,0},{3,1},{4,6},{5,7},{6,4},{7,5},{8,10},{9,11},{10,... | collective-permute-start | bytes 552968 | tf_op jit(solution)/shard_map/ppermute | solution.py:725
  259.9 6.6 %collective-permute-start.38 = (bf16[1,4,96,384]{3,2,1,0:T(8,128)(2,1)S(1)}, bf16[1,4,96,384]{3,2,1,0:T(8,128)(2,1)S(1)}, u32[]{:S(2)}, u32[]{:S(2)}) collective-permute-start(bf16[1,4,96,384]{3,2,1,0:T(8,128)(2,1)S(1)} %get-tuple-element.547), channel_id=1, source_target_pairs={{0,16},{4,20},{8,24},{12,28},{16,0},{20,4},{24,8},{28,12},{1,17},{... | collective-permute-start | bytes 884744 | tf_op jit(solution)/shard_map/ppermute | solution.py:721
  260.1 6.3 %collective-permute-start.39 = (bf16[1,4,96,384]{3,2,1,0:T(8,128)(2,1)S(1)}, bf16[1,4,96,384]{3,2,1,0:T(8,128)(2,1)S(1)}, u32[]{:S(2)}, u32[]{:S(2)}) collective-permute-start(bf16[1,4,96,384]{3,2,1,0:T(8,128)(2,1)S(1)} %get-tuple-element.548), channel_id=1, source_target_pairs={{0,8},{4,12},{8,0},{12,4},{16,24},{20,28},{24,16},{28,20},{1,9},{5... | collective-permute-start | bytes 884744 | tf_op jit(solution)/shard_map/ppermute | solution.py:721
  263.9 5.3 %collective-permute-start.45 = (bf16[72,768]{1,0:T(8,128)(2,1)S(1)}, bf16[72,768]{1,0:T(8,128)(2,1)S(1)}, u32[]{:S(2)}, u32[]{:S(2)}) collective-permute-start(bf16[72,768]{1,0:T(8,128)(2,1)S(1)} %bitcast.45), channel_id=1, source_target_pairs={{0,2},{1,3},{2,0},{3,1},{4,6},{5,7},{6,4},{7,5},{8,10},{9,11},{10,... | collective-permute-start | bytes 331784 | tf_op jit(solution)/shard_map/ppermute | solution.py:725
  263.9 11.3 %collective-permute-start.44 = (bf16[2,120,768]{2,1,0:T(8,128)(2,1)S(1)}, bf16[2,120,768]{2,1,0:T(8,128)(2,1)S(1)}, u32[]{:S(2)}, u32[]{:S(2)}) collective-permute-start(bf16[2,120,768]{2,1,0:T(8,128)(2,1)S(1)} %pad_maximum_fusion.15), channel_id=1, source_target_pairs={{0,1},{1,0},{2,3},{3,2},{4,5},{5,4},{6,7},{7,6},{8,9},{9,8},{10,11... | collective-permute-start | bytes 1105928 | tf_op jit(solution)/shard_map/ppermute | solution.py:725
  266.6 11.8 %collective-permute-start.42 = (bf16[2,4,96,384]{3,2,1,0:T(8,128)(2,1)S(1)}, bf16[2,4,96,384]{3,2,1,0:T(8,128)(2,1)S(1)}, u32[]{:S(2)}, u32[]{:S(2)}) collective-permute-start(bf16[2,4,96,384]{3,2,1,0:T(8,128)(2,1)S(1)} %pad_maximum_fusion.11), channel_id=1, source_target_pairs={{0,8},{4,12},{8,0},{12,4},{16,24},{20,28},{24,16},{28,20},{1,9},{5... | collective-permute-start | bytes 1769480 | tf_op jit(solution)/shard_map/ppermute | solution.py:721
  267.0 11.8 %collective-permute-start.43 = (bf16[2,4,96,384]{3,2,1,0:T(8,128)(2,1)S(1)}, bf16[2,4,96,384]{3,2,1,0:T(8,128)(2,1)S(1)}, u32[]{:S(2)}, u32[]{:S(2)}) collective-permute-start(bf16[2,4,96,384]{3,2,1,0:T(8,128)(2,1)S(1)} %pad_maximum_fusion.12), channel_id=1, source_target_pairs={{0,16},{4,20},{8,24},{12,28},{16,0},{20,4},{24,8},{28,12},{1,17},{... | collective-permute-start | bytes 1769480 | tf_op jit(solution)/shard_map/ppermute | solution.py:721
  268.2 21.3 %collective-permute-start.32 = (bf16[432,768]{1,0:T(8,128)(2,1)S(1)}, bf16[432,768]{1,0:T(8,128)(2,1)S(1)}, u32[]{:S(2)}, u32[]{:S(2)}) collective-permute-start(bf16[432,768]{1,0:T(8,128)(2,1)S(1)} %add_convert_fusion.1), channel_id=1, source_target_pairs={{0,1},{1,0},{2,3},{3,2},{4,5},{5,4},{6,7},{7,6},{8,9},{9,8},{10,11... | collective-permute-start | bytes 1990664 | tf_op jit(solution)/shard_map/ppermute | solution.py:725
  269.2 29.2 %collective-permute-start.50 = (bf16[2,72,768]{2,1,0:T(8,128)(2,1)S(1)}, bf16[2,72,768]{2,1,0:T(8,128)(2,1)S(1)}, u32[]{:S(2)}, u32[]{:S(2)}) collective-permute-start(bf16[2,72,768]{2,1,0:T(8,128)(2,1)S(1)} %pad_maximum_fusion.17), channel_id=1, source_target_pairs={{0,1},{1,0},{2,3},{3,2},{4,5},{5,4},{6,7},{7,6},{8,9},{9,8},{10,11... | collective-permute-start | bytes 663560 | tf_op jit(solution)/shard_map/ppermute | solution.py:725
  275.4 23.1 %collective-permute-start.48 = (bf16[1,4,120,384]{3,2,1,0:T(8,128)(2,1)S(1)}, bf16[1,4,120,384]{3,2,1,0:T(8,128)(2,1)S(1)}, u32[]{:S(2)}, u32[]{:S(2)}) collective-permute-start(bf16[1,4,120,384]{3,2,1,0:T(8,128)(2,1)S(1)} %get-tuple-element.592), channel_id=1, source_target_pairs={{0,16},{4,20},{8,24},{12,28},{16,0},{20,4},{24,8},{28,12},{1,17},{... | collective-permute-start | bytes 1105928 | tf_op jit(solution)/shard_map/ppermute | solution.py:721
  278.4 20.1 %collective-permute-start.49 = (bf16[1,4,120,384]{3,2,1,0:T(8,128)(2,1)S(1)}, bf16[1,4,120,384]{3,2,1,0:T(8,128)(2,1)S(1)}, u32[]{:S(2)}, u32[]{:S(2)}) collective-permute-start(bf16[1,4,120,384]{3,2,1,0:T(8,128)(2,1)S(1)} %get-tuple-element.593), channel_id=1, source_target_pairs={{0,8},{4,12},{8,0},{12,4},{16,24},{20,28},{24,16},{28,20},{1,9},{5... | collective-permute-start | bytes 1105928 | tf_op jit(solution)/shard_map/ppermute | solution.py:721
  289.5 12.8 %collective-permute-start.52 = (bf16[4,4,96,384]{3,2,1,0:T(8,128)(2,1)}, bf16[4,4,96,384]{3,2,1,0:T(8,128)(2,1)}, u32[]{:S(2)}, u32[]{:S(2)}) collective-permute-start(bf16[4,4,96,384]{3,2,1,0:T(8,128)(2,1)} %pad_maximum_fusion.3.a0), channel_id=1, source_target_pairs={{0,4},{4,0},{8,12},{12,8},{16,20},{20,16},{24,28},{28,24},{1,5},{5... | collective-permute-start | bytes 3538952 | tf_op jit(solution)/shard_map/ppermute | solution.py:721
  293.3 9.0 %collective-permute-start.53 = (bf16[4,4,96,384]{3,2,1,0:T(8,128)(2,1)}, bf16[4,4,96,384]{3,2,1,0:T(8,128)(2,1)}, u32[]{:S(2)}, u32[]{:S(2)}) collective-permute-start(bf16[4,4,96,384]{3,2,1,0:T(8,128)(2,1)} %pad_maximum_fusion.4.b0), channel_id=1, source_target_pairs={{0,4},{4,0},{8,12},{12,8},{16,20},{20,16},{24,28},{28,24},{1,5},{5... | collective-permute-start | bytes 3538952 | tf_op jit(solution)/shard_map/ppermute | solution.py:721
  298.5 3.0 collective-permute-start.47
  300.2 17.3 %collective-permute-start.57 = (bf16[2,4,120,384]{3,2,1,0:T(8,128)(2,1)}, bf16[2,4,120,384]{3,2,1,0:T(8,128)(2,1)S(1)}, u32[]{:S(2)}, u32[]{:S(2)}) collective-permute-start(bf16[2,4,120,384]{3,2,1,0:T(8,128)(2,1)} %pad_maximum_fusion.8), channel_id=1, source_target_pairs={{0,8},{4,12},{8,0},{12,4},{16,24},{20,28},{24,16},{28,20},{1,9},{5... | collective-permute-start | bytes 2211848 | tf_op jit(solution)/shard_map/ppermute | solution.py:721
  300.5 16.9 %collective-permute-start.58 = (bf16[2,4,120,384]{3,2,1,0:T(8,128)(2,1)S(1)}, bf16[2,4,120,384]{3,2,1,0:T(8,128)(2,1)}, u32[]{:S(2)}, u32[]{:S(2)}) collective-permute-start(bf16[2,4,120,384]{3,2,1,0:T(8,128)(2,1)S(1)} %pad_maximum_fusion.9), channel_id=1, source_target_pairs={{0,16},{4,20},{8,24},{12,28},{16,0},{20,4},{24,8},{28,12},{1,17},{... | collective-permute-start | bytes 2211848 | tf_op jit(solution)/shard_map/ppermute | solution.py:721
  301.5 6.4 %collective-permute-start.51 = (f32[12,768]{1,0:T(8,128)S(1)}, f32[12,768]{1,0:T(8,128)S(1)}, u32[]{:S(2)}, u32[]{:S(2)}) collective-permute-start(f32[12,768]{1,0:T(8,128)S(1)} %fusion), channel_id=1, source_target_pairs={{0,2},{1,3},{2,0},{3,1},{4,6},{5,7},{6,4},{7,5},{8,10},{9,11},{10,... | collective-permute-start | bytes 110600 | tf_op jit(solution)/shard_map/ppermute | solution.py:725
  319.6 25.1 %collective-permute-start.60 = (bf16[4,4,120,384]{3,2,1,0:T(8,128)(2,1)S(1)}, bf16[4,4,120,384]{3,2,1,0:T(8,128)(2,1)S(1)}, u32[]{:S(2)}, u32[]{:S(2)}) collective-permute-start(bf16[4,4,120,384]{3,2,1,0:T(8,128)(2,1)S(1)} %pad_maximum_fusion.a0), channel_id=1, source_target_pairs={{0,4},{4,0},{8,12},{12,8},{16,20},{20,16},{24,28},{28,24},{1,5},{5... | collective-permute-start | bytes 4423688 | tf_op jit(solution)/shard_map/ppermute | solution.py:721
  321.7 22.9 %collective-permute-start.61 = (bf16[4,4,120,384]{3,2,1,0:T(8,128)(2,1)S(1)}, bf16[4,4,120,384]{3,2,1,0:T(8,128)(2,1)S(1)}, u32[]{:S(2)}, u32[]{:S(2)}) collective-permute-start(bf16[4,4,120,384]{3,2,1,0:T(8,128)(2,1)S(1)} %pad_maximum_fusion.1.b0), channel_id=1, source_target_pairs={{0,4},{4,0},{8,12},{12,8},{16,20},{20,16},{24,28},{28,24},{1,5},{5... | collective-permute-start | bytes 4423688 | tf_op jit(solution)/shard_map/ppermute | solution.py:721
  321.8 6.6 %collective-permute-start.55 = (bf16[1,4,72,384]{3,2,1,0:T(8,128)(2,1)S(1)}, bf16[1,4,72,384]{3,2,1,0:T(8,128)(2,1)S(1)}, u32[]{:S(2)}, u32[]{:S(2)}) collective-permute-start(bf16[1,4,72,384]{3,2,1,0:T(8,128)(2,1)S(1)} %get-tuple-element.616), channel_id=1, source_target_pairs={{0,16},{4,20},{8,24},{12,28},{16,0},{20,4},{24,8},{28,12},{1,17},{... | collective-permute-start | bytes 663560 | tf_op jit(solution)/shard_map/ppermute | solution.py:721
  322.0 7.7 %collective-permute-start.56 = (bf16[1,4,72,384]{3,2,1,0:T(8,128)(2,1)S(1)}, bf16[1,4,72,384]{3,2,1,0:T(8,128)(2,1)S(1)}, u32[]{:S(2)}, u32[]{:S(2)}) collective-permute-start(bf16[1,4,72,384]{3,2,1,0:T(8,128)(2,1)S(1)} %get-tuple-element.617), channel_id=1, source_target_pairs={{0,8},{4,12},{8,0},{12,4},{16,24},{20,28},{24,16},{28,20},{1,9},{5... | collective-permute-start | bytes 663560 | tf_op jit(solution)/shard_map/ppermute | solution.py:721
  323.2 20.0 %collective-permute-start.46 = (bf16[432,768]{1,0:T(8,128)(2,1)S(1)}, bf16[432,768]{1,0:T(8,128)(2,1)S(1)}, u32[]{:S(2)}, u32[]{:S(2)}) collective-permute-start(bf16[432,768]{1,0:T(8,128)(2,1)S(1)} %copy-done.43), channel_id=1, source_target_pairs={{2,4},{3,5},{4,2},{5,3},{10,12},{11,13},{12,10},{13,11},{18,20},{1... | collective-permute-start | bytes 1990664 | tf_op jit(solution)/shard_map/ppermute | solution.py:738
  329.8 16.4 %collective-permute-start.63 = (bf16[2,4,72,384]{3,2,1,0:T(8,128)(2,1)S(1)}, bf16[2,4,72,384]{3,2,1,0:T(8,128)(2,1)S(1)}, u32[]{:S(2)}, u32[]{:S(2)}) collective-permute-start(bf16[2,4,72,384]{3,2,1,0:T(8,128)(2,1)S(1)} %pad_maximum_fusion.13), channel_id=1, source_target_pairs={{0,8},{4,12},{8,0},{12,4},{16,24},{20,28},{24,16},{28,20},{1,9},{5... | collective-permute-start | bytes 1327112 | tf_op jit(solution)/shard_map/ppermute | solution.py:721
  331.0 15.1 %collective-permute-start.64 = (bf16[2,4,72,384]{3,2,1,0:T(8,128)(2,1)S(1)}, bf16[2,4,72,384]{3,2,1,0:T(8,128)(2,1)S(1)}, u32[]{:S(2)}, u32[]{:S(2)}) collective-permute-start(bf16[2,4,72,384]{3,2,1,0:T(8,128)(2,1)S(1)} %pad_maximum_fusion.14), channel_id=1, source_target_pairs={{0,16},{4,20},{8,24},{12,28},{16,0},{20,4},{24,8},{28,12},{1,17},{... | collective-permute-start | bytes 1327112 | tf_op jit(solution)/shard_map/ppermute | solution.py:721
  343.2 2.9 collective-permute-start.59
  346.3 3.1 collective-permute-start.62
  348.1 9.7 %collective-permute-start.65 = (bf16[4,4,72,384]{3,2,1,0:T(8,128)(2,1)S(1)}, bf16[4,4,72,384]{3,2,1,0:T(8,128)(2,1)S(1)}, u32[]{:S(2)}, u32[]{:S(2)}) collective-permute-start(bf16[4,4,72,384]{3,2,1,0:T(8,128)(2,1)S(1)} %pad_maximum_fusion.6.a0), channel_id=1, source_target_pairs={{0,4},{4,0},{8,12},{12,8},{16,20},{20,16},{24,28},{28,24},{1,5},{5... | collective-permute-start | bytes 2654216 | tf_op jit(solution)/shard_map/ppermute | solution.py:721
  348.1 9.7 %collective-permute-start.66 = (bf16[4,4,72,384]{3,2,1,0:T(8,128)(2,1)S(1)}, bf16[4,4,72,384]{3,2,1,0:T(8,128)(2,1)}, u32[]{:S(2)}, u32[]{:S(2)}) collective-permute-start(bf16[4,4,72,384]{3,2,1,0:T(8,128)(2,1)S(1)} %pad_maximum_fusion.7.b0), channel_id=1, source_target_pairs={{0,4},{4,0},{8,12},{12,8},{16,20},{20,16},{24,28},{28,24},{1,5},{5... | collective-permute-start | bytes 2654216 | tf_op jit(solution)/shard_map/ppermute | solution.py:721
  (52 other events, 280.8 us)
